TPU v7x, 32 devices: a whole 2x2x4 slice. The times are simulated.
32 devices in a mesh: dp: 2 (over y), expert: 16 (over z, x, core).
Axes of the slice: x: 2, y: 2, z: 4, core: 2. Of those that a mesh axis runs over, the one named last changes fastest.
Arguments:
- activations: bfloat16 [4096, 4096], P(('dp', 'expert')), may hold values from -6 to 6
- cotangent: bfloat16 [4096, 4096], P(('dp', 'expert')), may hold values from -6 to 6
- expert_ids: int32 [4096, 1], P(('dp', 'expert')), may hold values from 0 to 127; in each aligned block of 128 rows (0 to 127, 128 to 255, ...) at most 2 rows name the same one
- gate_probs: float32 [4096, 1], P(('dp', 'expert')), may hold values from 0.2 to 1
- gate_up: bfloat16 [16, 2, 4096, 1536], P('expert', None, None, 'dp'), may hold values from -0.09375 to 0.09375
- down_proj: bfloat16 [16, 1536, 4096], P('expert', 'dp'), may hold values from -0.15625 to 0.15625
Outputs:
- input_grad: bfloat16 [4096, 4096], P(('dp', 'expert'))
- grad_gate_up: bfloat16 [16, 2, 4096, 1536], P('expert', None, None, 'dp')
- grad_down: bfloat16 [16, 1536, 4096], P('expert', 'dp')
Inputs may be any that keep to these rules, and one draw needn't show every extreme that they name: `expert_ids`: expert e < 16 is held by index e of the expert axis. Among the 128 tokens of one device no expert is named more than 2 times, a bound that some block reaches.
All inputs are finite; a program needn't handle non-finite values.
Results may differ from a plain program's by a relative error of at most 0.0058.
Values may be sent and summed in bfloat16 or wider, within the bound.
No kernel may reach another device: no remote copies, remote signals or barrier semaphores. Data moves between devices by JAX's collectives and lax.ppermute only.
A program may use at most 128 MiB of HBM per device.

v0:
```python
import functools

import jax
import jax.numpy as jnp
from jax import lax
from jax.experimental import pallas as pl
from jax.experimental.pallas import tpu as pltpu
from jax.sharding import PartitionSpec as P

CAP = 2
MIB = 1024 * 1024
VMEM = pl.BlockSpec(memory_space=pltpu.VMEM)
HBM = pl.BlockSpec(memory_space=pltpu.HBM)


def dot_nn(a, b):
    return lax.dot_general(a, b, (((1,), (0,)), ((), ())), preferred_element_type=jnp.float32)


def dot_nt(a, b):
    return lax.dot_general(a, b, (((1,), (1,)), ((), ())), preferred_element_type=jnp.float32)


def dot_tn(a, b):
    return lax.dot_general(a, b, (((0,), (0,)), ((), ())), preferred_element_type=jnp.float32)


def cost(flops, moved):
    return pl.CostEstimate(flops=int(flops), bytes_accessed=int(moved), transcendentals=0)


def params(mib):
    return pltpu.CompilerParams(vmem_limit_bytes=mib * MIB)


def in_hbm(value):
    return pltpu.with_memory_space_constraint(value, pltpu.HBM)


def bf16(*shape):
    return jax.ShapeDtypeStruct(shape, jnp.bfloat16)


def factors(experts):
    far = 1
    while 4 * far * far <= experts:
        far *= 2
    return far, experts // far


def route_kernel(experts, chunk, ids_hbm, probs_hbm, act_hbm, cot_hbm, *refs):
    far, near = factors(experts)
    sends, place_ref = refs[:far], refs[far]
    ids_ref, probs_ref, act, cot, sems = refs[far + 1 :]
    tokens, width = act.shape
    steps = width // chunk
    small = (
        pltpu.make_async_copy(ids_hbm, ids_ref, sems.at[2 * steps]),
        pltpu.make_async_copy(probs_hbm, probs_ref, sems.at[2 * steps + 1]),
    )
    large = []
    for step in range(steps):
        at = pl.ds(step * chunk, chunk)
        large.append(
            (
                pltpu.make_async_copy(act_hbm.at[:, at], act.at[:, at], sems.at[2 * step]),
                pltpu.make_async_copy(cot_hbm.at[:, at], cot.at[:, at], sems.at[2 * step + 1]),
            )
        )
    for one in small:
        one.start()
    for pair in large:
        for one in pair:
            one.start()
    for one in small:
        one.wait()

    me = lax.axis_index("expert")
    ids = ids_ref[...]
    inside = ids < experts
    units = lax.broadcasted_iota(jnp.int32, (experts, tokens), 0)
    onehot = jnp.where(units == ids, 1.0, 0.0)
    earlier = lax.broadcasted_iota(jnp.int32, (tokens, tokens), 0) < lax.broadcasted_iota(
        jnp.int32, (tokens, tokens), 1
    )
    before = dot_nn(onehot.astype(jnp.bfloat16), jnp.where(earlier, 1.0, 0.0).astype(jnp.bfloat16))
    rank = jnp.sum(before * onehot, axis=0, keepdims=True).astype(jnp.int32)
    slots = lax.broadcasted_iota(jnp.int32, (experts * CAP, tokens), 0)
    slot = jnp.where(inside, ids * CAP + rank, -1)
    place_ref[...] = jnp.where(slots == slot, 1.0, 0.0).astype(jnp.bfloat16)
    turned = jnp.where(inside, (ids ^ me) * CAP + rank, -1)
    pick = jnp.where(slots == turned, 1.0, 0.0)
    weight = jnp.sum(pick * probs_ref[...], axis=1, keepdims=True)
    pick = pick.astype(jnp.bfloat16)
    for step in range(steps):
        at = slice(step * chunk, (step + 1) * chunk)
        for one in large[step]:
            one.wait()
        rows_tok = dot_nn(pick, act[:, at]).astype(jnp.bfloat16)
        rows_cot = (weight * dot_nn(pick, cot[:, at])).astype(jnp.bfloat16)
        for unit in range(experts):
            rows = slice(unit * CAP, (unit + 1) * CAP)
            sends[unit // near][unit % near, :CAP, at] = rows_tok[rows]
            sends[unit // near][unit % near, CAP:, at] = rows_cot[rows]


def route(ids, probs, act, cot, experts):
    tokens, width = act.shape
    chunk = min(1024, width)
    far, near = factors(experts)
    out = pl.pallas_call(
        functools.partial(route_kernel, experts, chunk),
        in_specs=[HBM] * 4,
        out_specs=[VMEM] * (far + 1),
        out_shape=[bf16(near, 2 * CAP, width)] * far + [bf16(experts * CAP, tokens)],
        scratch_shapes=[
            pltpu.VMEM((1, tokens), jnp.int32),
            pltpu.VMEM((1, tokens), jnp.float32),
            pltpu.VMEM((tokens, width), jnp.bfloat16),
            pltpu.VMEM((tokens, width), jnp.bfloat16),
            pltpu.SemaphoreType.DMA((2 * (width // chunk) + 2,)),
        ],
        compiler_params=params(16),
        cost_estimate=cost(4 * experts * CAP * tokens * width, 4 * tokens * width),
        name="route_rows",
    )(in_hbm(ids), in_hbm(probs), in_hbm(act), in_hbm(cot))
    return out[:far], out[far]


def merge_kernel(far, *refs):
    pieces, outs = refs[:far], refs[far + 1 :]
    for index, out in enumerate(outs):
        rows = [piece[index, :CAP, :] for piece in pieces]
        rows += [piece[index, CAP:, :] for piece in pieces]
        out[...] = jnp.concatenate(rows, axis=0)


def merge(pieces, after):
    far = len(pieces)
    near, _, width = pieces[0].shape
    return pl.pallas_call(
        functools.partial(merge_kernel, far),
        in_specs=[VMEM] * far + [pl.BlockSpec(memory_space=pl.ANY)],
        out_specs=[VMEM] * near,
        out_shape=[bf16(2 * CAP * far, width)] * near,
        compiler_params=params(16),
        cost_estimate=cost(0, 8 * near * CAP * far * width),
        name="merge_rows",
    )(*pieces, after)


def load_kernel(chunk, pair_hbm, down_hbm, after, pair, down, sems):
    del after
    width = down.shape[1]
    copies = []
    for step in range(width // chunk):
        at = pl.ds(step * chunk, chunk)
        copies += [
            pltpu.make_async_copy(pair_hbm.at[:, at, :], pair.at[:, at, :], sems.at[0, step]),
            pltpu.make_async_copy(down_hbm.at[:, at], down.at[:, at], sems.at[1, step]),
        ]
    for one in copies:
        one.start()
    for one in copies:
        one.wait()


def load(pair, down, after):
    units, width = down.shape
    chunk = min(1024, width)
    return pl.pallas_call(
        functools.partial(load_kernel, chunk),
        in_specs=[HBM] * 2 + [pl.BlockSpec(memory_space=pl.ANY)],
        out_specs=[VMEM] * 2,
        out_shape=[pltpu.VMEM(pair.shape, jnp.bfloat16), pltpu.VMEM(down.shape, jnp.bfloat16)],
        scratch_shapes=[pltpu.SemaphoreType.DMA((2, width // chunk))],
        compiler_params=params(28),
        cost_estimate=cost(0, 6 * width * units),
        name="load_weights",
    )(in_hbm(pair), in_hbm(down), after)


def expert_kernel(experts, groups, chunk, *refs):
    far, near = factors(experts)
    count = groups * near
    got, pair, down = refs[:count], refs[count], refs[count + 1]
    gate_out, up_out, hidden_out, tok_all, cot_all, parts_hbm = refs[count + 2 : count + 8]
    parts, acc_gate, acc_up, acc_hid, sems = refs[count + 8 :]
    half = far * CAP
    width = got[0].shape[1]
    steps = width // chunk
    for step in range(steps):
        at = slice(step * chunk, (step + 1) * chunk)
        tok = jnp.concatenate([piece[:half, at] for piece in got], axis=0)
        cot = jnp.concatenate([piece[half:, at] for piece in got], axis=0)
        tok_all[:, at] = tok
        cot_all[:, at] = cot
        gate = dot_nn(tok, pair[0, at, :])
        up = dot_nn(tok, pair[1, at, :])
        hid = dot_nt(cot, down[:, at])
        if step == 0:
            acc_gate[...], acc_up[...], acc_hid[...] = gate, up, hid
        else:
            acc_gate[...] += gate
            acc_up[...] += up
            acc_hid[...] += hid
    pre_gate, pre_up, hidden_grad = acc_gate[...], acc_up[...], acc_hid[...]
    sigmoid_gate = jax.nn.sigmoid(pre_gate)
    activated = pre_gate * sigmoid_gate
    hidden_out[...] = (activated * pre_up).astype(jnp.bfloat16)
    gate_grad = (
        hidden_grad * pre_up * sigmoid_gate * (1.0 + pre_gate * (1.0 - sigmoid_gate))
    ).astype(jnp.bfloat16)
    up_grad = (hidden_grad * activated).astype(jnp.bfloat16)
    gate_out[...] = gate_grad
    up_out[...] = up_grad
    me, group = lax.axis_index("expert"), lax.axis_index("dp")
    homes = []
    for index in range(count):
        source = lax.rem(group - index // near + groups, groups) * experts
        homes += [source + (me ^ (high * near + index % near)) for high in range(far)]
    copies = []
    for step in range(steps):
        at = slice(step * chunk, (step + 1) * chunk)
        value = dot_nt(gate_grad, pair[0, at, :]) + dot_nt(up_grad, pair[1, at, :])
        value = value.astype(jnp.bfloat16)
        for block, home in enumerate(homes):
            parts[home, :, at] = value[block * CAP : (block + 1) * CAP]
        where = pl.ds(step * chunk, chunk)
        one = pltpu.make_async_copy(
            parts.at[:, :, where], parts_hbm.at[:, :, where], sems.at[step]
        )
        one.start()
        copies.append(one)
    for one in copies:
        one.wait()


def expert_rows(got, pair, down, experts, groups):
    width = got[0].shape[1]
    units = down.shape[0]
    chunk = min(1024, width)
    blocks = groups * experts
    total = blocks * CAP
    return pl.pallas_call(
        functools.partial(expert_kernel, experts, groups, chunk),
        in_specs=[VMEM] * (len(got) + 2),
        out_specs=[VMEM] * 5 + [HBM],
        out_shape=[bf16(total, units)] * 3
        + [bf16(total, width)] * 2
        + [pltpu.HBM((blocks, CAP, width), jnp.bfloat16)],
        scratch_shapes=[
            pltpu.VMEM((blocks, CAP, width), jnp.bfloat16),
            pltpu.VMEM((total, units), jnp.float32),
            pltpu.VMEM((total, units), jnp.float32),
            pltpu.VMEM((total, units), jnp.float32),
            pltpu.SemaphoreType.DMA((width // chunk,)),
        ],
        compiler_params=params(28),
        cost_estimate=cost(10 * total * width * units, 6 * width * units),
        name="expert_rows",
    )(
        *got,
        pltpu.with_memory_space_constraint(pair, pltpu.VMEM),
        pltpu.with_memory_space_constraint(down, pltpu.VMEM),
    )


def pair_grad_kernel(blocks, chunk, *refs):
    toks, gate_ref, up_ref = refs[:blocks], refs[blocks], refs[blocks + 1]
    out_hbm, buffer, sems = refs[blocks + 2 :]
    width = toks[0].shape[1]
    copies = []
    for step in range(width // chunk):
        at = slice(step * chunk, (step + 1) * chunk)
        tok = jnp.concatenate([ref[:, at] for ref in toks], axis=0)
        for side, ref in enumerate((gate_ref, up_ref)):
            buffer[side, at, :] = dot_tn(tok, ref[...]).astype(jnp.bfloat16)
        where = pl.ds(step * chunk, chunk)
        one = pltpu.make_async_copy(
            buffer.at[:, where, :], out_hbm.at[0, :, where, :], sems.at[step]
        )
        one.start()
        copies.append(one)
    for one in copies:
        one.wait()


def pair_grad(toks, gate_grad, up_grad):
    blocks = len(toks)
    width = toks[0].shape[1]
    total, units = gate_grad.shape
    chunk = min(512, width)
    return pl.pallas_call(
        functools.partial(pair_grad_kernel, blocks, chunk),
        in_specs=[VMEM] * (blocks + 2),
        out_specs=HBM,
        out_shape=bf16(1, 2, width, units),
        scratch_shapes=[
            pltpu.VMEM((2, width, units), jnp.bfloat16),
            pltpu.SemaphoreType.DMA((width // chunk,)),
        ],
        compiler_params=params(32),
        cost_estimate=cost(4 * total * width * units, 4 * width * units),
        name="pair_grad",
    )(*toks, gate_grad, up_grad)


def down_grad_kernel(blocks, chunk, *refs):
    cots, hidden_ref, out_hbm = refs[:blocks], refs[blocks], refs[blocks + 1]
    buffer, sems = refs[blocks + 2 :]
    width = cots[0].shape[1]
    copies = []
    for step in range(width // chunk):
        at = slice(step * chunk, (step + 1) * chunk)
        cot = jnp.concatenate([ref[:, at] for ref in cots], axis=0)
        buffer[:, at] = dot_tn(hidden_ref[...], cot).astype(jnp.bfloat16)
        where = pl.ds(step * chunk, chunk)
        one = pltpu.make_async_copy(buffer.at[:, where], out_hbm.at[0, :, where], sems.at[step])
        one.start()
        copies.append(one)
    for one in copies:
        one.wait()


def down_grad(cots, hidden):
    blocks = len(cots)
    width = cots[0].shape[1]
    total, units = hidden.shape
    chunk = min(1024, width)
    return pl.pallas_call(
        functools.partial(down_grad_kernel, blocks, chunk),
        in_specs=[VMEM] * (blocks + 1),
        out_specs=HBM,
        out_shape=bf16(1, units, width),
        scratch_shapes=[
            pltpu.VMEM((units, width), jnp.bfloat16),
            pltpu.SemaphoreType.DMA((width // chunk,)),
        ],
        compiler_params=params(24),
        cost_estimate=cost(2 * total * width * units, 2 * width * units),
        name="down_grad",
    )(*cots, hidden)


def spread_kernel(chunk, rows_ref, place_ref, out_hbm, buffer, sems):
    blocks, _, width = rows_ref.shape
    place = jnp.concatenate([place_ref[...]] * (blocks * CAP // place_ref.shape[0]), axis=0)
    copies = []
    for step in range(width // chunk):
        at = slice(step * chunk, (step + 1) * chunk)
        rows = jnp.concatenate([rows_ref[block, :, at] for block in range(blocks)], axis=0)
        buffer[:, at] = dot_tn(place, rows).astype(jnp.bfloat16)
        where = pl.ds(step * chunk, chunk)
        one = pltpu.make_async_copy(buffer.at[:, where], out_hbm.at[:, where], sems.at[step])
        one.start()
        copies.append(one)
    for one in copies:
        one.wait()


def spread(rows, place):
    width = rows.shape[2]
    slots, tokens = place.shape
    chunk = min(1024, width)
    return pl.pallas_call(
        functools.partial(spread_kernel, chunk),
        in_specs=[VMEM] * 2,
        out_specs=HBM,
        out_shape=bf16(tokens, width),
        scratch_shapes=[
            pltpu.VMEM((tokens, width), jnp.bfloat16),
            pltpu.SemaphoreType.DMA((width // chunk,)),
        ],
        compiler_params=params(16),
        cost_estimate=cost(2 * slots * tokens * width, 2 * tokens * width),
        name="spread_rows",
    )(rows, place)


def per_device(activations, cotangent, expert_ids, gate_probs, gate_up, down_proj):
    experts = lax.axis_size("expert")
    groups = lax.axis_size("dp")
    tokens = activations.shape[0]
    far, near = factors(experts)

    def send(value, by_group, by_expert):
        if by_group == 0 and by_expert == 0:
            return value
        pairs = []
        for group in range(groups):
            to = (group + by_group) % groups
            for i in range(experts):
                pairs.append((group * experts + i, to * experts + (i ^ by_expert)))
        return lax.ppermute(value, ("dp", "expert"), pairs)

    pieces, place = route(
        expert_ids.reshape(1, tokens),
        gate_probs.reshape(1, tokens),
        activations,
        cotangent,
        experts,
    )
    pair, down = load(gate_up[0], down_proj[0], place)
    arrived = [send(pieces[high], 0, high * near) for high in reversed(range(far))]
    merged = merge(arrived[::-1], pltpu.with_memory_space_constraint(down, pltpu.VMEM))
    got = [send(merged[low], group, low) for group in range(groups) for low in range(near)]
    gate_grad, up_grad, hidden, tok, cot, parts = expert_rows(got, pair, down, experts, groups)
    returned = lax.all_to_all(parts, ("dp", "expert"), split_axis=0, concat_axis=0, tiled=True)
    down_total = down_grad([cot], hidden)
    pair_total = pair_grad([tok], gate_grad, up_grad)
    input_grad = spread(returned, place)
    return input_grad, pair_total, down_total


def solution(mesh):
    rows = P(("dp", "expert"), None)
    pair, down = P("expert", None, None, "dp"), P("expert", "dp", None)
    return jax.shard_map(
        per_device,
        mesh=mesh,
        in_specs=(rows, rows, rows, rows, pair, down),
        out_specs=(rows, pair, down),
        check_vma=False,
    )
```

profile of v0, /device:TPU:0, one launch (start us, length us, event | category | flops | bytes accessed | tf_op | source)
XLA Modules:
  0.0 66.7 jit_solution(13146394790014069552)
XLA Ops:
  0.6 2.0 %route_rows.1 = (bf16[4,4,4096]{2,1,0:T(4,128)(2,1)S(1)}, bf16[4,4,4096]{2,1,0:T(4,128)(2,1)S(1)}, bf16[4,4,4096]{2,1,0:T(4,128)(2,1)S(1)}, bf16[4,4,4096]{2,1,0:T(4,128)(2,1)S(1)}, bf16[32,128]{1,0:T(8,128)(2,1)S(1)}) custom-call(s32[1,128]{1,0:T(1,128)} %bitcast.6, f32[1,128]{1,0:T(1,128)} %bitcast.7, bf16[128,4096]{1,0:T(8,128)(2,1)} %act_hbm.1, ...), custom_call_target="tpu_custom_call" | custom-call | flops 67108864 | bytes 2097152 | tf_op jit(solution)/shard_map/route_rows/pallas_call | solution.py:111
  2.7 3.1 %collective-permute-start = (bf16[4,4,4096]{2,1,0:T(4,128)(2,1)S(1)}, bf16[4,4,4096]{2,1,0:T(4,128)(2,1)S(1)}, u32[]{:S(2)}, u32[]{:S(2)}) collective-permute-start(bf16[4,4,4096]{2,1,0:T(4,128)(2,1)S(1)} %get-tuple-element.21), channel_id=1, source_target_pairs={{0,4},{1,5},{2,6},{3,7},{4,0},{5,1},{6,2},{7,3},{8,12},{9,13},{10,... | collective-permute-start | bytes 393224 | tf_op jit(solution)/shard_map/ppermute | solution.py:395
  5.8 2.6 %collective-permute-start.1 = (bf16[4,4,4096]{2,1,0:T(4,128)(2,1)S(1)}, bf16[4,4,4096]{2,1,0:T(4,128)(2,1)S(1)}, u32[]{:S(2)}, u32[]{:S(2)}) collective-permute-start(bf16[4,4,4096]{2,1,0:T(4,128)(2,1)S(1)} %get-tuple-element.22), channel_id=1, source_target_pairs={{0,8},{1,9},{2,10},{3,11},{4,12},{5,13},{6,14},{7,15},{8,0},{9,1},... | collective-permute-start | bytes 393224 | tf_op jit(solution)/shard_map/ppermute | solution.py:395
  8.4 6.5 %load_weights.1 = (bf16[2,4096,768]{2,1,0:T(8,128)(2,1)S(1)}, bf16[768,4096]{1,0:T(8,128)(2,1)S(1)}) custom-call(bf16[2,4096,768]{2,1,0:T(8,128)(2,1)} %bitcast.4, bf16[768,4096]{1,0:T(8,128)(2,1)} %bitcast.5, bf16[32,128]{1,0:T(8,128)(2,1)S(1)} %get-tuple-element.24.after.place_ref), custom_call_target="tpu_custom_call" | custom-call | bytes 18874368 | tf_op jit(solution)/shard_map/load_weights/pallas_call | solution.py:171
  14.9 0.0 collective-permute-done.refs_1_
  14.9 3.8 %collective-permute-done.1.refs_2_ = bf16[4,4,4096]{2,1,0:T(4,128)(2,1)S(1)} collective-permute-done((bf16[4,4,4096]{2,1,0:T(4,128)(2,1)S(1)}, bf16[4,4,4096]{2,1,0:T(4,128)(2,1)S(1)}, u32[]{:S(2)}, u32[]{:S(2)}) %collective-permute-start.1) | collective-permute-done | bytes 131104 | tf_op jit(solution)/shard_map/ppermute | solution.py:395
  18.7 0.4 merge_rows.1
  19.1 1.6 %collective-permute-start.6 = (bf16[16,4096]{1,0:T(8,128)(2,1)S(1)}, bf16[16,4096]{1,0:T(8,128)(2,1)S(1)}, u32[]{:S(2)}, u32[]{:S(2)}) collective-permute-start(bf16[16,4096]{1,0:T(8,128)(2,1)S(1)} %get-tuple-element.26.refs_0_), channel_id=1, source_target_pairs={{0,16},{1,17},{2,18},{3,19},{4,20},{5,21},{6,22},{7,23},{8,24},{9,... | collective-permute-start | bytes 393224 | tf_op jit(solution)/shard_map/ppermute | solution.py:395
  20.6 0.6 collective-permute-start.3
  21.3 2.5 %collective-permute-start.8 = (bf16[16,4096]{1,0:T(8,128)(2,1)S(1)}, bf16[16,4096]{1,0:T(8,128)(2,1)S(1)}, u32[]{:S(2)}, u32[]{:S(2)}) collective-permute-start(bf16[16,4096]{1,0:T(8,128)(2,1)S(1)} %get-tuple-element.28), channel_id=1, source_target_pairs={{0,18},{1,19},{2,16},{3,17},{4,22},{5,23},{6,20},{7,21},{8,26},{9,... | collective-permute-start | bytes 393224 | tf_op jit(solution)/shard_map/ppermute | solution.py:395
  23.7 0.5 collective-permute-start.4
  24.3 2.5 %collective-permute-done.6.refs_4_ = bf16[16,4096]{1,0:T(8,128)(2,1)S(1)} collective-permute-done((bf16[16,4096]{1,0:T(8,128)(2,1)S(1)}, bf16[16,4096]{1,0:T(8,128)(2,1)S(1)}, u32[]{:S(2)}, u32[]{:S(2)}) %collective-permute-start.6) | collective-permute-done | bytes 131104 | tf_op jit(solution)/shard_map/ppermute | solution.py:395
  26.8 0.0 collective-permute-start.9
  26.8 2.4 %collective-permute-done.7.refs_5_ = bf16[16,4096]{1,0:T(8,128)(2,1)S(1)} collective-permute-done((bf16[16,4096]{1,0:T(8,128)(2,1)S(1)}, bf16[16,4096]{1,0:T(8,128)(2,1)S(1)}, u32[]{:S(2)}, u32[]{:S(2)}) %collective-permute-start.7) | collective-permute-done | bytes 131104 | tf_op jit(solution)/shard_map/ppermute | solution.py:395
  29.2 1.7 %collective-permute-start.5 = (bf16[16,4096]{1,0:T(8,128)(2,1)S(1)}, bf16[16,4096]{1,0:T(8,128)(2,1)S(1)}, u32[]{:S(2)}, u32[]{:S(2)}) collective-permute-start(bf16[16,4096]{1,0:T(8,128)(2,1)S(1)} %get-tuple-element.29), channel_id=1, source_target_pairs={{0,3},{1,2},{2,1},{3,0},{4,7},{5,6},{6,5},{7,4},{8,11},{9,10},{10,... | collective-permute-start | bytes 393224 | tf_op jit(solution)/shard_map/ppermute | solution.py:395
  30.9 0.0 collective-permute-done.3.refs_1_
  30.9 1.3 %collective-permute-done.9.refs_7_ = bf16[16,4096]{1,0:T(8,128)(2,1)S(1)} collective-permute-done((bf16[16,4096]{1,0:T(8,128)(2,1)S(1)}, bf16[16,4096]{1,0:T(8,128)(2,1)S(1)}, u32[]{:S(2)}, u32[]{:S(2)}) %collective-permute-start.9) | collective-permute-done | bytes 131104 | tf_op jit(solution)/shard_map/ppermute | solution.py:395
  32.2 3.4 %collective-permute-done.5.refs_3_ = bf16[16,4096]{1,0:T(8,128)(2,1)S(1)} collective-permute-done((bf16[16,4096]{1,0:T(8,128)(2,1)S(1)}, bf16[16,4096]{1,0:T(8,128)(2,1)S(1)}, u32[]{:S(2)}, u32[]{:S(2)}) %collective-permute-start.5) | collective-permute-done | bytes 131104 | tf_op jit(solution)/shard_map/ppermute | solution.py:395
  35.7 8.9 %expert_rows.1 = (bf16[64,768]{1,0:T(8,128)(2,1)S(1)}, bf16[64,768]{1,0:T(8,128)(2,1)S(1)}, bf16[64,768]{1,0:T(8,128)(2,1)S(1)}, bf16[64,4096]{1,0:T(8,128)(2,1)...) custom-call(bf16[16,4096]{1,0:T(8,128)(2,1)S(1)} %get-tuple-element.26.refs_0_, ...), custom_call_target="tpu_custom_call" | custom-call | flops 2013265920 | bytes 18874368 | tf_op jit(solution)/shard_map/expert_rows/pallas_call | solution.py:245
  44.6 4.9 %all-to-all-start = ((bf16[32,2,4096]{2,1,0:T(2,128)(2,1)}), bf16[32,2,4096]{2,1,0:T(2,128)(2,1)S(1)}, u32[]{:S(2)}, u32[]{:S(2)}) async-start(bf16[32,2,4096]{2,1,0:T(2,128)(2,1)} %get-tuple-element.31), calls=%async_computation | async-start | bytes 1048576 | tf_op jit(solution)/shard_map/all_to_all | solution.py:409
  49.5 3.3 %down_grad.1 = bf16[1,768,4096]{2,1,0:T(8,128)(2,1)} custom-call(bf16[64,4096]{1,0:T(8,128)(2,1)S(1)} %get-tuple-element.35.refs_0_, bf16[64,768]{1,0:T(8,128)(2,1)S(1)} %get-tuple-element.36.refs_1_), custom_call_target="tpu_custom_call" | custom-call | flops 402653184 | bytes 6291456 | tf_op jit(solution)/shard_map/down_grad/pallas_call | solution.py:331
  52.8 5.3 %pair_grad.1 = bf16[1,2,4096,768]{3,2,1,0:T(8,128)(2,1)} custom-call(bf16[64,4096]{1,0:T(8,128)(2,1)S(1)} %get-tuple-element.32.refs_0_, bf16[64,768]{1,0:T(8,128)(2,1)S(1)} %get-tuple-element.33.refs_1_, bf16[64,768]{1,0:T(8,128)(2,1)S(1)} %get-tuple-element.34.refs_2_), custom_call_target="tpu_custom_call" | custom-call | flops 805306368 | bytes 12582912 | tf_op jit(solution)/shard_map/pair_grad/pallas_call | solution.py:294
  58.1 7.1 %all-to-all-done.rows_ref = bf16[32,2,4096]{2,1,0:T(2,128)(2,1)S(1)} async-done(((bf16[32,2,4096]{2,1,0:T(2,128)(2,1)}), bf16[32,2,4096]{2,1,0:T(2,128)(2,1)S(1)}, u32[]{:S(2)}, u32[]{:S(2)}) %all-to-all-start) | async-done | bytes 524320 | tf_op jit(solution)/shard_map/all_to_all | solution.py:409
  65.2 1.4 %spread_rows.1 = bf16[128,4096]{1,0:T(8,128)(2,1)} custom-call(bf16[32,2,4096]{2,1,0:T(2,128)(2,1)S(1)} %all-to-all-done.rows_ref, bf16[32,128]{1,0:T(8,128)(2,1)S(1)} %get-tuple-element.24.after.place_ref), custom_call_target="tpu_custom_call" | custom-call | flops 33554432 | bytes 1048576 | tf_op jit(solution)/shard_map/spread_rows/pallas_call | solution.py:366
  (5 shorter events, 0.0 us)
Async XLA Ops:
  2.7 12.2 %collective-permute-start = (bf16[4,4,4096]{2,1,0:T(4,128)(2,1)S(1)}, bf16[4,4,4096]{2,1,0:T(4,128)(2,1)S(1)}, u32[]{:S(2)}, u32[]{:S(2)}) collective-permute-start(bf16[4,4,4096]{2,1,0:T(4,128)(2,1)S(1)} %get-tuple-element.21), channel_id=1, source_target_pairs={{0,4},{1,5},{2,6},{3,7},{4,0},{5,1},{6,2},{7,3},{8,12},{9,13},{10,... | collective-permute-start | bytes 393224 | tf_op jit(solution)/shard_map/ppermute | solution.py:395
  5.8 12.9 %collective-permute-start.1 = (bf16[4,4,4096]{2,1,0:T(4,128)(2,1)S(1)}, bf16[4,4,4096]{2,1,0:T(4,128)(2,1)S(1)}, u32[]{:S(2)}, u32[]{:S(2)}) collective-permute-start(bf16[4,4,4096]{2,1,0:T(4,128)(2,1)S(1)} %get-tuple-element.22), channel_id=1, source_target_pairs={{0,8},{1,9},{2,10},{3,11},{4,12},{5,13},{6,14},{7,15},{8,0},{9,1},... | collective-permute-start | bytes 393224 | tf_op jit(solution)/shard_map/ppermute | solution.py:395
  8.4 10.3 %collective-permute-start.2 = (bf16[4,4,4096]{2,1,0:T(4,128)(2,1)S(1)}, bf16[4,4,4096]{2,1,0:T(4,128)(2,1)S(1)}, u32[]{:S(2)}, u32[]{:S(2)}) collective-permute-start(bf16[4,4,4096]{2,1,0:T(4,128)(2,1)S(1)} %get-tuple-element.23), channel_id=1, source_target_pairs={{0,12},{1,13},{2,14},{3,15},{4,8},{5,9},{6,10},{7,11},{8,4},{9,5},... | collective-permute-start | bytes 393224 | tf_op jit(solution)/shard_map/ppermute | solution.py:395
  19.1 7.7 %collective-permute-start.6 = (bf16[16,4096]{1,0:T(8,128)(2,1)S(1)}, bf16[16,4096]{1,0:T(8,128)(2,1)S(1)}, u32[]{:S(2)}, u32[]{:S(2)}) collective-permute-start(bf16[16,4096]{1,0:T(8,128)(2,1)S(1)} %get-tuple-element.26.refs_0_), channel_id=1, source_target_pairs={{0,16},{1,17},{2,18},{3,19},{4,20},{5,21},{6,22},{7,23},{8,24},{9,... | collective-permute-start | bytes 393224 | tf_op jit(solution)/shard_map/ppermute | solution.py:395
  20.6 8.6 %collective-permute-start.7 = (bf16[16,4096]{1,0:T(8,128)(2,1)S(1)}, bf16[16,4096]{1,0:T(8,128)(2,1)S(1)}, u32[]{:S(2)}, u32[]{:S(2)}) collective-permute-start(bf16[16,4096]{1,0:T(8,128)(2,1)S(1)} %get-tuple-element.27), channel_id=1, source_target_pairs={{0,17},{1,16},{2,19},{3,18},{4,21},{5,20},{6,23},{7,22},{8,25},{9,... | collective-permute-start | bytes 393224 | tf_op jit(solution)/shard_map/ppermute | solution.py:395
  20.6 10.3 %collective-permute-start.3 = (bf16[16,4096]{1,0:T(8,128)(2,1)S(1)}, bf16[16,4096]{1,0:T(8,128)(2,1)S(1)}, u32[]{:S(2)}, u32[]{:S(2)}) collective-permute-start(bf16[16,4096]{1,0:T(8,128)(2,1)S(1)} %get-tuple-element.27), channel_id=1, source_target_pairs={{0,1},{1,0},{2,3},{3,2},{4,5},{5,4},{6,7},{7,6},{8,9},{9,8},{10,11... | collective-permute-start | bytes 393224 | tf_op jit(solution)/shard_map/ppermute | solution.py:395
  21.3 9.7 %collective-permute-start.8 = (bf16[16,4096]{1,0:T(8,128)(2,1)S(1)}, bf16[16,4096]{1,0:T(8,128)(2,1)S(1)}, u32[]{:S(2)}, u32[]{:S(2)}) collective-permute-start(bf16[16,4096]{1,0:T(8,128)(2,1)S(1)} %get-tuple-element.28), channel_id=1, source_target_pairs={{0,18},{1,19},{2,16},{3,17},{4,22},{5,23},{6,20},{7,21},{8,26},{9,... | collective-permute-start | bytes 393224 | tf_op jit(solution)/shard_map/ppermute | solution.py:395
  23.7 7.2 %collective-permute-start.4 = (bf16[16,4096]{1,0:T(8,128)(2,1)S(1)}, bf16[16,4096]{1,0:T(8,128)(2,1)S(1)}, u32[]{:S(2)}, u32[]{:S(2)}) collective-permute-start(bf16[16,4096]{1,0:T(8,128)(2,1)S(1)} %get-tuple-element.28), channel_id=1, source_target_pairs={{0,2},{1,3},{2,0},{3,1},{4,6},{5,7},{6,4},{7,5},{8,10},{9,11},{10,... | collective-permute-start | bytes 393224 | tf_op jit(solution)/shard_map/ppermute | solution.py:395
  26.8 5.4 %collective-permute-start.9 = (bf16[16,4096]{1,0:T(8,128)(2,1)S(1)}, bf16[16,4096]{1,0:T(8,128)(2,1)S(1)}, u32[]{:S(2)}, u32[]{:S(2)}) collective-permute-start(bf16[16,4096]{1,0:T(8,128)(2,1)S(1)} %get-tuple-element.29), channel_id=1, source_target_pairs={{0,19},{1,18},{2,17},{3,16},{4,23},{5,22},{6,21},{7,20},{8,27},{9,... | collective-permute-start | bytes 393224 | tf_op jit(solution)/shard_map/ppermute | solution.py:395
  29.2 6.4 %collective-permute-start.5 = (bf16[16,4096]{1,0:T(8,128)(2,1)S(1)}, bf16[16,4096]{1,0:T(8,128)(2,1)S(1)}, u32[]{:S(2)}, u32[]{:S(2)}) collective-permute-start(bf16[16,4096]{1,0:T(8,128)(2,1)S(1)} %get-tuple-element.29), channel_id=1, source_target_pairs={{0,3},{1,2},{2,1},{3,0},{4,7},{5,6},{6,5},{7,4},{8,11},{9,10},{10,... | collective-permute-start | bytes 393224 | tf_op jit(solution)/shard_map/ppermute | solution.py:395
  44.6 20.6 %all-to-all-start = ((bf16[32,2,4096]{2,1,0:T(2,128)(2,1)}), bf16[32,2,4096]{2,1,0:T(2,128)(2,1)S(1)}, u32[]{:S(2)}, u32[]{:S(2)}) async-start(bf16[32,2,4096]{2,1,0:T(2,128)(2,1)} %get-tuple-element.31), calls=%async_computation | async-start | bytes 1048576 | tf_op jit(solution)/shard_map/all_to_all | solution.py:409
where the time goes:
time: 67 us; the launch traced here: 66.7 us
  Pallas kernels  27.8 us (41%)
  waiting for transfers between devices  20.7 us (31%)
  starting transfers between devices  17.5 us (26%)
  between operations  0.87 us (1%)
    ppermute x10, waiting for transfers between devices, send(): return lax.ppermute(value, ('dp', 'expert'), pairs)  13.5 us
    ppermute x10, starting transfers between devices, send(): return lax.ppermute(value, ('dp', 'expert'), pairs)  12.6 us
    pallas_call x1, Pallas kernels, expert_rows(): pl.pallas_call(functools.partial(expert_kernel, experts, groups, chunk),...  8.9 us
    all_to_all x1, waiting for transfers between devices, per_device(): lax.all_to_all(parts, ('dp', 'expert'), split_axis=0, concat_axis=0, tile...  7.14 us
    pallas_call x1, Pallas kernels, load(): pl.pallas_call(functools.partial(load_kernel, chunk), in_specs=[HBM] * 2...  6.5 us
    pallas_call x1, Pallas kernels, pair_grad(): pl.pallas_call(functools.partial(pair_grad_kernel, blocks, chunk), in_spe...  5.26 us
    all_to_all x1, starting transfers between devices, per_device(): lax.all_to_all(parts, ('dp', 'expert'), split_axis=0, concat_axis=0, tile...  4.88 us
    pallas_call x1, Pallas kernels, down_grad(): pl.pallas_call(functools.partial(down_grad_kernel, blocks, chunk), in_spe...  3.32 us
  transfers between devices with their start and end apart: 11, of which 6 were waited for; matrix products, arithmetic and copies ran while one was open for 0% of the time, Pallas kernels for 23%

commit v1 on v0

--- a/solution.py
+++ b/solution.py
@@ -404,7 +404,8 @@
     pair, down = load(gate_up[0], down_proj[0], place)
     arrived = [send(pieces[high], 0, high * near) for high in reversed(range(far))]
     merged = merge(arrived[::-1], pltpu.with_memory_space_constraint(down, pltpu.VMEM))
-    got = [send(merged[low], group, low) for group in range(groups) for low in range(near)]
+    mine = [send(merged[low], 0, low) for low in range(near)]
+    got = [send(mine[low], group, 0) for group in range(groups) for low in range(near)]
     gate_grad, up_grad, hidden, tok, cot, parts = expert_rows(got, pair, down, experts, groups)
     returned = lax.all_to_all(parts, ("dp", "expert"), split_axis=0, concat_axis=0, tiled=True)
     down_total = down_grad([cot], hidden)

time: 67 us -> 67 us (level)
  transfers between devices with their start and end apart: 11 -> 11, of which waited for: 6 -> 7; matrix products, arithmetic and copies ran while one was open for 0% -> 0% of each run, Pallas kernels for 23% -> 23%
where the time goes in v1:
time: 67 us; the launch traced here: 66.8 us
  Pallas kernels  27.7 us (41%)
  waiting for transfers between devices  20.1 us (30%)
  starting transfers between devices  18.1 us (27%)
  between operations  0.87 us (1%)
    ppermute x10, waiting for transfers between devices, send(): return lax.ppermute(value, ('dp', 'expert'), pairs)  12.9 us
    ppermute x10, starting transfers between devices, send(): return lax.ppermute(value, ('dp', 'expert'), pairs)  12.7 us
    pallas_call x1, Pallas kernels, expert_rows(): pl.pallas_call(functools.partial(expert_kernel, experts, groups, chunk),...  8.9 us
    all_to_all x1, waiting for transfers between devices, per_device(): lax.all_to_all(parts, ('dp', 'expert'), split_axis=0, concat_axis=0, tile...  7.14 us
    pallas_call x1, Pallas kernels, load(): pl.pallas_call(functools.partial(load_kernel, chunk), in_specs=[HBM] * 2...  6.5 us
    all_to_all x1, starting transfers between devices, per_device(): lax.all_to_all(parts, ('dp', 'expert'), split_axis=0, concat_axis=0, tile...  5.42 us
    pallas_call x1, Pallas kernels, pair_grad(): pl.pallas_call(functools.partial(pair_grad_kernel, blocks, chunk), in_spe...  5.26 us
    pallas_call x1, Pallas kernels, down_grad(): pl.pallas_call(functools.partial(down_grad_kernel, blocks, chunk), in_spe...  3.32 us
  transfers between devices with their start and end apart: 11, of which 7 were waited for; matrix products, arithmetic and copies ran while one was open for 0% of the time, Pallas kernels for 23%

profile of v1, /device:TPU:0, one launch (start us, length us, event | category | flops | bytes accessed | tf_op | source)
XLA Modules:
  0.0 66.8 jit_solution(11502416274886847416)
XLA Ops:
  0.6 2.0 %route_rows.1 = (bf16[4,4,4096]{2,1,0:T(4,128)(2,1)S(1)}, bf16[4,4,4096]{2,1,0:T(4,128)(2,1)S(1)}, bf16[4,4,4096]{2,1,0:T(4,128)(2,1)S(1)}, bf16[4,4,4096]{2,1,0:T(4,128)(2,1)S(1)}, bf16[32,128]{1,0:T(8,128)(2,1)S(1)}) custom-call(s32[1,128]{1,0:T(1,128)} %bitcast.6, f32[1,128]{1,0:T(1,128)} %bitcast.7, bf16[128,4096]{1,0:T(8,128)(2,1)} %act_hbm.1, ...), custom_call_target="tpu_custom_call" | custom-call | flops 67108864 | bytes 2097152 | tf_op jit(solution)/shard_map/route_rows/pallas_call | solution.py:111
  2.7 3.1 %collective-permute-start = (bf16[4,4,4096]{2,1,0:T(4,128)(2,1)S(1)}, bf16[4,4,4096]{2,1,0:T(4,128)(2,1)S(1)}, u32[]{:S(2)}, u32[]{:S(2)}) collective-permute-start(bf16[4,4,4096]{2,1,0:T(4,128)(2,1)S(1)} %get-tuple-element.21), channel_id=1, source_target_pairs={{0,4},{1,5},{2,6},{3,7},{4,0},{5,1},{6,2},{7,3},{8,12},{9,13},{10,... | collective-permute-start | bytes 393224 | tf_op jit(solution)/shard_map/ppermute | solution.py:395
  5.8 2.6 %collective-permute-start.1 = (bf16[4,4,4096]{2,1,0:T(4,128)(2,1)S(1)}, bf16[4,4,4096]{2,1,0:T(4,128)(2,1)S(1)}, u32[]{:S(2)}, u32[]{:S(2)}) collective-permute-start(bf16[4,4,4096]{2,1,0:T(4,128)(2,1)S(1)} %get-tuple-element.22), channel_id=1, source_target_pairs={{0,8},{1,9},{2,10},{3,11},{4,12},{5,13},{6,14},{7,15},{8,0},{9,1},... | collective-permute-start | bytes 393224 | tf_op jit(solution)/shard_map/ppermute | solution.py:395
  8.4 6.5 %load_weights.1 = (bf16[2,4096,768]{2,1,0:T(8,128)(2,1)S(1)}, bf16[768,4096]{1,0:T(8,128)(2,1)S(1)}) custom-call(bf16[2,4096,768]{2,1,0:T(8,128)(2,1)} %bitcast.4, bf16[768,4096]{1,0:T(8,128)(2,1)} %bitcast.5, bf16[32,128]{1,0:T(8,128)(2,1)S(1)} %get-tuple-element.24.after.place_ref), custom_call_target="tpu_custom_call" | custom-call | bytes 18874368 | tf_op jit(solution)/shard_map/load_weights/pallas_call | solution.py:171
  14.9 3.8 %collective-permute-done.1.refs_2_ = bf16[4,4,4096]{2,1,0:T(4,128)(2,1)S(1)} collective-permute-done((bf16[4,4,4096]{2,1,0:T(4,128)(2,1)S(1)}, bf16[4,4,4096]{2,1,0:T(4,128)(2,1)S(1)}, u32[]{:S(2)}, u32[]{:S(2)}) %collective-permute-start.1) | collective-permute-done | bytes 131104 | tf_op jit(solution)/shard_map/ppermute | solution.py:395
  18.7 0.4 merge_rows.1
  19.1 0.1 collective-permute-start.3
  19.1 1.6 %collective-permute-start.4 = (bf16[16,4096]{1,0:T(8,128)(2,1)S(1)}, bf16[16,4096]{1,0:T(8,128)(2,1)S(1)}, u32[]{:S(2)}, u32[]{:S(2)}) collective-permute-start(bf16[16,4096]{1,0:T(8,128)(2,1)S(1)} %get-tuple-element.28), channel_id=1, source_target_pairs={{0,2},{1,3},{2,0},{3,1},{4,6},{5,7},{6,4},{7,5},{8,10},{9,11},{10,... | collective-permute-start | bytes 393224 | tf_op jit(solution)/shard_map/ppermute | solution.py:395
  20.7 0.3 collective-permute-start.5
  21.0 1.5 %collective-permute-start.6 = (bf16[16,4096]{1,0:T(8,128)(2,1)S(1)}, bf16[16,4096]{1,0:T(8,128)(2,1)S(1)}, u32[]{:S(2)}, u32[]{:S(2)}) collective-permute-start(bf16[16,4096]{1,0:T(8,128)(2,1)S(1)} %get-tuple-element.26.refs_0_), channel_id=1, source_target_pairs={{0,16},{1,17},{2,18},{3,19},{4,20},{5,21},{6,22},{7,23},{8,24},{9,... | collective-permute-start | bytes 393224 | tf_op jit(solution)/shard_map/ppermute | solution.py:395
  22.5 0.5 collective-permute-start.7
  23.0 2.5 %collective-permute-done.4.refs_2_ = bf16[16,4096]{1,0:T(8,128)(2,1)S(1)} collective-permute-done((bf16[16,4096]{1,0:T(8,128)(2,1)S(1)}, bf16[16,4096]{1,0:T(8,128)(2,1)S(1)}, u32[]{:S(2)}, u32[]{:S(2)}) %collective-permute-start.4) | collective-permute-done | bytes 131104 | tf_op jit(solution)/shard_map/ppermute | solution.py:395
  25.5 1.5 %collective-permute-start.8 = (bf16[16,4096]{1,0:T(8,128)(2,1)S(1)}, bf16[16,4096]{1,0:T(8,128)(2,1)S(1)}, u32[]{:S(2)}, u32[]{:S(2)}) collective-permute-start(bf16[16,4096]{1,0:T(8,128)(2,1)S(1)} %collective-permute-done.4.refs_2_), channel_id=1, source_target_pairs={{0,16},{1,17},{2,18},{3,19},{4,20},{5,21},{6,22},{7,23},{8,24},{9,... | collective-permute-start | bytes 393224 | tf_op jit(solution)/shard_map/ppermute | solution.py:395
  27.0 0.4 collective-permute-done.5.refs_3_
  27.4 1.5 %collective-permute-start.9 = (bf16[16,4096]{1,0:T(8,128)(2,1)S(1)}, bf16[16,4096]{1,0:T(8,128)(2,1)S(1)}, u32[]{:S(2)}, u32[]{:S(2)}) collective-permute-start(bf16[16,4096]{1,0:T(8,128)(2,1)S(1)} %collective-permute-done.5.refs_3_), channel_id=1, source_target_pairs={{0,16},{1,17},{2,18},{3,19},{4,20},{5,21},{6,22},{7,23},{8,24},{9,... | collective-permute-start | bytes 393224 | tf_op jit(solution)/shard_map/ppermute | solution.py:395
  28.9 1.2 %collective-permute-done.7.refs_5_ = bf16[16,4096]{1,0:T(8,128)(2,1)S(1)} collective-permute-done((bf16[16,4096]{1,0:T(8,128)(2,1)S(1)}, bf16[16,4096]{1,0:T(8,128)(2,1)S(1)}, u32[]{:S(2)}, u32[]{:S(2)}) %collective-permute-start.7) | collective-permute-done | bytes 131104 | tf_op jit(solution)/shard_map/ppermute | solution.py:395
  30.1 2.8 %collective-permute-done.8.refs_6_ = bf16[16,4096]{1,0:T(8,128)(2,1)S(1)} collective-permute-done((bf16[16,4096]{1,0:T(8,128)(2,1)S(1)}, bf16[16,4096]{1,0:T(8,128)(2,1)S(1)}, u32[]{:S(2)}, u32[]{:S(2)}) %collective-permute-start.8) | collective-permute-done | bytes 131104 | tf_op jit(solution)/shard_map/ppermute | solution.py:395
  32.9 2.2 %collective-permute-done.9.refs_7_ = bf16[16,4096]{1,0:T(8,128)(2,1)S(1)} collective-permute-done((bf16[16,4096]{1,0:T(8,128)(2,1)S(1)}, bf16[16,4096]{1,0:T(8,128)(2,1)S(1)}, u32[]{:S(2)}, u32[]{:S(2)}) %collective-permute-start.9) | collective-permute-done | bytes 131104 | tf_op jit(solution)/shard_map/ppermute | solution.py:395
  35.2 8.9 %expert_rows.1 = (bf16[64,768]{1,0:T(8,128)(2,1)S(1)}, bf16[64,768]{1,0:T(8,128)(2,1)S(1)}, bf16[64,768]{1,0:T(8,128)(2,1)S(1)}, bf16[64,4096]{1,0:T(8,128)(2,1)...) custom-call(bf16[16,4096]{1,0:T(8,128)(2,1)S(1)} %get-tuple-element.26.refs_0_, ...), custom_call_target="tpu_custom_call" | custom-call | flops 2013265920 | bytes 18874368 | tf_op jit(solution)/shard_map/expert_rows/pallas_call | solution.py:245
  44.1 5.4 %all-to-all-start = ((bf16[32,2,4096]{2,1,0:T(2,128)(2,1)}), bf16[32,2,4096]{2,1,0:T(2,128)(2,1)S(1)}, u32[]{:S(2)}, u32[]{:S(2)}) async-start(bf16[32,2,4096]{2,1,0:T(2,128)(2,1)} %get-tuple-element.31), calls=%async_computation | async-start | bytes 1048576 | tf_op jit(solution)/shard_map/all_to_all | solution.py:410
  49.5 3.3 %down_grad.1 = bf16[1,768,4096]{2,1,0:T(8,128)(2,1)} custom-call(bf16[64,4096]{1,0:T(8,128)(2,1)S(1)} %get-tuple-element.35.refs_0_, bf16[64,768]{1,0:T(8,128)(2,1)S(1)} %get-tuple-element.36.refs_1_), custom_call_target="tpu_custom_call" | custom-call | flops 402653184 | bytes 6291456 | tf_op jit(solution)/shard_map/down_grad/pallas_call | solution.py:331
  52.8 5.3 %pair_grad.1 = bf16[1,2,4096,768]{3,2,1,0:T(8,128)(2,1)} custom-call(bf16[64,4096]{1,0:T(8,128)(2,1)S(1)} %get-tuple-element.32.refs_0_, bf16[64,768]{1,0:T(8,128)(2,1)S(1)} %get-tuple-element.33.refs_1_, bf16[64,768]{1,0:T(8,128)(2,1)S(1)} %get-tuple-element.34.refs_2_), custom_call_target="tpu_custom_call" | custom-call | flops 805306368 | bytes 12582912 | tf_op jit(solution)/shard_map/pair_grad/pallas_call | solution.py:294
  58.1 7.1 %all-to-all-done.rows_ref = bf16[32,2,4096]{2,1,0:T(2,128)(2,1)S(1)} async-done(((bf16[32,2,4096]{2,1,0:T(2,128)(2,1)}), bf16[32,2,4096]{2,1,0:T(2,128)(2,1)S(1)}, u32[]{:S(2)}, u32[]{:S(2)}) %all-to-all-start) | async-done | bytes 524320 | tf_op jit(solution)/shard_map/all_to_all | solution.py:410
  65.2 1.4 %spread_rows.1 = bf16[128,4096]{1,0:T(8,128)(2,1)} custom-call(bf16[32,2,4096]{2,1,0:T(2,128)(2,1)S(1)} %all-to-all-done.rows_ref, bf16[32,128]{1,0:T(8,128)(2,1)S(1)} %get-tuple-element.24.after.place_ref), custom_call_target="tpu_custom_call" | custom-call | flops 33554432 | bytes 1048576 | tf_op jit(solution)/shard_map/spread_rows/pallas_call | solution.py:366
  (5 shorter events, 0.0 us)
Async XLA Ops:
  2.7 12.2 %collective-permute-start = (bf16[4,4,4096]{2,1,0:T(4,128)(2,1)S(1)}, bf16[4,4,4096]{2,1,0:T(4,128)(2,1)S(1)}, u32[]{:S(2)}, u32[]{:S(2)}) collective-permute-start(bf16[4,4,4096]{2,1,0:T(4,128)(2,1)S(1)} %get-tuple-element.21), channel_id=1, source_target_pairs={{0,4},{1,5},{2,6},{3,7},{4,0},{5,1},{6,2},{7,3},{8,12},{9,13},{10,... | collective-permute-start | bytes 393224 | tf_op jit(solution)/shard_map/ppermute | solution.py:395
  5.8 12.9 %collective-permute-start.1 = (bf16[4,4,4096]{2,1,0:T(4,128)(2,1)S(1)}, bf16[4,4,4096]{2,1,0:T(4,128)(2,1)S(1)}, u32[]{:S(2)}, u32[]{:S(2)}) collective-permute-start(bf16[4,4,4096]{2,1,0:T(4,128)(2,1)S(1)} %get-tuple-element.22), channel_id=1, source_target_pairs={{0,8},{1,9},{2,10},{3,11},{4,12},{5,13},{6,14},{7,15},{8,0},{9,1},... | collective-permute-start | bytes 393224 | tf_op jit(solution)/shard_map/ppermute | solution.py:395
  8.4 10.3 %collective-permute-start.2 = (bf16[4,4,4096]{2,1,0:T(4,128)(2,1)S(1)}, bf16[4,4,4096]{2,1,0:T(4,128)(2,1)S(1)}, u32[]{:S(2)}, u32[]{:S(2)}) collective-permute-start(bf16[4,4,4096]{2,1,0:T(4,128)(2,1)S(1)} %get-tuple-element.23), channel_id=1, source_target_pairs={{0,12},{1,13},{2,14},{3,15},{4,8},{5,9},{6,10},{7,11},{8,4},{9,5},... | collective-permute-start | bytes 393224 | tf_op jit(solution)/shard_map/ppermute | solution.py:395
  19.1 3.5 %collective-permute-start.3 = (bf16[16,4096]{1,0:T(8,128)(2,1)S(1)}, bf16[16,4096]{1,0:T(8,128)(2,1)S(1)}, u32[]{:S(2)}, u32[]{:S(2)}) collective-permute-start(bf16[16,4096]{1,0:T(8,128)(2,1)S(1)} %get-tuple-element.27), channel_id=1, source_target_pairs={{0,1},{1,0},{2,3},{3,2},{4,5},{5,4},{6,7},{7,6},{8,9},{9,8},{10,11... | collective-permute-start | bytes 393224 | tf_op jit(solution)/shard_map/ppermute | solution.py:395
  19.1 6.4 %collective-permute-start.4 = (bf16[16,4096]{1,0:T(8,128)(2,1)S(1)}, bf16[16,4096]{1,0:T(8,128)(2,1)S(1)}, u32[]{:S(2)}, u32[]{:S(2)}) collective-permute-start(bf16[16,4096]{1,0:T(8,128)(2,1)S(1)} %get-tuple-element.28), channel_id=1, source_target_pairs={{0,2},{1,3},{2,0},{3,1},{4,6},{5,7},{6,4},{7,5},{8,10},{9,11},{10,... | collective-permute-start | bytes 393224 | tf_op jit(solution)/shard_map/ppermute | solution.py:395
  20.7 6.7 %collective-permute-start.5 = (bf16[16,4096]{1,0:T(8,128)(2,1)S(1)}, bf16[16,4096]{1,0:T(8,128)(2,1)S(1)}, u32[]{:S(2)}, u32[]{:S(2)}) collective-permute-start(bf16[16,4096]{1,0:T(8,128)(2,1)S(1)} %get-tuple-element.29), channel_id=1, source_target_pairs={{0,3},{1,2},{2,1},{3,0},{4,7},{5,6},{6,5},{7,4},{8,11},{9,10},{10,... | collective-permute-start | bytes 393224 | tf_op jit(solution)/shard_map/ppermute | solution.py:395
  21.0 7.9 %collective-permute-start.6 = (bf16[16,4096]{1,0:T(8,128)(2,1)S(1)}, bf16[16,4096]{1,0:T(8,128)(2,1)S(1)}, u32[]{:S(2)}, u32[]{:S(2)}) collective-permute-start(bf16[16,4096]{1,0:T(8,128)(2,1)S(1)} %get-tuple-element.26.refs_0_), channel_id=1, source_target_pairs={{0,16},{1,17},{2,18},{3,19},{4,20},{5,21},{6,22},{7,23},{8,24},{9,... | collective-permute-start | bytes 393224 | tf_op jit(solution)/shard_map/ppermute | solution.py:395
  22.5 7.6 %collective-permute-start.7 = (bf16[16,4096]{1,0:T(8,128)(2,1)S(1)}, bf16[16,4096]{1,0:T(8,128)(2,1)S(1)}, u32[]{:S(2)}, u32[]{:S(2)}) collective-permute-start(bf16[16,4096]{1,0:T(8,128)(2,1)S(1)} %collective-permute-done.3.refs_1_), channel_id=1, source_target_pairs={{0,16},{1,17},{2,18},{3,19},{4,20},{5,21},{6,22},{7,23},{8,24},{9,... | collective-permute-start | bytes 393224 | tf_op jit(solution)/shard_map/ppermute | solution.py:395
  25.5 7.4 %collective-permute-start.8 = (bf16[16,4096]{1,0:T(8,128)(2,1)S(1)}, bf16[16,4096]{1,0:T(8,128)(2,1)S(1)}, u32[]{:S(2)}, u32[]{:S(2)}) collective-permute-start(bf16[16,4096]{1,0:T(8,128)(2,1)S(1)} %collective-permute-done.4.refs_2_), channel_id=1, source_target_pairs={{0,16},{1,17},{2,18},{3,19},{4,20},{5,21},{6,22},{7,23},{8,24},{9,... | collective-permute-start | bytes 393224 | tf_op jit(solution)/shard_map/ppermute | solution.py:395
  27.4 7.8 %collective-permute-start.9 = (bf16[16,4096]{1,0:T(8,128)(2,1)S(1)}, bf16[16,4096]{1,0:T(8,128)(2,1)S(1)}, u32[]{:S(2)}, u32[]{:S(2)}) collective-permute-start(bf16[16,4096]{1,0:T(8,128)(2,1)S(1)} %collective-permute-done.5.refs_3_), channel_id=1, source_target_pairs={{0,16},{1,17},{2,18},{3,19},{4,20},{5,21},{6,22},{7,23},{8,24},{9,... | collective-permute-start | bytes 393224 | tf_op jit(solution)/shard_map/ppermute | solution.py:395
  44.1 21.2 %all-to-all-start = ((bf16[32,2,4096]{2,1,0:T(2,128)(2,1)}), bf16[32,2,4096]{2,1,0:T(2,128)(2,1)S(1)}, u32[]{:S(2)}, u32[]{:S(2)}) async-start(bf16[32,2,4096]{2,1,0:T(2,128)(2,1)} %get-tuple-element.31), calls=%async_computation | async-start | bytes 1048576 | tf_op jit(solution)/shard_map/all_to_all | solution.py:410

commit v2 on v0

--- a/solution.py
+++ b/solution.py
@@ -128,81 +128,87 @@
 
 
 def merge_kernel(far, *refs):
-    pieces, outs = refs[:far], refs[far + 1 :]
+    pieces, outs = refs[:far], refs[len(refs) - refs[0].shape[0] :]
     for index, out in enumerate(outs):
         rows = [piece[index, :CAP, :] for piece in pieces]
         rows += [piece[index, CAP:, :] for piece in pieces]
         out[...] = jnp.concatenate(rows, axis=0)
 
 
-def merge(pieces, after):
+def merge(pieces, after=()):
     far = len(pieces)
     near, _, width = pieces[0].shape
     return pl.pallas_call(
         functools.partial(merge_kernel, far),
-        in_specs=[VMEM] * far + [pl.BlockSpec(memory_space=pl.ANY)],
+        in_specs=[VMEM] * far + [pl.BlockSpec(memory_space=pl.ANY)] * len(after),
         out_specs=[VMEM] * near,
         out_shape=[bf16(2 * CAP * far, width)] * near,
         compiler_params=params(16),
         cost_estimate=cost(0, 8 * near * CAP * far * width),
         name="merge_rows",
-    )(*pieces, after)
-
-
-def load_kernel(chunk, pair_hbm, down_hbm, after, pair, down, sems):
+    )(*pieces, *after)
+
+
+def load_kernel(chunk, pair_hbm, after, pair, sems):
     del after
-    width = down.shape[1]
+    width = pair.shape[1]
     copies = []
     for step in range(width // chunk):
         at = pl.ds(step * chunk, chunk)
-        copies += [
-            pltpu.make_async_copy(pair_hbm.at[:, at, :], pair.at[:, at, :], sems.at[0, step]),
-            pltpu.make_async_copy(down_hbm.at[:, at], down.at[:, at], sems.at[1, step]),
-        ]
+        one = pltpu.make_async_copy(pair_hbm.at[:, at, :], pair.at[:, at, :], sems.at[step])
+        one.start()
+        copies.append(one)
     for one in copies:
-        one.start()
-    for one in copies:
-        one.wait()
-
-
-def load(pair, down, after):
-    units, width = down.shape
+        one.wait()
+
+
+def load(pair, after):
+    _, width, units = pair.shape
     chunk = min(1024, width)
     return pl.pallas_call(
         functools.partial(load_kernel, chunk),
-        in_specs=[HBM] * 2 + [pl.BlockSpec(memory_space=pl.ANY)],
-        out_specs=[VMEM] * 2,
-        out_shape=[pltpu.VMEM(pair.shape, jnp.bfloat16), pltpu.VMEM(down.shape, jnp.bfloat16)],
-        scratch_shapes=[pltpu.SemaphoreType.DMA((2, width // chunk))],
-        compiler_params=params(28),
-        cost_estimate=cost(0, 6 * width * units),
+        in_specs=[HBM, pl.BlockSpec(memory_space=pl.ANY)],
+        out_specs=VMEM,
+        out_shape=pltpu.VMEM(pair.shape, jnp.bfloat16),
+        scratch_shapes=[pltpu.SemaphoreType.DMA((width // chunk,))],
+        compiler_params=params(20),
+        cost_estimate=cost(0, 4 * width * units),
         name="load_weights",
-    )(in_hbm(pair), in_hbm(down), after)
-
-
-def expert_kernel(experts, groups, chunk, *refs):
-    far, near = factors(experts)
-    count = groups * near
-    got, pair, down = refs[:count], refs[count], refs[count + 1]
+    )(in_hbm(pair), after)
+
+
+def expert_kernel(homes, experts, groups, chunk, count, *refs):
+    got, pair, down_hbm = refs[:count], refs[count], refs[count + 1]
     gate_out, up_out, hidden_out, tok_all, cot_all, parts_hbm = refs[count + 2 : count + 8]
-    parts, acc_gate, acc_up, acc_hid, sems = refs[count + 8 :]
-    half = far * CAP
+    down, parts, acc_gate, acc_up, acc_hid, sems = refs[count + 8 :]
     width = got[0].shape[1]
     steps = width // chunk
-    for step in range(steps):
-        at = slice(step * chunk, (step + 1) * chunk)
-        tok = jnp.concatenate([piece[:half, at] for piece in got], axis=0)
-        cot = jnp.concatenate([piece[half:, at] for piece in got], axis=0)
-        tok_all[:, at] = tok
-        cot_all[:, at] = cot
-        gate = dot_nn(tok, pair[0, at, :])
-        up = dot_nn(tok, pair[1, at, :])
-        hid = dot_nt(cot, down[:, at])
+    downs = []
+    for step in range(steps):
+        at = pl.ds(step * chunk, chunk)
+        one = pltpu.make_async_copy(down_hbm.at[:, at], down.at[:, at], sems.at[0, step])
+        one.start()
+        downs.append(one)
+    for step in range(steps):
+        at = slice(step * chunk, (step + 1) * chunk)
+        tok = [piece[: piece.shape[0] // 2, at] for piece in got]
+        cot = [piece[piece.shape[0] // 2 :, at] for piece in got]
+        tok_all[:, at] = jnp.concatenate(tok, axis=0)
+        cot_all[:, at] = jnp.concatenate(cot, axis=0)
+        gate = dot_nn(tok_all[:, at], pair[0, at, :])
+        up = dot_nn(tok_all[:, at], pair[1, at, :])
         if step == 0:
-            acc_gate[...], acc_up[...], acc_hid[...] = gate, up, hid
+            acc_gate[...], acc_up[...] = gate, up
         else:
             acc_gate[...] += gate
             acc_up[...] += up
+    for step in range(steps):
+        at = slice(step * chunk, (step + 1) * chunk)
+        downs[step].wait()
+        hid = dot_nt(cot_all[:, at], down[:, at])
+        if step == 0:
+            acc_hid[...] = hid
+        else:
             acc_hid[...] += hid
     pre_gate, pre_up, hidden_grad = acc_gate[...], acc_up[...], acc_hid[...]
     sigmoid_gate = jax.nn.sigmoid(pre_gate)
@@ -215,20 +221,19 @@
     gate_out[...] = gate_grad
     up_out[...] = up_grad
     me, group = lax.axis_index("expert"), lax.axis_index("dp")
-    homes = []
-    for index in range(count):
-        source = lax.rem(group - index // near + groups, groups) * experts
-        homes += [source + (me ^ (high * near + index % near)) for high in range(far)]
+    rows = [
+        lax.rem(group - back + groups, groups) * experts + (me ^ turn) for back, turn in homes
+    ]
     copies = []
     for step in range(steps):
         at = slice(step * chunk, (step + 1) * chunk)
         value = dot_nt(gate_grad, pair[0, at, :]) + dot_nt(up_grad, pair[1, at, :])
         value = value.astype(jnp.bfloat16)
-        for block, home in enumerate(homes):
-            parts[home, :, at] = value[block * CAP : (block + 1) * CAP]
+        for block, row in enumerate(rows):
+            parts[row, :, at] = value[block * CAP : (block + 1) * CAP]
         where = pl.ds(step * chunk, chunk)
         one = pltpu.make_async_copy(
-            parts.at[:, :, where], parts_hbm.at[:, :, where], sems.at[step]
+            parts.at[:, :, where], parts_hbm.at[:, :, where], sems.at[1, step]
         )
         one.start()
         copies.append(one)
@@ -236,34 +241,31 @@
         one.wait()
 
 
-def expert_rows(got, pair, down, experts, groups):
+def expert_rows(got, homes, pair, down, experts, groups):
     width = got[0].shape[1]
     units = down.shape[0]
     chunk = min(1024, width)
     blocks = groups * experts
     total = blocks * CAP
     return pl.pallas_call(
-        functools.partial(expert_kernel, experts, groups, chunk),
-        in_specs=[VMEM] * (len(got) + 2),
+        functools.partial(expert_kernel, homes, experts, groups, chunk, len(got)),
+        in_specs=[VMEM] * (len(got) + 1) + [HBM],
         out_specs=[VMEM] * 5 + [HBM],
         out_shape=[bf16(total, units)] * 3
         + [bf16(total, width)] * 2
         + [pltpu.HBM((blocks, CAP, width), jnp.bfloat16)],
         scratch_shapes=[
+            pltpu.VMEM(down.shape, jnp.bfloat16),
             pltpu.VMEM((blocks, CAP, width), jnp.bfloat16),
             pltpu.VMEM((total, units), jnp.float32),
             pltpu.VMEM((total, units), jnp.float32),
             pltpu.VMEM((total, units), jnp.float32),
-            pltpu.SemaphoreType.DMA((width // chunk,)),
+            pltpu.SemaphoreType.DMA((2, width // chunk)),
         ],
         compiler_params=params(28),
         cost_estimate=cost(10 * total * width * units, 6 * width * units),
         name="expert_rows",
-    )(
-        *got,
-        pltpu.with_memory_space_constraint(pair, pltpu.VMEM),
-        pltpu.with_memory_space_constraint(down, pltpu.VMEM),
-    )
+    )(*got, pltpu.with_memory_space_constraint(pair, pltpu.VMEM), in_hbm(down))
 
 
 def pair_grad_kernel(blocks, chunk, *refs):
@@ -401,11 +403,31 @@
         cotangent,
         experts,
     )
-    pair, down = load(gate_up[0], down_proj[0], place)
-    arrived = [send(pieces[high], 0, high * near) for high in reversed(range(far))]
-    merged = merge(arrived[::-1], pltpu.with_memory_space_constraint(down, pltpu.VMEM))
-    got = [send(merged[low], group, low) for group in range(groups) for low in range(near)]
-    gate_grad, up_grad, hidden, tok, cot, parts = expert_rows(got, pair, down, experts, groups)
+    early, late = range(far // 2), range(far // 2, far)
+    arrived = [send(pieces[high], 0, high * near) for high in late]
+    both = [send(pieces[high], group, high * near) for group in range(groups) for high in early]
+    pair = load(gate_up[0], place)
+    both = merge(both)
+    loaded = pltpu.with_memory_space_constraint(pair, pltpu.VMEM)
+    own = merge(arrived, (loaded, both[0]))
+    got = [send(both[low], 0, low) for low in range(near)]
+    mine = [send(own[low], 0, low) for low in range(near)]
+    got += [send(mine[low], group, 0) for group in range(groups) for low in range(near)]
+    homes = [
+        (group, high * near + low)
+        for low in range(near)
+        for group in range(groups)
+        for high in early
+    ]
+    homes += [
+        (group, high * near + low)
+        for group in range(groups)
+        for low in range(near)
+        for high in late
+    ]
+    gate_grad, up_grad, hidden, tok, cot, parts = expert_rows(
+        got, homes, pair, down_proj[0], experts, groups
+    )
     returned = lax.all_to_all(parts, ("dp", "expert"), split_axis=0, concat_axis=0, tiled=True)
     down_total = down_grad([cot], hidden)
     pair_total = pair_grad([tok], gate_grad, up_grad)

time: 67 us -> 66.9 us (level)
  starting transfers between devices: 17.5 us -> 23.7 us
  waiting for transfers between devices: 20.7 us -> 14.8 us
    ppermute x10 -> x15, waiting for transfers between devices: 13.5 us -> 7.61 us  [send(): return lax.ppermute(value, ('dp', 'expert'), pairs)]
    ppermute x10 -> x15, starting transfers between devices: 12.6 us -> 17.8 us  [send(): return lax.ppermute(value, ('dp', 'expert'), pairs)]
    all_to_all x1, starting transfers between devices: 4.88 us -> 5.95 us  [per_device(): lax.all_to_all(parts, ('dp', 'expert'), split_axis=0, concat_axis=0, tile...]
    pallas_call x2, Pallas kernels: 15.4 us -> 14.7 us  [the longest x1 10 us: expert_rows(): pl.pallas_call(functools.partial(expert_kernel, homes, experts, groups, c...]
  transfers between devices with their start and end apart: 11 -> 16, of which waited for: 6 -> 5; matrix products, arithmetic and copies ran while one was open for 0% -> 0% of each run, Pallas kernels for 23% -> 20%
where the time goes in v2:
time: 66.9 us; the launch traced here: 66.6 us
  Pallas kernels  27.2 us (41%)
  starting transfers between devices  23.7 us (35%)
  waiting for transfers between devices  14.8 us (22%)
  between operations  0.91 us (1%)
    ppermute x15, starting transfers between devices, send(): return lax.ppermute(value, ('dp', 'expert'), pairs)  17.8 us
    pallas_call x1, Pallas kernels, expert_rows(): pl.pallas_call(functools.partial(expert_kernel, homes, experts, groups, c...  10 us
    ppermute x15, waiting for transfers between devices, send(): return lax.ppermute(value, ('dp', 'expert'), pairs)  7.61 us
    all_to_all x1, waiting for transfers between devices, per_device(): lax.all_to_all(parts, ('dp', 'expert'), split_axis=0, concat_axis=0, tile...  7.14 us
    all_to_all x1, starting transfers between devices, per_device(): lax.all_to_all(parts, ('dp', 'expert'), split_axis=0, concat_axis=0, tile...  5.95 us
    pallas_call x1, Pallas kernels, pair_grad(): pl.pallas_call(functools.partial(pair_grad_kernel, blocks, chunk), in_spe...  5.25 us
    pallas_call x1, Pallas kernels, load(): pl.pallas_call(functools.partial(load_kernel, chunk), in_specs=[HBM, pl.B...  4.68 us
    pallas_call x1, Pallas kernels, down_grad(): pl.pallas_call(functools.partial(down_grad_kernel, blocks, chunk), in_spe...  3.33 us
  transfers between devices with their start and end apart: 16, of which 5 were waited for; matrix products, arithmetic and copies ran while one was open for 0% of the time, Pallas kernels for 20%

profile of v2, /device:TPU:0, one launch (start us, length us, event | category | flops | bytes accessed | tf_op | source)
XLA Modules:
  0.0 66.6 jit_solution(5030115931561271148)
XLA Ops:
  0.6 2.0 %route_rows.1 = (bf16[4,4,4096]{2,1,0:T(4,128)(2,1)S(1)}, bf16[4,4,4096]{2,1,0:T(4,128)(2,1)S(1)}, bf16[4,4,4096]{2,1,0:T(4,128)(2,1)S(1)}, bf16[4,4,4096]{2,1,0:T(4,128)(2,1)S(1)}, bf16[32,128]{1,0:T(8,128)(2,1)S(1)}) custom-call(s32[1,128]{1,0:T(1,128)} %bitcast.6, f32[1,128]{1,0:T(1,128)} %bitcast.7, bf16[128,4096]{1,0:T(8,128)(2,1)} %act_hbm.1, ...), custom_call_target="tpu_custom_call" | custom-call | flops 67108864 | bytes 2097152 | tf_op jit(solution)/shard_map/route_rows/pallas_call | solution.py:111
  2.7 3.1 %collective-permute-start = (bf16[4,4,4096]{2,1,0:T(4,128)(2,1)S(1)}, bf16[4,4,4096]{2,1,0:T(4,128)(2,1)S(1)}, u32[]{:S(2)}, u32[]{:S(2)}) collective-permute-start(bf16[4,4,4096]{2,1,0:T(4,128)(2,1)S(1)} %get-tuple-element.23), channel_id=1, source_target_pairs={{0,4},{1,5},{2,6},{3,7},{4,0},{5,1},{6,2},{7,3},{8,12},{9,13},{10,... | collective-permute-start | bytes 393224 | tf_op jit(solution)/shard_map/ppermute | solution.py:397
  5.7 1.4 %collective-permute-start.2 = (bf16[4,4,4096]{2,1,0:T(4,128)(2,1)S(1)}, bf16[4,4,4096]{2,1,0:T(4,128)(2,1)S(1)}, u32[]{:S(2)}, u32[]{:S(2)}) collective-permute-start(bf16[4,4,4096]{2,1,0:T(4,128)(2,1)S(1)} %get-tuple-element.23), channel_id=1, source_target_pairs={{0,20},{1,21},{2,22},{3,23},{4,16},{5,17},{6,18},{7,19},{8,28},{9,... | collective-permute-start | bytes 393224 | tf_op jit(solution)/shard_map/ppermute | solution.py:397
  7.3 3.0 %collective-permute-start.6 = (bf16[4,4,4096]{2,1,0:T(4,128)(2,1)S(1)}, bf16[4,4,4096]{2,1,0:T(4,128)(2,1)S(1)}, u32[]{:S(2)}, u32[]{:S(2)}) collective-permute-start(bf16[4,4,4096]{2,1,0:T(4,128)(2,1)S(1)} %get-tuple-element.28), channel_id=1, source_target_pairs={{0,8},{1,9},{2,10},{3,11},{4,12},{5,13},{6,14},{7,15},{8,0},{9,1},... | collective-permute-start | bytes 393224 | tf_op jit(solution)/shard_map/ppermute | solution.py:397
  10.2 1.3 %collective-permute-start.7 = (bf16[4,4,4096]{2,1,0:T(4,128)(2,1)S(1)}, bf16[4,4,4096]{2,1,0:T(4,128)(2,1)S(1)}, u32[]{:S(2)}, u32[]{:S(2)}) collective-permute-start(bf16[4,4,4096]{2,1,0:T(4,128)(2,1)S(1)} %get-tuple-element.29), channel_id=1, source_target_pairs={{0,12},{1,13},{2,14},{3,15},{4,8},{5,9},{6,10},{7,11},{8,4},{9,5},... | collective-permute-start | bytes 393224 | tf_op jit(solution)/shard_map/ppermute | solution.py:397
  11.6 4.7 %load_weights.1.refs_2_.refs_12_ = bf16[2,4096,768]{2,1,0:T(8,128)(2,1)S(1)} custom-call(bf16[2,4096,768]{2,1,0:T(8,128)(2,1)} %bitcast.4, bf16[32,128]{1,0:T(8,128)(2,1)S(1)} %get-tuple-element.30.after.place_ref), custom_call_target="tpu_custom_call" | custom-call | bytes 12582912 | tf_op jit(solution)/shard_map/load_weights/pallas_call | solution.py:168
  16.3 0.4 merge_rows.2
  16.7 3.3 %collective-permute-done.7.refs_1_ = bf16[4,4,4096]{2,1,0:T(4,128)(2,1)S(1)} collective-permute-done((bf16[4,4,4096]{2,1,0:T(4,128)(2,1)S(1)}, bf16[4,4,4096]{2,1,0:T(4,128)(2,1)S(1)}, u32[]{:S(2)}, u32[]{:S(2)}) %collective-permute-start.7) | collective-permute-done | bytes 131104 | tf_op jit(solution)/shard_map/ppermute | solution.py:397
  20.3 1.7 %collective-permute-start.9 = (bf16[8,4096]{1,0:T(8,128)(2,1)S(1)}, bf16[8,4096]{1,0:T(8,128)(2,1)S(1)}, u32[]{:S(2)}, u32[]{:S(2)}) collective-permute-start(bf16[8,4096]{1,0:T(8,128)(2,1)S(1)} %get-tuple-element.33), channel_id=1, source_target_pairs={{0,2},{1,3},{2,0},{3,1},{4,6},{5,7},{6,4},{7,5},{8,10},{9,11},{10,... | collective-permute-start | bytes 196616 | tf_op jit(solution)/shard_map/ppermute | solution.py:397
  22.1 1.7 %collective-permute-start.11 = (bf16[8,4096]{1,0:T(8,128)(2,1)S(1)}, bf16[8,4096]{1,0:T(8,128)(2,1)S(1)}, u32[]{:S(2)}, u32[]{:S(2)}) collective-permute-start(bf16[8,4096]{1,0:T(8,128)(2,1)S(1)} %get-tuple-element.31.refs_4_), channel_id=1, source_target_pairs={{0,16},{1,17},{2,18},{3,19},{4,20},{5,21},{6,22},{7,23},{8,24},{9,... | collective-permute-start | bytes 196616 | tf_op jit(solution)/shard_map/ppermute | solution.py:397
  23.9 0.4 collective-permute-start.12
  24.2 0.6 collective-permute-done.9.refs_6_
  24.8 2.1 %collective-permute-start.4 = (bf16[16,4096]{1,0:T(8,128)(2,1)S(1)}, bf16[16,4096]{1,0:T(8,128)(2,1)S(1)}, u32[]{:S(2)}, u32[]{:S(2)}) collective-permute-start(bf16[16,4096]{1,0:T(8,128)(2,1)S(1)} %get-tuple-element.26), channel_id=1, source_target_pairs={{0,2},{1,3},{2,0},{3,1},{4,6},{5,7},{6,4},{7,5},{8,10},{9,11},{10,... | collective-permute-start | bytes 393224 | tf_op jit(solution)/shard_map/ppermute | solution.py:397
  26.9 0.7 %collective-permute-start.5 = (bf16[16,4096]{1,0:T(8,128)(2,1)S(1)}, bf16[16,4096]{1,0:T(8,128)(2,1)S(1)}, u32[]{:S(2)}, u32[]{:S(2)}) collective-permute-start(bf16[16,4096]{1,0:T(8,128)(2,1)S(1)} %get-tuple-element.27), channel_id=1, source_target_pairs={{0,3},{1,2},{2,1},{3,0},{4,7},{5,6},{6,5},{7,4},{8,11},{9,10},{10,... | collective-permute-start | bytes 393224 | tf_op jit(solution)/shard_map/ppermute | solution.py:397
  27.6 1.5 %collective-permute-start.13 = (bf16[8,4096]{1,0:T(8,128)(2,1)S(1)}, bf16[8,4096]{1,0:T(8,128)(2,1)S(1)}, u32[]{:S(2)}, u32[]{:S(2)}) collective-permute-start(bf16[8,4096]{1,0:T(8,128)(2,1)S(1)} %collective-permute-done.9.refs_6_), channel_id=1, source_target_pairs={{0,16},{1,17},{2,18},{3,19},{4,20},{5,21},{6,22},{7,23},{8,24},{9,... | collective-permute-start | bytes 196616 | tf_op jit(solution)/shard_map/ppermute | solution.py:397
  29.1 0.5 collective-permute-start.14
  29.6 2.7 %collective-permute-done.13.refs_10_ = bf16[8,4096]{1,0:T(8,128)(2,1)S(1)} collective-permute-done((bf16[8,4096]{1,0:T(8,128)(2,1)S(1)}, bf16[8,4096]{1,0:T(8,128)(2,1)S(1)}, u32[]{:S(2)}, u32[]{:S(2)}) %collective-permute-start.13) | collective-permute-done | bytes 65568 | tf_op jit(solution)/shard_map/ppermute | solution.py:397
  32.4 1.0 %collective-permute-done.14.refs_11_ = bf16[8,4096]{1,0:T(8,128)(2,1)S(1)} collective-permute-done((bf16[8,4096]{1,0:T(8,128)(2,1)S(1)}, bf16[8,4096]{1,0:T(8,128)(2,1)S(1)}, u32[]{:S(2)}, u32[]{:S(2)}) %collective-permute-start.14) | collective-permute-done | bytes 65568 | tf_op jit(solution)/shard_map/ppermute | solution.py:397
  33.4 10.0 %expert_rows.1 = (bf16[64,768]{1,0:T(8,128)(2,1)S(1)}, bf16[64,768]{1,0:T(8,128)(2,1)S(1)}, bf16[64,768]{1,0:T(8,128)(2,1)S(1)}, bf16[64,4096]{1,0:T(8,128)(2,1)...) custom-call(bf16[16,4096]{1,0:T(8,128)(2,1)S(1)} %get-tuple-element.24.refs_3_.refs_0_, ...), custom_call_target="tpu_custom_call" | custom-call | flops 2013265920 | bytes 18874368 | tf_op jit(solution)/shard_map/expert_rows/pallas_call | solution.py:250
  43.4 5.9 %all-to-all-start = ((bf16[32,2,4096]{2,1,0:T(2,128)(2,1)}), bf16[32,2,4096]{2,1,0:T(2,128)(2,1)S(1)}, u32[]{:S(2)}, u32[]{:S(2)}) async-start(bf16[32,2,4096]{2,1,0:T(2,128)(2,1)} %get-tuple-element.35), calls=%async_computation | async-start | bytes 1048576 | tf_op jit(solution)/shard_map/all_to_all | solution.py:431
  49.4 3.3 %down_grad.1 = bf16[1,768,4096]{2,1,0:T(8,128)(2,1)} custom-call(bf16[64,4096]{1,0:T(8,128)(2,1)S(1)} %get-tuple-element.39.refs_0_, bf16[64,768]{1,0:T(8,128)(2,1)S(1)} %get-tuple-element.40.refs_1_), custom_call_target="tpu_custom_call" | custom-call | flops 402653184 | bytes 6291456 | tf_op jit(solution)/shard_map/down_grad/pallas_call | solution.py:333
  52.7 5.3 %pair_grad.1 = bf16[1,2,4096,768]{3,2,1,0:T(8,128)(2,1)} custom-call(bf16[64,4096]{1,0:T(8,128)(2,1)S(1)} %get-tuple-element.36.refs_0_, bf16[64,768]{1,0:T(8,128)(2,1)S(1)} %get-tuple-element.37.refs_1_, bf16[64,768]{1,0:T(8,128)(2,1)S(1)} %get-tuple-element.38.refs_2_), custom_call_target="tpu_custom_call" | custom-call | flops 805306368 | bytes 12582912 | tf_op jit(solution)/shard_map/pair_grad/pallas_call | solution.py:296
  58.0 7.1 %all-to-all-done.rows_ref = bf16[32,2,4096]{2,1,0:T(2,128)(2,1)S(1)} async-done(((bf16[32,2,4096]{2,1,0:T(2,128)(2,1)}), bf16[32,2,4096]{2,1,0:T(2,128)(2,1)S(1)}, u32[]{:S(2)}, u32[]{:S(2)}) %all-to-all-start) | async-done | bytes 524320 | tf_op jit(solution)/shard_map/all_to_all | solution.py:431
  65.1 1.3 %spread_rows.1 = bf16[128,4096]{1,0:T(8,128)(2,1)} custom-call(bf16[32,2,4096]{2,1,0:T(2,128)(2,1)S(1)} %all-to-all-done.rows_ref, bf16[32,128]{1,0:T(8,128)(2,1)S(1)} %get-tuple-element.30.after.place_ref), custom_call_target="tpu_custom_call" | custom-call | flops 33554432 | bytes 1048576 | tf_op jit(solution)/shard_map/spread_rows/pallas_call | solution.py:368
  (16 shorter events, 0.6 us)
Async XLA Ops:
  2.7 13.6 %collective-permute-start = (bf16[4,4,4096]{2,1,0:T(4,128)(2,1)S(1)}, bf16[4,4,4096]{2,1,0:T(4,128)(2,1)S(1)}, u32[]{:S(2)}, u32[]{:S(2)}) collective-permute-start(bf16[4,4,4096]{2,1,0:T(4,128)(2,1)S(1)} %get-tuple-element.23), channel_id=1, source_target_pairs={{0,4},{1,5},{2,6},{3,7},{4,0},{5,1},{6,2},{7,3},{8,12},{9,13},{10,... | collective-permute-start | bytes 393224 | tf_op jit(solution)/shard_map/ppermute | solution.py:397
  5.7 10.6 %collective-permute-start.2 = (bf16[4,4,4096]{2,1,0:T(4,128)(2,1)S(1)}, bf16[4,4,4096]{2,1,0:T(4,128)(2,1)S(1)}, u32[]{:S(2)}, u32[]{:S(2)}) collective-permute-start(bf16[4,4,4096]{2,1,0:T(4,128)(2,1)S(1)} %get-tuple-element.23), channel_id=1, source_target_pairs={{0,20},{1,21},{2,22},{3,23},{4,16},{5,17},{6,18},{7,19},{8,28},{9,... | collective-permute-start | bytes 393224 | tf_op jit(solution)/shard_map/ppermute | solution.py:397
  7.1 9.2 %collective-permute-start.1 = (bf16[4,4,4096]{2,1,0:T(4,128)(2,1)S(1)}, bf16[4,4,4096]{2,1,0:T(4,128)(2,1)S(1)}, u32[]{:S(2)}, u32[]{:S(2)}) collective-permute-start(bf16[4,4,4096]{2,1,0:T(4,128)(2,1)S(1)} %get-tuple-element.22.refs_0_), channel_id=1, source_target_pairs={{0,16},{1,17},{2,18},{3,19},{4,20},{5,21},{6,22},{7,23},{8,24},{9,... | collective-permute-start | bytes 393224 | tf_op jit(solution)/shard_map/ppermute | solution.py:397
  7.3 9.4 %collective-permute-start.6 = (bf16[4,4,4096]{2,1,0:T(4,128)(2,1)S(1)}, bf16[4,4,4096]{2,1,0:T(4,128)(2,1)S(1)}, u32[]{:S(2)}, u32[]{:S(2)}) collective-permute-start(bf16[4,4,4096]{2,1,0:T(4,128)(2,1)S(1)} %get-tuple-element.28), channel_id=1, source_target_pairs={{0,8},{1,9},{2,10},{3,11},{4,12},{5,13},{6,14},{7,15},{8,0},{9,1},... | collective-permute-start | bytes 393224 | tf_op jit(solution)/shard_map/ppermute | solution.py:397
  10.2 9.8 %collective-permute-start.7 = (bf16[4,4,4096]{2,1,0:T(4,128)(2,1)S(1)}, bf16[4,4,4096]{2,1,0:T(4,128)(2,1)S(1)}, u32[]{:S(2)}, u32[]{:S(2)}) collective-permute-start(bf16[4,4,4096]{2,1,0:T(4,128)(2,1)S(1)} %get-tuple-element.29), channel_id=1, source_target_pairs={{0,12},{1,13},{2,14},{3,15},{4,8},{5,9},{6,10},{7,11},{8,4},{9,5},... | collective-permute-start | bytes 393224 | tf_op jit(solution)/shard_map/ppermute | solution.py:397
  20.2 3.7 %collective-permute-start.8 = (bf16[8,4096]{1,0:T(8,128)(2,1)S(1)}, bf16[8,4096]{1,0:T(8,128)(2,1)S(1)}, u32[]{:S(2)}, u32[]{:S(2)}) collective-permute-start(bf16[8,4096]{1,0:T(8,128)(2,1)S(1)} %get-tuple-element.32), channel_id=1, source_target_pairs={{0,1},{1,0},{2,3},{3,2},{4,5},{5,4},{6,7},{7,6},{8,9},{9,8},{10,11... | collective-permute-start | bytes 196616 | tf_op jit(solution)/shard_map/ppermute | solution.py:397
  20.3 4.5 %collective-permute-start.9 = (bf16[8,4096]{1,0:T(8,128)(2,1)S(1)}, bf16[8,4096]{1,0:T(8,128)(2,1)S(1)}, u32[]{:S(2)}, u32[]{:S(2)}) collective-permute-start(bf16[8,4096]{1,0:T(8,128)(2,1)S(1)} %get-tuple-element.33), channel_id=1, source_target_pairs={{0,2},{1,3},{2,0},{3,1},{4,6},{5,7},{6,4},{7,5},{8,10},{9,11},{10,... | collective-permute-start | bytes 196616 | tf_op jit(solution)/shard_map/ppermute | solution.py:397
  22.0 4.9 %collective-permute-start.10 = (bf16[8,4096]{1,0:T(8,128)(2,1)S(1)}, bf16[8,4096]{1,0:T(8,128)(2,1)S(1)}, u32[]{:S(2)}, u32[]{:S(2)}) collective-permute-start(bf16[8,4096]{1,0:T(8,128)(2,1)S(1)} %get-tuple-element.34), channel_id=1, source_target_pairs={{0,3},{1,2},{2,1},{3,0},{4,7},{5,6},{6,5},{7,4},{8,11},{9,10},{10,... | collective-permute-start | bytes 196616 | tf_op jit(solution)/shard_map/ppermute | solution.py:397
  22.1 5.4 %collective-permute-start.11 = (bf16[8,4096]{1,0:T(8,128)(2,1)S(1)}, bf16[8,4096]{1,0:T(8,128)(2,1)S(1)}, u32[]{:S(2)}, u32[]{:S(2)}) collective-permute-start(bf16[8,4096]{1,0:T(8,128)(2,1)S(1)} %get-tuple-element.31.refs_4_), channel_id=1, source_target_pairs={{0,16},{1,17},{2,18},{3,19},{4,20},{5,21},{6,22},{7,23},{8,24},{9,... | collective-permute-start | bytes 196616 | tf_op jit(solution)/shard_map/ppermute | solution.py:397
  23.8 9.5 %collective-permute-start.3 = (bf16[16,4096]{1,0:T(8,128)(2,1)S(1)}, bf16[16,4096]{1,0:T(8,128)(2,1)S(1)}, u32[]{:S(2)}, u32[]{:S(2)}) collective-permute-start(bf16[16,4096]{1,0:T(8,128)(2,1)S(1)} %get-tuple-element.25), channel_id=1, source_target_pairs={{0,1},{1,0},{2,3},{3,2},{4,5},{5,4},{6,7},{7,6},{8,9},{9,8},{10,11... | collective-permute-start | bytes 393224 | tf_op jit(solution)/shard_map/ppermute | solution.py:397
  23.9 5.2 %collective-permute-start.12 = (bf16[8,4096]{1,0:T(8,128)(2,1)S(1)}, bf16[8,4096]{1,0:T(8,128)(2,1)S(1)}, u32[]{:S(2)}, u32[]{:S(2)}) collective-permute-start(bf16[8,4096]{1,0:T(8,128)(2,1)S(1)} %collective-permute-done.8.refs_5_), channel_id=1, source_target_pairs={{0,16},{1,17},{2,18},{3,19},{4,20},{5,21},{6,22},{7,23},{8,24},{9,... | collective-permute-start | bytes 196616 | tf_op jit(solution)/shard_map/ppermute | solution.py:397
  24.8 8.6 %collective-permute-start.4 = (bf16[16,4096]{1,0:T(8,128)(2,1)S(1)}, bf16[16,4096]{1,0:T(8,128)(2,1)S(1)}, u32[]{:S(2)}, u32[]{:S(2)}) collective-permute-start(bf16[16,4096]{1,0:T(8,128)(2,1)S(1)} %get-tuple-element.26), channel_id=1, source_target_pairs={{0,2},{1,3},{2,0},{3,1},{4,6},{5,7},{6,4},{7,5},{8,10},{9,11},{10,... | collective-permute-start | bytes 393224 | tf_op jit(solution)/shard_map/ppermute | solution.py:397
  26.9 6.4 %collective-permute-start.5 = (bf16[16,4096]{1,0:T(8,128)(2,1)S(1)}, bf16[16,4096]{1,0:T(8,128)(2,1)S(1)}, u32[]{:S(2)}, u32[]{:S(2)}) collective-permute-start(bf16[16,4096]{1,0:T(8,128)(2,1)S(1)} %get-tuple-element.27), channel_id=1, source_target_pairs={{0,3},{1,2},{2,1},{3,0},{4,7},{5,6},{6,5},{7,4},{8,11},{9,10},{10,... | collective-permute-start | bytes 393224 | tf_op jit(solution)/shard_map/ppermute | solution.py:397
  27.6 4.8 %collective-permute-start.13 = (bf16[8,4096]{1,0:T(8,128)(2,1)S(1)}, bf16[8,4096]{1,0:T(8,128)(2,1)S(1)}, u32[]{:S(2)}, u32[]{:S(2)}) collective-permute-start(bf16[8,4096]{1,0:T(8,128)(2,1)S(1)} %collective-permute-done.9.refs_6_), channel_id=1, source_target_pairs={{0,16},{1,17},{2,18},{3,19},{4,20},{5,21},{6,22},{7,23},{8,24},{9,... | collective-permute-start | bytes 196616 | tf_op jit(solution)/shard_map/ppermute | solution.py:397
  29.1 4.3 %collective-permute-start.14 = (bf16[8,4096]{1,0:T(8,128)(2,1)S(1)}, bf16[8,4096]{1,0:T(8,128)(2,1)S(1)}, u32[]{:S(2)}, u32[]{:S(2)}) collective-permute-start(bf16[8,4096]{1,0:T(8,128)(2,1)S(1)} %collective-permute-done.10.refs_7_), channel_id=1, source_target_pairs={{0,16},{1,17},{2,18},{3,19},{4,20},{5,21},{6,22},{7,23},{8,24},{9,... | collective-permute-start | bytes 196616 | tf_op jit(solution)/shard_map/ppermute | solution.py:397
  43.4 21.7 %all-to-all-start = ((bf16[32,2,4096]{2,1,0:T(2,128)(2,1)}), bf16[32,2,4096]{2,1,0:T(2,128)(2,1)S(1)}, u32[]{:S(2)}, u32[]{:S(2)}) async-start(bf16[32,2,4096]{2,1,0:T(2,128)(2,1)} %get-tuple-element.35), calls=%async_computation | async-start | bytes 1048576 | tf_op jit(solution)/shard_map/all_to_all | solution.py:431

commit v3 on v0

v3 whole, which is shorter than its diff:
```python
import functools

import jax
import jax.numpy as jnp
from jax import lax
from jax.experimental import pallas as pl
from jax.experimental.pallas import tpu as pltpu
from jax.sharding import PartitionSpec as P

CAP = 2
HALVES = 2
MIB = 1024 * 1024
VMEM = pl.BlockSpec(memory_space=pltpu.VMEM)
HBM = pl.BlockSpec(memory_space=pltpu.HBM)


def dot_nn(a, b):
    return lax.dot_general(a, b, (((1,), (0,)), ((), ())), preferred_element_type=jnp.float32)


def dot_nt(a, b):
    return lax.dot_general(a, b, (((1,), (1,)), ((), ())), preferred_element_type=jnp.float32)


def dot_tn(a, b):
    return lax.dot_general(a, b, (((0,), (0,)), ((), ())), preferred_element_type=jnp.float32)


def cost(flops, moved):
    return pl.CostEstimate(flops=int(flops), bytes_accessed=int(moved), transcendentals=0)


def params(mib):
    return pltpu.CompilerParams(vmem_limit_bytes=mib * MIB)


def in_hbm(value):
    return pltpu.with_memory_space_constraint(value, pltpu.HBM)


def bf16(*shape):
    return jax.ShapeDtypeStruct(shape, jnp.bfloat16)


def factors(experts):
    far = 1
    while 4 * far * far <= experts:
        far *= 2
    return far, experts // far


def route_kernel(experts, chunk, ids_hbm, probs_hbm, act_hbm, cot_hbm, *refs):
    far, near = factors(experts)
    sends, place_ref = refs[: HALVES * far], refs[HALVES * far]
    ids_ref, probs_ref, act, cot, sems = refs[HALVES * far + 1 :]
    tokens, width = act.shape
    half = width // HALVES
    steps = width // chunk
    small = (
        pltpu.make_async_copy(ids_hbm, ids_ref, sems.at[2 * steps]),
        pltpu.make_async_copy(probs_hbm, probs_ref, sems.at[2 * steps + 1]),
    )
    large = []
    for step in range(steps):
        at = pl.ds(step * chunk, chunk)
        large.append(
            (
                pltpu.make_async_copy(act_hbm.at[:, at], act.at[:, at], sems.at[2 * step]),
                pltpu.make_async_copy(cot_hbm.at[:, at], cot.at[:, at], sems.at[2 * step + 1]),
            )
        )
    for one in small:
        one.start()
    for pair in large:
        for one in pair:
            one.start()
    for one in small:
        one.wait()

    me = lax.axis_index("expert")
    ids = ids_ref[...]
    inside = ids < experts
    units = lax.broadcasted_iota(jnp.int32, (experts, tokens), 0)
    onehot = jnp.where(units == ids, 1.0, 0.0)
    earlier = lax.broadcasted_iota(jnp.int32, (tokens, tokens), 0) < lax.broadcasted_iota(
        jnp.int32, (tokens, tokens), 1
    )
    before = dot_nn(onehot.astype(jnp.bfloat16), jnp.where(earlier, 1.0, 0.0).astype(jnp.bfloat16))
    rank = jnp.sum(before * onehot, axis=0, keepdims=True).astype(jnp.int32)
    slots = lax.broadcasted_iota(jnp.int32, (experts * CAP, tokens), 0)
    slot = jnp.where(inside, ids * CAP + rank, -1)
    place_ref[...] = jnp.where(slots == slot, 1.0, 0.0).astype(jnp.bfloat16)
    turned = jnp.where(inside, (ids ^ me) * CAP + rank, -1)
    pick = jnp.where(slots == turned, 1.0, 0.0)
    weight = jnp.sum(pick * probs_ref[...], axis=1, keepdims=True)
    pick = pick.astype(jnp.bfloat16)
    for step in range(steps):
        at = slice(step * chunk, (step + 1) * chunk)
        for one in large[step]:
            one.wait()
        rows_tok = dot_nn(pick, act[:, at]).astype(jnp.bfloat16)
        rows_cot = (weight * dot_nn(pick, cot[:, at])).astype(jnp.bfloat16)
        for unit in range(experts):
            rows = slice(unit * CAP, (unit + 1) * CAP)
            target = sends[step * chunk // half * far + unit // near]
            there = slice(step * chunk % half, step * chunk % half + chunk)
            target[unit % near, :CAP, there] = rows_tok[rows]
            target[unit % near, CAP:, there] = rows_cot[rows]


def route(ids, probs, act, cot, experts):
    tokens, width = act.shape
    chunk = min(1024, width // HALVES)
    far, near = factors(experts)
    out = pl.pallas_call(
        functools.partial(route_kernel, experts, chunk),
        in_specs=[HBM] * 4,
        out_specs=[VMEM] * (HALVES * far + 1),
        out_shape=[bf16(near, 2 * CAP, width // HALVES)] * (HALVES * far)
        + [bf16(experts * CAP, tokens)],
        scratch_shapes=[
            pltpu.VMEM((1, tokens), jnp.int32),
            pltpu.VMEM((1, tokens), jnp.float32),
            pltpu.VMEM((tokens, width), jnp.bfloat16),
            pltpu.VMEM((tokens, width), jnp.bfloat16),
            pltpu.SemaphoreType.DMA((2 * (width // chunk) + 2,)),
        ],
        compiler_params=params(16),
        cost_estimate=cost(4 * experts * CAP * tokens * width, 4 * tokens * width),
        name="route_rows",
    )(in_hbm(ids), in_hbm(probs), in_hbm(act), in_hbm(cot))
    return [out[half * far : (half + 1) * far] for half in range(HALVES)], out[HALVES * far]


def merge_kernel(far, *refs):
    pieces, outs = refs[:far], refs[far:]
    for index, out in enumerate(outs):
        rows = [piece[index, :CAP, :] for piece in pieces]
        rows += [piece[index, CAP:, :] for piece in pieces]
        out[...] = jnp.concatenate(rows, axis=0)


def merge(pieces):
    far = len(pieces)
    near, _, width = pieces[0].shape
    return pl.pallas_call(
        functools.partial(merge_kernel, far),
        in_specs=[VMEM] * far,
        out_specs=[VMEM] * near,
        out_shape=[bf16(2 * CAP * far, width)] * near,
        compiler_params=params(16),
        cost_estimate=cost(0, 8 * near * CAP * far * width),
        name="merge_rows",
    )(*pieces)


def stack_kernel(number, *refs):
    pieces, out = refs[:number], refs[number]
    rows = pieces[0].shape[0] // 2
    for index, piece in enumerate(pieces):
        out[index * rows : (index + 1) * rows, :] = piece[:rows, :]
        out[(number + index) * rows : (number + index + 1) * rows, :] = piece[rows:, :]


def stack(pieces):
    number = len(pieces)
    rows, width = pieces[0].shape
    return pl.pallas_call(
        functools.partial(stack_kernel, number),
        in_specs=[VMEM] * number,
        out_specs=VMEM,
        out_shape=bf16(number * rows, width),
        compiler_params=params(16),
        cost_estimate=cost(0, 4 * number * rows * width),
        name="stack_rows",
    )(*pieces)


def upper(refs, at):
    return jnp.concatenate([ref[: ref.shape[0] // 2, at] for ref in refs], axis=0)


def lower(refs, at):
    return jnp.concatenate([ref[ref.shape[0] // 2 :, at] for ref in refs], axis=0)


def first_kernel(groups, chunk, *refs):
    rows, pair_hbm, down_hbm = refs[:groups], refs[groups], refs[groups + 1]
    gate, up, hid, pair, down, sems = refs[groups + 2 :]
    half, width = rows[0].shape[1], down.shape[1]
    pairs, downs = [], []
    for step in range(width // chunk):
        at = pl.ds(step * chunk, chunk)
        pairs.append(
            pltpu.make_async_copy(pair_hbm.at[:, at, :], pair.at[:, at, :], sems.at[0, step])
        )
        downs.append(pltpu.make_async_copy(down_hbm.at[:, at], down.at[:, at], sems.at[1, step]))
        pairs[step].start()
        downs[step].start()
    for step in range(half // chunk):
        at = slice(step * chunk, (step + 1) * chunk)
        tok, cot = upper(rows, at), lower(rows, at)
        pairs[step].wait()
        part_gate = dot_nn(tok, pair[0, at, :])
        part_up = dot_nn(tok, pair[1, at, :])
        downs[step].wait()
        part_hid = dot_nt(cot, down[:, at])
        if step == 0:
            gate[...], up[...], hid[...] = part_gate, part_up, part_hid
        else:
            gate[...] += part_gate
            up[...] += part_up
            hid[...] += part_hid
    for step in range(half // chunk, width // chunk):
        pairs[step].wait()
        downs[step].wait()


def first_half(rows, pair, down):
    groups = len(rows)
    total = groups * rows[0].shape[0] // 2
    half = rows[0].shape[1]
    units, width = down.shape
    chunk = min(1024, half)
    return pl.pallas_call(
        functools.partial(first_kernel, groups, chunk),
        in_specs=[VMEM] * groups + [HBM] * 2,
        out_specs=[VMEM] * 5,
        out_shape=[jax.ShapeDtypeStruct((total, units), jnp.float32)] * 3
        + [pltpu.VMEM(pair.shape, jnp.bfloat16), pltpu.VMEM(down.shape, jnp.bfloat16)],
        scratch_shapes=[pltpu.SemaphoreType.DMA((2, width // chunk))],
        compiler_params=params(28),
        cost_estimate=cost(6 * total * half * units, 6 * width * units),
        name="first_half",
    )(*rows, in_hbm(pair), in_hbm(down))


def second_kernel(homes, experts, groups, chunk, *refs):
    rows, sums = refs[:groups], refs[groups : groups + 3]
    pair, down = refs[groups + 3 : groups + 5]
    gate_out, up_out, hidden_out, parts_hbm, parts, sems = refs[groups + 5 :]
    half, width = rows[0].shape[1], down.shape[1]
    pre_gate, pre_up, hidden_grad = (ref[...] for ref in sums)
    for step in range(half // chunk):
        at = slice(step * chunk, (step + 1) * chunk)
        there = slice(half + step * chunk, half + (step + 1) * chunk)
        tok, cot = upper(rows, at), lower(rows, at)
        pre_gate = pre_gate + dot_nn(tok, pair[0, there, :])
        pre_up = pre_up + dot_nn(tok, pair[1, there, :])
        hidden_grad = hidden_grad + dot_nt(cot, down[:, there])
    sigmoid_gate = jax.nn.sigmoid(pre_gate)
    activated = pre_gate * sigmoid_gate
    hidden_out[...] = (activated * pre_up).astype(jnp.bfloat16)
    gate_grad = (
        hidden_grad * pre_up * sigmoid_gate * (1.0 + pre_gate * (1.0 - sigmoid_gate))
    ).astype(jnp.bfloat16)
    up_grad = (hidden_grad * activated).astype(jnp.bfloat16)
    gate_out[...] = gate_grad
    up_out[...] = up_grad
    me, group = lax.axis_index("expert"), lax.axis_index("dp")
    targets = [
        lax.rem(group - back + groups, groups) * experts + (me ^ turn) for back, turn in homes
    ]
    copies = []
    for step in range(width // chunk):
        at = slice(step * chunk, (step + 1) * chunk)
        value = dot_nt(gate_grad, pair[0, at, :]) + dot_nt(up_grad, pair[1, at, :])
        value = value.astype(jnp.bfloat16)
        for block, target in enumerate(targets):
            parts[target, :, at] = value[block * CAP : (block + 1) * CAP]
        where = pl.ds(step * chunk, chunk)
        one = pltpu.make_async_copy(
            parts.at[:, :, where], parts_hbm.at[:, :, where], sems.at[step]
        )
        one.start()
        copies.append(one)
    for one in copies:
        one.wait()


def second_half(rows, sums, pair, down, homes, experts):
    groups = len(rows)
    total, units = sums[0].shape
    half, width = rows[0].shape[1], down.shape[1]
    chunk = min(1024, half)
    blocks = total // CAP
    return pl.pallas_call(
        functools.partial(second_kernel, homes, experts, groups, chunk),
        in_specs=[VMEM] * (groups + 5),
        out_specs=[VMEM] * 3 + [HBM],
        out_shape=[bf16(total, units)] * 3 + [pltpu.HBM((blocks, CAP, width), jnp.bfloat16)],
        scratch_shapes=[
            pltpu.VMEM((blocks, CAP, width), jnp.bfloat16),
            pltpu.SemaphoreType.DMA((width // chunk,)),
        ],
        compiler_params=params(28),
        cost_estimate=cost(7 * total * width * units, 6 * width * units),
        name="second_half",
    )(
        *rows,
        *sums,
        pltpu.with_memory_space_constraint(pair, pltpu.VMEM),
        pltpu.with_memory_space_constraint(down, pltpu.VMEM),
    )


def pair_grad_kernel(groups, chunk, *refs):
    rows, gate_ref, up_ref = refs[: HALVES * groups], refs[HALVES * groups], refs[HALVES * groups + 1]
    out_hbm, buffer, sems = refs[HALVES * groups + 2 :]
    half = rows[0].shape[1]
    copies = []
    for step in range(HALVES * half // chunk):
        at = slice(step * chunk, (step + 1) * chunk)
        there = slice(step * chunk % half, step * chunk % half + chunk)
        which = step * chunk // half
        tok = upper(rows[which * groups : (which + 1) * groups], there)
        for side, ref in enumerate((gate_ref, up_ref)):
            buffer[side, at, :] = dot_tn(tok, ref[...]).astype(jnp.bfloat16)
        where = pl.ds(step * chunk, chunk)
        one = pltpu.make_async_copy(
            buffer.at[:, where, :], out_hbm.at[0, :, where, :], sems.at[step]
        )
        one.start()
        copies.append(one)
    for one in copies:
        one.wait()


def pair_grad(rows, gate_grad, up_grad):
    groups = len(rows) // HALVES
    width = HALVES * rows[0].shape[1]
    total, units = gate_grad.shape
    chunk = min(512, width // HALVES)
    return pl.pallas_call(
        functools.partial(pair_grad_kernel, groups, chunk),
        in_specs=[VMEM] * (len(rows) + 2),
        out_specs=HBM,
        out_shape=bf16(1, 2, width, units),
        scratch_shapes=[
            pltpu.VMEM((2, width, units), jnp.bfloat16),
            pltpu.SemaphoreType.DMA((width // chunk,)),
        ],
        compiler_params=params(32),
        cost_estimate=cost(4 * total * width * units, 4 * width * units),
        name="pair_grad",
    )(*rows, gate_grad, up_grad)


def down_grad_kernel(groups, chunk, *refs):
    rows, hidden_ref = refs[: HALVES * groups], refs[HALVES * groups]
    out_hbm, buffer, sems = refs[HALVES * groups + 1 :]
    half = rows[0].shape[1]
    copies = []
    for step in range(HALVES * half // chunk):
        at = slice(step * chunk, (step + 1) * chunk)
        there = slice(step * chunk % half, step * chunk % half + chunk)
        which = step * chunk // half
        cot = lower(rows[which * groups : (which + 1) * groups], there)
        buffer[:, at] = dot_tn(hidden_ref[...], cot).astype(jnp.bfloat16)
        where = pl.ds(step * chunk, chunk)
        one = pltpu.make_async_copy(buffer.at[:, where], out_hbm.at[0, :, where], sems.at[step])
        one.start()
        copies.append(one)
    for one in copies:
        one.wait()


def down_grad(rows, hidden):
    groups = len(rows) // HALVES
    width = HALVES * rows[0].shape[1]
    total, units = hidden.shape
    chunk = min(1024, width // HALVES)
    return pl.pallas_call(
        functools.partial(down_grad_kernel, groups, chunk),
        in_specs=[VMEM] * (len(rows) + 1),
        out_specs=HBM,
        out_shape=bf16(1, units, width),
        scratch_shapes=[
            pltpu.VMEM((units, width), jnp.bfloat16),
            pltpu.SemaphoreType.DMA((width // chunk,)),
        ],
        compiler_params=params(24),
        cost_estimate=cost(2 * total * width * units, 2 * width * units),
        name="down_grad",
    )(*rows, hidden)


def spread_kernel(chunk, rows_ref, place_ref, out_hbm, buffer, sems):
    blocks, _, width = rows_ref.shape
    place = jnp.concatenate([place_ref[...]] * (blocks * CAP // place_ref.shape[0]), axis=0)
    copies = []
    for step in range(width // chunk):
        at = slice(step * chunk, (step + 1) * chunk)
        rows = jnp.concatenate([rows_ref[block, :, at] for block in range(blocks)], axis=0)
        buffer[:, at] = dot_tn(place, rows).astype(jnp.bfloat16)
        where = pl.ds(step * chunk, chunk)
        one = pltpu.make_async_copy(buffer.at[:, where], out_hbm.at[:, where], sems.at[step])
        one.start()
        copies.append(one)
    for one in copies:
        one.wait()


def spread(rows, place):
    width = rows.shape[2]
    slots, tokens = place.shape
    chunk = min(1024, width)
    return pl.pallas_call(
        functools.partial(spread_kernel, chunk),
        in_specs=[VMEM] * 2,
        out_specs=HBM,
        out_shape=bf16(tokens, width),
        scratch_shapes=[
            pltpu.VMEM((tokens, width), jnp.bfloat16),
            pltpu.SemaphoreType.DMA((width // chunk,)),
        ],
        compiler_params=params(16),
        cost_estimate=cost(2 * slots * tokens * width, 2 * tokens * width),
        name="spread_rows",
    )(rows, place)


def per_device(activations, cotangent, expert_ids, gate_probs, gate_up, down_proj):
    experts = lax.axis_size("expert")
    groups = lax.axis_size("dp")
    tokens = activations.shape[0]
    far, near = factors(experts)

    def send(value, by_group, by_expert):
        if by_group == 0 and by_expert == 0:
            return value
        pairs = []
        for group in range(groups):
            to = (group + by_group) % groups
            for i in range(experts):
                pairs.append((group * experts + i, to * experts + (i ^ by_expert)))
        return lax.ppermute(value, ("dp", "expert"), pairs)

    pieces, place = route(
        expert_ids.reshape(1, tokens),
        gate_probs.reshape(1, tokens),
        activations,
        cotangent,
        experts,
    )
    halves = []
    for half in range(HALVES):
        merged = merge([send(pieces[half][high], 0, high * near) for high in range(far)])
        own = stack([send(merged[low], 0, low) for low in range(near)])
        halves.append([send(own, group, 0) for group in range(groups)])
    homes = [
        (group, high * near + low)
        for group in range(groups)
        for low in range(near)
        for high in range(far)
    ]
    *sums, pair, down = first_half(halves[0], gate_up[0], down_proj[0])
    gate_grad, up_grad, hidden, parts = second_half(halves[1], sums, pair, down, homes, experts)
    rows = halves[0] + halves[1]
    returned = lax.all_to_all(parts, ("dp", "expert"), split_axis=0, concat_axis=0, tiled=True)
    down_total = down_grad(rows, hidden)
    pair_total = pair_grad(rows, gate_grad, up_grad)
    input_grad = spread(returned, place)
    return input_grad, pair_total, down_total


def solution(mesh):
    rows = P(("dp", "expert"), None)
    pair, down = P("expert", None, None, "dp"), P("expert", "dp", None)
    return jax.shard_map(
        per_device,
        mesh=mesh,
        in_specs=(rows, rows, rows, rows, pair, down),
        out_specs=(rows, pair, down),
        check_vma=False,
    )
```

time: 67 us -> 68.1 us (1.016)
  starting transfers between devices: 17.5 us -> 23.8 us
  waiting for transfers between devices: 20.7 us -> 17.6 us
  Pallas kernels: 27.8 us -> 25.5 us
    ppermute x10 -> x14, starting transfers between devices: 12.6 us -> 17.1 us  [send(): return lax.ppermute(value, ('dp', 'expert'), pairs)]
    ppermute x10 -> x14, waiting for transfers between devices: 13.5 us -> 10.5 us  [send(): return lax.ppermute(value, ('dp', 'expert'), pairs)]
    pallas_call x4 -> x6, Pallas kernels: 24 us -> 21.8 us  [the longest x1 6.66 us: second_half(): pl.pallas_call(functools.partial(second_kernel, homes, experts, groups, c...]
    all_to_all x1, starting transfers between devices: 4.88 us -> 6.71 us  [per_device(): lax.all_to_all(parts, ('dp', 'expert'), split_axis=0, concat_axis=0, tile...]
  transfers between devices with their start and end apart: 11 -> 15, of which waited for: 6 -> 7; matrix products, arithmetic and copies ran while one was open for 0% -> 0% of each run, Pallas kernels for 23% -> 23%
where the time goes in v3:
time: 68.1 us; the launch traced here: 67.9 us
  Pallas kernels  25.5 us (37%)
  starting transfers between devices  23.8 us (35%)
  waiting for transfers between devices  17.6 us (26%)
  between operations  0.89 us (1%)
    ppermute x14, starting transfers between devices, send(): return lax.ppermute(value, ('dp', 'expert'), pairs)  17.1 us
    ppermute x14, waiting for transfers between devices, send(): return lax.ppermute(value, ('dp', 'expert'), pairs)  10.5 us
    all_to_all x1, waiting for transfers between devices, per_device(): lax.all_to_all(parts, ('dp', 'expert'), split_axis=0, concat_axis=0, tile...  7.15 us
    all_to_all x1, starting transfers between devices, per_device(): lax.all_to_all(parts, ('dp', 'expert'), split_axis=0, concat_axis=0, tile...  6.71 us
    pallas_call x1, Pallas kernels, second_half(): pl.pallas_call(functools.partial(second_kernel, homes, experts, groups, c...  6.66 us
    pallas_call x1, Pallas kernels, first_half(): pl.pallas_call(functools.partial(first_kernel, groups, chunk), in_specs=[...  6.5 us
    pallas_call x1, Pallas kernels, pair_grad(): pl.pallas_call(functools.partial(pair_grad_kernel, groups, chunk), in_spe...  5.25 us
    pallas_call x1, Pallas kernels, down_grad(): pl.pallas_call(functools.partial(down_grad_kernel, groups, chunk), in_spe...  3.32 us
  transfers between devices with their start and end apart: 15, of which 7 were waited for; matrix products, arithmetic and copies ran while one was open for 0% of the time, Pallas kernels for 23%

profile of v3, /device:TPU:0, one launch (start us, length us, event | category | flops | bytes accessed | tf_op | source)
XLA Modules:
  0.0 67.9 jit_solution(12955126966126476095)
XLA Ops:
  0.6 2.0 %route_rows.1 = (bf16[4,4,2048]{2,1,0:T(4,128)(2,1)S(1)}, bf16[4,4,2048]{2,1,0:T(4,128)(2,1)S(1)}, bf16[4,4,2048]{2,1,0:T(4,128)(2,1)S(1)}, bf16[4,4,2048]{2,1,0...) custom-call(s32[1,128]{1,0:T(1,128)} %bitcast.6, ...), custom_call_target="tpu_custom_call" | custom-call | flops 67108864 | bytes 2097152 | tf_op jit(solution)/shard_map/route_rows/pallas_call | solution.py:115
  2.7 3.1 %collective-permute-start.7 = (bf16[4,4,2048]{2,1,0:T(4,128)(2,1)S(1)}, bf16[4,4,2048]{2,1,0:T(4,128)(2,1)S(1)}, u32[]{:S(2)}, u32[]{:S(2)}) collective-permute-start(bf16[4,4,2048]{2,1,0:T(4,128)(2,1)S(1)} %get-tuple-element.38), channel_id=1, source_target_pairs={{0,4},{1,5},{2,6},{3,7},{4,0},{5,1},{6,2},{7,3},{8,12},{9,13},{10,... | collective-permute-start | bytes 196616 | tf_op jit(solution)/shard_map/ppermute | solution.py:437
  5.8 2.6 %collective-permute-start.8 = (bf16[4,4,2048]{2,1,0:T(4,128)(2,1)S(1)}, bf16[4,4,2048]{2,1,0:T(4,128)(2,1)S(1)}, u32[]{:S(2)}, u32[]{:S(2)}) collective-permute-start(bf16[4,4,2048]{2,1,0:T(4,128)(2,1)S(1)} %get-tuple-element.39), channel_id=1, source_target_pairs={{0,8},{1,9},{2,10},{3,11},{4,12},{5,13},{6,14},{7,15},{8,0},{9,1},... | collective-permute-start | bytes 196616 | tf_op jit(solution)/shard_map/ppermute | solution.py:437
  8.3 0.9 %collective-permute-start = (bf16[4,4,2048]{2,1,0:T(4,128)(2,1)S(1)}, bf16[4,4,2048]{2,1,0:T(4,128)(2,1)S(1)}, u32[]{:S(2)}, u32[]{:S(2)}) collective-permute-start(bf16[4,4,2048]{2,1,0:T(4,128)(2,1)S(1)} %get-tuple-element.30), channel_id=1, source_target_pairs={{0,4},{1,5},{2,6},{3,7},{4,0},{5,1},{6,2},{7,3},{8,12},{9,13},{10,... | collective-permute-start | bytes 196616 | tf_op jit(solution)/shard_map/ppermute | solution.py:437
  9.3 3.5 %collective-permute-start.1 = (bf16[4,4,2048]{2,1,0:T(4,128)(2,1)S(1)}, bf16[4,4,2048]{2,1,0:T(4,128)(2,1)S(1)}, u32[]{:S(2)}, u32[]{:S(2)}) collective-permute-start(bf16[4,4,2048]{2,1,0:T(4,128)(2,1)S(1)} %get-tuple-element.31), channel_id=1, source_target_pairs={{0,8},{1,9},{2,10},{3,11},{4,12},{5,13},{6,14},{7,15},{8,0},{9,1},... | collective-permute-start | bytes 196616 | tf_op jit(solution)/shard_map/ppermute | solution.py:437
  12.7 0.4 collective-permute-done.8.refs_2_
  13.1 1.8 %collective-permute-done.9.refs_3_ = bf16[4,4,2048]{2,1,0:T(4,128)(2,1)S(1)} collective-permute-done((bf16[4,4,2048]{2,1,0:T(4,128)(2,1)S(1)}, bf16[4,4,2048]{2,1,0:T(4,128)(2,1)S(1)}, u32[]{:S(2)}, u32[]{:S(2)}) %collective-permute-start.9) | collective-permute-done | bytes 65568 | tf_op jit(solution)/shard_map/ppermute | solution.py:437
  15.2 1.5 %collective-permute-start.11 = (bf16[16,2048]{1,0:T(8,128)(2,1)S(1)}, bf16[16,2048]{1,0:T(8,128)(2,1)S(1)}, u32[]{:S(2)}, u32[]{:S(2)}) collective-permute-start(bf16[16,2048]{1,0:T(8,128)(2,1)S(1)} %get-tuple-element.43), channel_id=1, source_target_pairs={{0,2},{1,3},{2,0},{3,1},{4,6},{5,7},{6,4},{7,5},{8,10},{9,11},{10,... | collective-permute-start | bytes 196616 | tf_op jit(solution)/shard_map/ppermute | solution.py:437
  16.7 0.3 collective-permute-start.12
  17.1 2.3 %collective-permute-done.1.refs_2_ = bf16[4,4,2048]{2,1,0:T(4,128)(2,1)S(1)} collective-permute-done((bf16[4,4,2048]{2,1,0:T(4,128)(2,1)S(1)}, bf16[4,4,2048]{2,1,0:T(4,128)(2,1)S(1)}, u32[]{:S(2)}, u32[]{:S(2)}) %collective-permute-start.1) | collective-permute-done | bytes 65568 | tf_op jit(solution)/shard_map/ppermute | solution.py:437
  19.6 1.6 %collective-permute-start.4 = (bf16[16,2048]{1,0:T(8,128)(2,1)S(1)}, bf16[16,2048]{1,0:T(8,128)(2,1)S(1)}, u32[]{:S(2)}, u32[]{:S(2)}) collective-permute-start(bf16[16,2048]{1,0:T(8,128)(2,1)S(1)} %get-tuple-element.35), channel_id=1, source_target_pairs={{0,2},{1,3},{2,0},{3,1},{4,6},{5,7},{6,4},{7,5},{8,10},{9,11},{10,... | collective-permute-start | bytes 196616 | tf_op jit(solution)/shard_map/ppermute | solution.py:437
  21.2 0.3 collective-permute-start.5
  21.5 1.6 %collective-permute-start.13 = (bf16[64,2048]{1,0:T(8,128)(2,1)S(1)}, bf16[64,2048]{1,0:T(8,128)(2,1)S(1)}, u32[]{:S(2)}, u32[]{:S(2)}) collective-permute-start(bf16[64,2048]{1,0:T(8,128)(2,1)S(1)} %stack_rows.3.refs_0_), channel_id=1, source_target_pairs={{0,16},{1,17},{2,18},{3,19},{4,20},{5,21},{6,22},{7,23},{8,24},{9,... | collective-permute-start | bytes 786440 | tf_op jit(solution)/shard_map/ppermute | solution.py:437
  23.1 1.0 %collective-permute-done.4.refs_2_ = bf16[16,2048]{1,0:T(8,128)(2,1)S(1)} collective-permute-done((bf16[16,2048]{1,0:T(8,128)(2,1)S(1)}, bf16[16,2048]{1,0:T(8,128)(2,1)S(1)}, u32[]{:S(2)}, u32[]{:S(2)}) %collective-permute-start.4) | collective-permute-done | bytes 65568 | tf_op jit(solution)/shard_map/ppermute | solution.py:437
  24.1 1.1 %collective-permute-done.5.refs_3_ = bf16[16,2048]{1,0:T(8,128)(2,1)S(1)} collective-permute-done((bf16[16,2048]{1,0:T(8,128)(2,1)S(1)}, bf16[16,2048]{1,0:T(8,128)(2,1)S(1)}, u32[]{:S(2)}, u32[]{:S(2)}) %collective-permute-start.5) | collective-permute-done | bytes 65568 | tf_op jit(solution)/shard_map/ppermute | solution.py:437
  25.2 1.6 %collective-permute-start.6 = (bf16[64,2048]{1,0:T(8,128)(2,1)S(1)}, bf16[64,2048]{1,0:T(8,128)(2,1)S(1)}, u32[]{:S(2)}, u32[]{:S(2)}) collective-permute-start(bf16[64,2048]{1,0:T(8,128)(2,1)S(1)} %stack_rows.2.refs_0_.refs_2_), channel_id=1, source_target_pairs={{0,16},{1,17},{2,18},{3,19},{4,20},{5,21},{6,22},{7,23},{8,24},{9,... | collective-permute-start | bytes 786440 | tf_op jit(solution)/shard_map/ppermute | solution.py:437
  26.8 3.9 %collective-permute-done.13.refs_1_ = bf16[64,2048]{1,0:T(8,128)(2,1)S(1)} collective-permute-done((bf16[64,2048]{1,0:T(8,128)(2,1)S(1)}, bf16[64,2048]{1,0:T(8,128)(2,1)S(1)}, u32[]{:S(2)}, u32[]{:S(2)}) %collective-permute-start.13) | collective-permute-done | bytes 262176 | tf_op jit(solution)/shard_map/ppermute | solution.py:437
  30.7 6.5 %first_half.1 = (f32[64,768]{1,0:T(8,128)S(1)}, f32[64,768]{1,0:T(8,128)S(1)}, f32[64,768]{1,0:T(8,128)S(1)}, bf16[2,4096,768]{2,1,0:T(8,128)(2,1)S(1)}, bf16[768,4096]{1,0:T(8,128)(2,1)S(1)}) custom-call(bf16[64,2048]{1,0:T(8,128)(2,1)S(1)} %stack_rows.3.refs_0_, bf16[64,2048]{1,0:T(8,128)(2,1)S(1)} %collective-permute-done.13.refs_1_, ...), custom_call_target="tpu_custom_call" | custom-call | flops 603979776 | bytes 18874368 | tf_op jit(solution)/shard_map/first_half/pallas_call | solution.py:225
  37.2 6.7 %second_half.1 = (bf16[64,768]{1,0:T(8,128)(2,1)S(1)}, bf16[64,768]{1,0:T(8,128)(2,1)S(1)}, bf16[64,768]{1,0:T(8,128)(2,1)S(1)}, bf16[32,2,4096]{2,1,0:T(2,128)(2,1)}) custom-call(bf16[64,2048]{1,0:T(8,128)(2,1)S(1)} %stack_rows.2.refs_0_.refs_2_, bf16[64,2048]{1,0:T(8,128)(2,1)S(1)} %collective-permute-done.6.refs_1_.refs_3_, ...), custom_call_target="tpu_custom_call" | custom-call | flops 1409286144 | bytes 18874368 | tf_op jit(solution)/shard_map/second_half/pallas_call | solution.py:287
  43.9 6.7 %all-to-all-start = ((bf16[32,2,4096]{2,1,0:T(2,128)(2,1)}), bf16[32,2,4096]{2,1,0:T(2,128)(2,1)S(1)}, u32[]{:S(2)}, u32[]{:S(2)}) async-start(bf16[32,2,4096]{2,1,0:T(2,128)(2,1)} %get-tuple-element.50), calls=%async_computation | async-start | bytes 1048576 | tf_op jit(solution)/shard_map/all_to_all | solution.py:460
  50.6 3.3 %down_grad.1 = bf16[1,768,4096]{2,1,0:T(8,128)(2,1)} custom-call(bf16[64,2048]{1,0:T(8,128)(2,1)S(1)} %stack_rows.3.refs_0_, bf16[64,2048]{1,0:T(8,128)(2,1)S(1)} %collective-permute-done.13.refs_1_, bf16[64,2048]{1,0:T(8,128)(2,1)S(1)} %stack_rows.2.refs_0_.refs_2_, bf16[64,2048]{1,0:T(8,128)(2,1)S(1)} %collective-permute-done.6.refs_1_.refs_3_, ...), custom_call_target="tpu_custom_call" | custom-call | flops 402653184 | bytes 6291456 | tf_op jit(solution)/shard_map/down_grad/pallas_call | solution.py:373
  53.9 5.2 %pair_grad.1 = bf16[1,2,4096,768]{3,2,1,0:T(8,128)(2,1)} custom-call(bf16[64,2048]{1,0:T(8,128)(2,1)S(1)} %stack_rows.3.refs_0_, bf16[64,2048]{1,0:T(8,128)(2,1)S(1)} %collective-permute-done.13.refs_1_, bf16[64,2048]{1,0:T(8,128)(2,1)S(1)} %stack_rows.2.refs_0_.refs_2_, bf16[64,2048]{1,0:T(8,128)(2,1)S(1)} %collective-permute-done.6.refs_1_.refs_3_, ...), custom_call_target="tpu_custom_call" | custom-call | flops 805306368 | bytes 12582912 | tf_op jit(solution)/shard_map/pair_grad/pallas_call | solution.py:334
  59.2 7.1 %all-to-all-done.rows_ref = bf16[32,2,4096]{2,1,0:T(2,128)(2,1)S(1)} async-done(((bf16[32,2,4096]{2,1,0:T(2,128)(2,1)}), bf16[32,2,4096]{2,1,0:T(2,128)(2,1)S(1)}, u32[]{:S(2)}, u32[]{:S(2)}) %all-to-all-start) | async-done | bytes 524320 | tf_op jit(solution)/shard_map/all_to_all | solution.py:460
  66.3 1.4 %spread_rows.1 = bf16[128,4096]{1,0:T(8,128)(2,1)} custom-call(bf16[32,2,4096]{2,1,0:T(2,128)(2,1)S(1)} %all-to-all-done.rows_ref, bf16[32,128]{1,0:T(8,128)(2,1)S(1)} %get-tuple-element.51.place_ref), custom_call_target="tpu_custom_call" | custom-call | flops 33554432 | bytes 1048576 | tf_op jit(solution)/shard_map/spread_rows/pallas_call | solution.py:408
  (16 shorter events, 0.6 us)
Async XLA Ops:
  2.7 10.1 %collective-permute-start.7 = (bf16[4,4,2048]{2,1,0:T(4,128)(2,1)S(1)}, bf16[4,4,2048]{2,1,0:T(4,128)(2,1)S(1)}, u32[]{:S(2)}, u32[]{:S(2)}) collective-permute-start(bf16[4,4,2048]{2,1,0:T(4,128)(2,1)S(1)} %get-tuple-element.38), channel_id=1, source_target_pairs={{0,4},{1,5},{2,6},{3,7},{4,0},{5,1},{6,2},{7,3},{8,12},{9,13},{10,... | collective-permute-start | bytes 196616 | tf_op jit(solution)/shard_map/ppermute | solution.py:437
  5.8 7.3 %collective-permute-start.8 = (bf16[4,4,2048]{2,1,0:T(4,128)(2,1)S(1)}, bf16[4,4,2048]{2,1,0:T(4,128)(2,1)S(1)}, u32[]{:S(2)}, u32[]{:S(2)}) collective-permute-start(bf16[4,4,2048]{2,1,0:T(4,128)(2,1)S(1)} %get-tuple-element.39), channel_id=1, source_target_pairs={{0,8},{1,9},{2,10},{3,11},{4,12},{5,13},{6,14},{7,15},{8,0},{9,1},... | collective-permute-start | bytes 196616 | tf_op jit(solution)/shard_map/ppermute | solution.py:437
  8.3 6.6 %collective-permute-start.9 = (bf16[4,4,2048]{2,1,0:T(4,128)(2,1)S(1)}, bf16[4,4,2048]{2,1,0:T(4,128)(2,1)S(1)}, u32[]{:S(2)}, u32[]{:S(2)}) collective-permute-start(bf16[4,4,2048]{2,1,0:T(4,128)(2,1)S(1)} %get-tuple-element.40), channel_id=1, source_target_pairs={{0,12},{1,13},{2,14},{3,15},{4,8},{5,9},{6,10},{7,11},{8,4},{9,5},... | collective-permute-start | bytes 196616 | tf_op jit(solution)/shard_map/ppermute | solution.py:437
  8.3 8.4 %collective-permute-start = (bf16[4,4,2048]{2,1,0:T(4,128)(2,1)S(1)}, bf16[4,4,2048]{2,1,0:T(4,128)(2,1)S(1)}, u32[]{:S(2)}, u32[]{:S(2)}) collective-permute-start(bf16[4,4,2048]{2,1,0:T(4,128)(2,1)S(1)} %get-tuple-element.30), channel_id=1, source_target_pairs={{0,4},{1,5},{2,6},{3,7},{4,0},{5,1},{6,2},{7,3},{8,12},{9,13},{10,... | collective-permute-start | bytes 196616 | tf_op jit(solution)/shard_map/ppermute | solution.py:437
  9.3 10.1 %collective-permute-start.1 = (bf16[4,4,2048]{2,1,0:T(4,128)(2,1)S(1)}, bf16[4,4,2048]{2,1,0:T(4,128)(2,1)S(1)}, u32[]{:S(2)}, u32[]{:S(2)}) collective-permute-start(bf16[4,4,2048]{2,1,0:T(4,128)(2,1)S(1)} %get-tuple-element.31), channel_id=1, source_target_pairs={{0,8},{1,9},{2,10},{3,11},{4,12},{5,13},{6,14},{7,15},{8,0},{9,1},... | collective-permute-start | bytes 196616 | tf_op jit(solution)/shard_map/ppermute | solution.py:437
  12.7 6.6 %collective-permute-start.2 = (bf16[4,4,2048]{2,1,0:T(4,128)(2,1)S(1)}, bf16[4,4,2048]{2,1,0:T(4,128)(2,1)S(1)}, u32[]{:S(2)}, u32[]{:S(2)}) collective-permute-start(bf16[4,4,2048]{2,1,0:T(4,128)(2,1)S(1)} %get-tuple-element.32), channel_id=1, source_target_pairs={{0,12},{1,13},{2,14},{3,15},{4,8},{5,9},{6,10},{7,11},{8,4},{9,5},... | collective-permute-start | bytes 196616 | tf_op jit(solution)/shard_map/ppermute | solution.py:437
  15.1 6.1 %collective-permute-start.10 = (bf16[16,2048]{1,0:T(8,128)(2,1)S(1)}, bf16[16,2048]{1,0:T(8,128)(2,1)S(1)}, u32[]{:S(2)}, u32[]{:S(2)}) collective-permute-start(bf16[16,2048]{1,0:T(8,128)(2,1)S(1)} %get-tuple-element.42), channel_id=1, source_target_pairs={{0,1},{1,0},{2,3},{3,2},{4,5},{5,4},{6,7},{7,6},{8,9},{9,8},{10,11... | collective-permute-start | bytes 196616 | tf_op jit(solution)/shard_map/ppermute | solution.py:437
  15.2 6.3 %collective-permute-start.11 = (bf16[16,2048]{1,0:T(8,128)(2,1)S(1)}, bf16[16,2048]{1,0:T(8,128)(2,1)S(1)}, u32[]{:S(2)}, u32[]{:S(2)}) collective-permute-start(bf16[16,2048]{1,0:T(8,128)(2,1)S(1)} %get-tuple-element.43), channel_id=1, source_target_pairs={{0,2},{1,3},{2,0},{3,1},{4,6},{5,7},{6,4},{7,5},{8,10},{9,11},{10,... | collective-permute-start | bytes 196616 | tf_op jit(solution)/shard_map/ppermute | solution.py:437
  16.7 4.7 %collective-permute-start.12 = (bf16[16,2048]{1,0:T(8,128)(2,1)S(1)}, bf16[16,2048]{1,0:T(8,128)(2,1)S(1)}, u32[]{:S(2)}, u32[]{:S(2)}) collective-permute-start(bf16[16,2048]{1,0:T(8,128)(2,1)S(1)} %get-tuple-element.44), channel_id=1, source_target_pairs={{0,3},{1,2},{2,1},{3,0},{4,7},{5,6},{6,5},{7,4},{8,11},{9,10},{10,... | collective-permute-start | bytes 196616 | tf_op jit(solution)/shard_map/ppermute | solution.py:437
  19.5 3.6 %collective-permute-start.3 = (bf16[16,2048]{1,0:T(8,128)(2,1)S(1)}, bf16[16,2048]{1,0:T(8,128)(2,1)S(1)}, u32[]{:S(2)}, u32[]{:S(2)}) collective-permute-start(bf16[16,2048]{1,0:T(8,128)(2,1)S(1)} %get-tuple-element.34), channel_id=1, source_target_pairs={{0,1},{1,0},{2,3},{3,2},{4,5},{5,4},{6,7},{7,6},{8,9},{9,8},{10,11... | collective-permute-start | bytes 196616 | tf_op jit(solution)/shard_map/ppermute | solution.py:437
  19.6 4.5 %collective-permute-start.4 = (bf16[16,2048]{1,0:T(8,128)(2,1)S(1)}, bf16[16,2048]{1,0:T(8,128)(2,1)S(1)}, u32[]{:S(2)}, u32[]{:S(2)}) collective-permute-start(bf16[16,2048]{1,0:T(8,128)(2,1)S(1)} %get-tuple-element.35), channel_id=1, source_target_pairs={{0,2},{1,3},{2,0},{3,1},{4,6},{5,7},{6,4},{7,5},{8,10},{9,11},{10,... | collective-permute-start | bytes 196616 | tf_op jit(solution)/shard_map/ppermute | solution.py:437
  21.2 4.0 %collective-permute-start.5 = (bf16[16,2048]{1,0:T(8,128)(2,1)S(1)}, bf16[16,2048]{1,0:T(8,128)(2,1)S(1)}, u32[]{:S(2)}, u32[]{:S(2)}) collective-permute-start(bf16[16,2048]{1,0:T(8,128)(2,1)S(1)} %get-tuple-element.36), channel_id=1, source_target_pairs={{0,3},{1,2},{2,1},{3,0},{4,7},{5,6},{6,5},{7,4},{8,11},{9,10},{10,... | collective-permute-start | bytes 196616 | tf_op jit(solution)/shard_map/ppermute | solution.py:437
  21.5 9.2 %collective-permute-start.13 = (bf16[64,2048]{1,0:T(8,128)(2,1)S(1)}, bf16[64,2048]{1,0:T(8,128)(2,1)S(1)}, u32[]{:S(2)}, u32[]{:S(2)}) collective-permute-start(bf16[64,2048]{1,0:T(8,128)(2,1)S(1)} %stack_rows.3.refs_0_), channel_id=1, source_target_pairs={{0,16},{1,17},{2,18},{3,19},{4,20},{5,21},{6,22},{7,23},{8,24},{9,... | collective-permute-start | bytes 786440 | tf_op jit(solution)/shard_map/ppermute | solution.py:437
  25.2 12.0 %collective-permute-start.6 = (bf16[64,2048]{1,0:T(8,128)(2,1)S(1)}, bf16[64,2048]{1,0:T(8,128)(2,1)S(1)}, u32[]{:S(2)}, u32[]{:S(2)}) collective-permute-start(bf16[64,2048]{1,0:T(8,128)(2,1)S(1)} %stack_rows.2.refs_0_.refs_2_), channel_id=1, source_target_pairs={{0,16},{1,17},{2,18},{3,19},{4,20},{5,21},{6,22},{7,23},{8,24},{9,... | collective-permute-start | bytes 786440 | tf_op jit(solution)/shard_map/ppermute | solution.py:437
  43.9 22.4 %all-to-all-start = ((bf16[32,2,4096]{2,1,0:T(2,128)(2,1)}), bf16[32,2,4096]{2,1,0:T(2,128)(2,1)S(1)}, u32[]{:S(2)}, u32[]{:S(2)}) async-start(bf16[32,2,4096]{2,1,0:T(2,128)(2,1)} %get-tuple-element.50), calls=%async_computation | async-start | bytes 1048576 | tf_op jit(solution)/shard_map/all_to_all | solution.py:460

commit v4 on v0

--- a/solution.py
+++ b/solution.py
@@ -128,25 +128,25 @@
 
 
 def merge_kernel(far, *refs):
-    pieces, outs = refs[:far], refs[far + 1 :]
+    pieces, outs = refs[:far], refs[len(refs) - refs[0].shape[0] :]
     for index, out in enumerate(outs):
         rows = [piece[index, :CAP, :] for piece in pieces]
         rows += [piece[index, CAP:, :] for piece in pieces]
         out[...] = jnp.concatenate(rows, axis=0)
 
 
-def merge(pieces, after):
+def merge(pieces, after=()):
     far = len(pieces)
     near, _, width = pieces[0].shape
     return pl.pallas_call(
         functools.partial(merge_kernel, far),
-        in_specs=[VMEM] * far + [pl.BlockSpec(memory_space=pl.ANY)],
+        in_specs=[VMEM] * far + [pl.BlockSpec(memory_space=pl.ANY)] * len(after),
         out_specs=[VMEM] * near,
         out_shape=[bf16(2 * CAP * far, width)] * near,
         compiler_params=params(16),
         cost_estimate=cost(0, 8 * near * CAP * far * width),
         name="merge_rows",
-    )(*pieces, after)
+    )(*pieces, *after)
 
 
 def load_kernel(chunk, pair_hbm, down_hbm, after, pair, down, sems):
@@ -180,13 +180,11 @@
     )(in_hbm(pair), in_hbm(down), after)
 
 
-def expert_kernel(experts, groups, chunk, *refs):
-    far, near = factors(experts)
-    count = groups * near
+def expert_kernel(homes, experts, groups, chunk, count, *refs):
     got, pair, down = refs[:count], refs[count], refs[count + 1]
     gate_out, up_out, hidden_out, tok_all, cot_all, parts_hbm = refs[count + 2 : count + 8]
     parts, acc_gate, acc_up, acc_hid, sems = refs[count + 8 :]
-    half = far * CAP
+    half = got[0].shape[0] // 2
     width = got[0].shape[1]
     steps = width // chunk
     for step in range(steps):
@@ -215,17 +213,16 @@
     gate_out[...] = gate_grad
     up_out[...] = up_grad
     me, group = lax.axis_index("expert"), lax.axis_index("dp")
-    homes = []
-    for index in range(count):
-        source = lax.rem(group - index // near + groups, groups) * experts
-        homes += [source + (me ^ (high * near + index % near)) for high in range(far)]
+    rows = [
+        lax.rem(group - back + groups, groups) * experts + (me ^ turn) for back, turn in homes
+    ]
     copies = []
     for step in range(steps):
         at = slice(step * chunk, (step + 1) * chunk)
         value = dot_nt(gate_grad, pair[0, at, :]) + dot_nt(up_grad, pair[1, at, :])
         value = value.astype(jnp.bfloat16)
-        for block, home in enumerate(homes):
-            parts[home, :, at] = value[block * CAP : (block + 1) * CAP]
+        for block, row in enumerate(rows):
+            parts[row, :, at] = value[block * CAP : (block + 1) * CAP]
         where = pl.ds(step * chunk, chunk)
         one = pltpu.make_async_copy(
             parts.at[:, :, where], parts_hbm.at[:, :, where], sems.at[step]
@@ -236,14 +233,14 @@
         one.wait()
 
 
-def expert_rows(got, pair, down, experts, groups):
+def expert_rows(got, homes, pair, down, experts, groups):
     width = got[0].shape[1]
     units = down.shape[0]
     chunk = min(1024, width)
     blocks = groups * experts
     total = blocks * CAP
     return pl.pallas_call(
-        functools.partial(expert_kernel, experts, groups, chunk),
+        functools.partial(expert_kernel, homes, experts, groups, chunk, len(got)),
         in_specs=[VMEM] * (len(got) + 2),
         out_specs=[VMEM] * 5 + [HBM],
         out_shape=[bf16(total, units)] * 3
@@ -402,10 +399,24 @@
         experts,
     )
     pair, down = load(gate_up[0], down_proj[0], place)
-    arrived = [send(pieces[high], 0, high * near) for high in reversed(range(far))]
-    merged = merge(arrived[::-1], pltpu.with_memory_space_constraint(down, pltpu.VMEM))
-    got = [send(merged[low], group, low) for group in range(groups) for low in range(near)]
-    gate_grad, up_grad, hidden, tok, cot, parts = expert_rows(got, pair, down, experts, groups)
+    arrived = [send(pieces[high], 0, high * near) for high in range(far)]
+    early, late = range(far // 2), range(far // 2, far)
+    first = [send(pieces[high], group, high * near) for group in range(1, groups) for high in early]
+    second = [send(arrived[high], group, 0) for group in range(1, groups) for high in late]
+    loaded = pltpu.with_memory_space_constraint(down, pltpu.VMEM)
+    first = merge([arrived[high] for high in early] + first, (loaded,))
+    second = merge([arrived[high] for high in late] + second, (first[0],))
+    got = [send(rows[low], 0, low) for rows in (first, second) for low in range(near)]
+    homes = [
+        (group, high * near + low)
+        for part in (early, late)
+        for low in range(near)
+        for group in range(groups)
+        for high in part
+    ]
+    gate_grad, up_grad, hidden, tok, cot, parts = expert_rows(
+        got, homes, pair, down, experts, groups
+    )
     returned = lax.all_to_all(parts, ("dp", "expert"), split_axis=0, concat_axis=0, tiled=True)
     down_total = down_grad([cot], hidden)
     pair_total = pair_grad([tok], gate_grad, up_grad)

time: 67 us -> 67.6 us (level)
  starting transfers between devices: 17.5 us -> 20.6 us
  waiting for transfers between devices: 20.7 us -> 17.7 us
    ppermute x10 -> x13, waiting for transfers between devices: 13.5 us -> 10.6 us  [send(): return lax.ppermute(value, ('dp', 'expert'), pairs)]
    ppermute x10 -> x13, starting transfers between devices: 12.6 us -> 14.9 us  [send(): return lax.ppermute(value, ('dp', 'expert'), pairs)]
    all_to_all x1, starting transfers between devices: 4.88 us -> 5.7 us  [per_device(): lax.all_to_all(parts, ('dp', 'expert'), split_axis=0, concat_axis=0, tile...]
  transfers between devices with their start and end apart: 11 -> 14, of which waited for: 6 -> 8; matrix products, arithmetic and copies ran while one was open for 0% -> 0% of each run, Pallas kernels for 23% -> 24%
where the time goes in v4:
time: 67.6 us; the launch traced here: 67.3 us
  Pallas kernels  28.1 us (42%)
  starting transfers between devices  20.6 us (30%)
  waiting for transfers between devices  17.7 us (26%)
  between operations  0.88 us (1%)
    ppermute x13, starting transfers between devices, send(): return lax.ppermute(value, ('dp', 'expert'), pairs)  14.9 us
    ppermute x13, waiting for transfers between devices, send(): return lax.ppermute(value, ('dp', 'expert'), pairs)  10.6 us
    pallas_call x1, Pallas kernels, expert_rows(): pl.pallas_call(functools.partial(expert_kernel, homes, experts, groups, c...  8.89 us
    all_to_all x1, waiting for transfers between devices, per_device(): lax.all_to_all(parts, ('dp', 'expert'), split_axis=0, concat_axis=0, tile...  7.14 us
    pallas_call x1, Pallas kernels, load(): pl.pallas_call(functools.partial(load_kernel, chunk), in_specs=[HBM] * 2...  6.5 us
    all_to_all x1, starting transfers between devices, per_device(): lax.all_to_all(parts, ('dp', 'expert'), split_axis=0, concat_axis=0, tile...  5.7 us
    pallas_call x1, Pallas kernels, pair_grad(): pl.pallas_call(functools.partial(pair_grad_kernel, blocks, chunk), in_spe...  5.25 us
    pallas_call x1, Pallas kernels, down_grad(): pl.pallas_call(functools.partial(down_grad_kernel, blocks, chunk), in_spe...  3.33 us
  transfers between devices with their start and end apart: 14, of which 8 were waited for; matrix products, arithmetic and copies ran while one was open for 0% of the time, Pallas kernels for 24%

profile of v4, /device:TPU:0, one launch (start us, length us, event | category | flops | bytes accessed | tf_op | source)
XLA Modules:
  0.0 67.3 jit_solution(5003497291308385769)
XLA Ops:
  0.6 2.0 %route_rows.1 = (bf16[4,4,4096]{2,1,0:T(4,128)(2,1)S(1)}, bf16[4,4,4096]{2,1,0:T(4,128)(2,1)S(1)}, bf16[4,4,4096]{2,1,0:T(4,128)(2,1)S(1)}, bf16[4,4,4096]{2,1,0:T(4,128)(2,1)S(1)}, bf16[32,128]{1,0:T(8,128)(2,1)S(1)}) custom-call(s32[1,128]{1,0:T(1,128)} %bitcast.6, f32[1,128]{1,0:T(1,128)} %bitcast.7, bf16[128,4096]{1,0:T(8,128)(2,1)} %act_hbm.1, ...), custom_call_target="tpu_custom_call" | custom-call | flops 67108864 | bytes 2097152 | tf_op jit(solution)/shard_map/route_rows/pallas_call | solution.py:111
  2.7 4.1 %collective-permute-start.6 = (bf16[4,4,4096]{2,1,0:T(4,128)(2,1)S(1)}, bf16[4,4,4096]{2,1,0:T(4,128)(2,1)S(1)}, u32[]{:S(2)}, u32[]{:S(2)}) collective-permute-start(bf16[4,4,4096]{2,1,0:T(4,128)(2,1)S(1)} %get-tuple-element.32), channel_id=1, source_target_pairs={{0,8},{1,9},{2,10},{3,11},{4,12},{5,13},{6,14},{7,15},{8,0},{9,1},... | collective-permute-start | bytes 393224 | tf_op jit(solution)/shard_map/ppermute | solution.py:392
  6.8 1.4 %collective-permute-start.7 = (bf16[4,4,4096]{2,1,0:T(4,128)(2,1)S(1)}, bf16[4,4,4096]{2,1,0:T(4,128)(2,1)S(1)}, u32[]{:S(2)}, u32[]{:S(2)}) collective-permute-start(bf16[4,4,4096]{2,1,0:T(4,128)(2,1)S(1)} %get-tuple-element.33), channel_id=1, source_target_pairs={{0,12},{1,13},{2,14},{3,15},{4,8},{5,9},{6,10},{7,11},{8,4},{9,5},... | collective-permute-start | bytes 393224 | tf_op jit(solution)/shard_map/ppermute | solution.py:392
  8.1 1.5 %collective-permute-start.1 = (bf16[4,4,4096]{2,1,0:T(4,128)(2,1)S(1)}, bf16[4,4,4096]{2,1,0:T(4,128)(2,1)S(1)}, u32[]{:S(2)}, u32[]{:S(2)}) collective-permute-start(bf16[4,4,4096]{2,1,0:T(4,128)(2,1)S(1)} %get-tuple-element.24.refs_0_), channel_id=1, source_target_pairs={{0,16},{1,17},{2,18},{3,19},{4,20},{5,21},{6,22},{7,23},{8,24},{9,... | collective-permute-start | bytes 393224 | tf_op jit(solution)/shard_map/ppermute | solution.py:392
  9.8 1.8 %collective-permute-start = (bf16[4,4,4096]{2,1,0:T(4,128)(2,1)S(1)}, bf16[4,4,4096]{2,1,0:T(4,128)(2,1)S(1)}, u32[]{:S(2)}, u32[]{:S(2)}) collective-permute-start(bf16[4,4,4096]{2,1,0:T(4,128)(2,1)S(1)} %get-tuple-element.25), channel_id=1, source_target_pairs={{0,4},{1,5},{2,6},{3,7},{4,0},{5,1},{6,2},{7,3},{8,12},{9,13},{10,... | collective-permute-start | bytes 393224 | tf_op jit(solution)/shard_map/ppermute | solution.py:392
  11.6 6.5 %load_weights.1 = (bf16[2,4096,768]{2,1,0:T(8,128)(2,1)S(1)}, bf16[768,4096]{1,0:T(8,128)(2,1)S(1)}) custom-call(bf16[2,4096,768]{2,1,0:T(8,128)(2,1)} %bitcast.4, bf16[768,4096]{1,0:T(8,128)(2,1)} %bitcast.5, bf16[32,128]{1,0:T(8,128)(2,1)S(1)} %get-tuple-element.26.after.place_ref), custom_call_target="tpu_custom_call" | custom-call | bytes 18874368 | tf_op jit(solution)/shard_map/load_weights/pallas_call | solution.py:171
  18.1 1.6 %collective-permute-start.8 = (bf16[4,4,4096]{2,1,0:T(4,128)(2,1)S(1)}, bf16[4,4,4096]{2,1,0:T(4,128)(2,1)S(1)}, u32[]{:S(2)}, u32[]{:S(2)}) collective-permute-start(bf16[4,4,4096]{2,1,0:T(4,128)(2,1)S(1)} %collective-permute-done.6.refs_0_), channel_id=1, source_target_pairs={{0,16},{1,17},{2,18},{3,19},{4,20},{5,21},{6,22},{7,23},{8,24},{9,... | collective-permute-start | bytes 393224 | tf_op jit(solution)/shard_map/ppermute | solution.py:392
  19.7 0.5 collective-permute-start.9
  20.2 0.8 %collective-permute-done.refs_1_ = bf16[4,4,4096]{2,1,0:T(4,128)(2,1)S(1)} collective-permute-done((bf16[4,4,4096]{2,1,0:T(4,128)(2,1)S(1)}, bf16[4,4,4096]{2,1,0:T(4,128)(2,1)S(1)}, u32[]{:S(2)}, u32[]{:S(2)}) %collective-permute-start) | collective-permute-done | bytes 131104 | tf_op jit(solution)/shard_map/ppermute | solution.py:392
  21.1 0.4 merge_rows.2
  21.5 1.6 %collective-permute-start.4 = (bf16[16,4096]{1,0:T(8,128)(2,1)S(1)}, bf16[16,4096]{1,0:T(8,128)(2,1)S(1)}, u32[]{:S(2)}, u32[]{:S(2)}) collective-permute-start(bf16[16,4096]{1,0:T(8,128)(2,1)S(1)} %get-tuple-element.30), channel_id=1, source_target_pairs={{0,2},{1,3},{2,0},{3,1},{4,6},{5,7},{6,4},{7,5},{8,10},{9,11},{10,... | collective-permute-start | bytes 393224 | tf_op jit(solution)/shard_map/ppermute | solution.py:392
  23.8 1.4 %collective-permute-done.9.refs_3_ = bf16[4,4,4096]{2,1,0:T(4,128)(2,1)S(1)} collective-permute-done((bf16[4,4,4096]{2,1,0:T(4,128)(2,1)S(1)}, bf16[4,4,4096]{2,1,0:T(4,128)(2,1)S(1)}, u32[]{:S(2)}, u32[]{:S(2)}) %collective-permute-start.9) | collective-permute-done | bytes 131104 | tf_op jit(solution)/shard_map/ppermute | solution.py:392
  25.2 0.4 merge_rows.3
  25.6 1.5 %collective-permute-start.11 = (bf16[16,4096]{1,0:T(8,128)(2,1)S(1)}, bf16[16,4096]{1,0:T(8,128)(2,1)S(1)}, u32[]{:S(2)}, u32[]{:S(2)}) collective-permute-start(bf16[16,4096]{1,0:T(8,128)(2,1)S(1)} %get-tuple-element.36), channel_id=1, source_target_pairs={{0,2},{1,3},{2,0},{3,1},{4,6},{5,7},{6,4},{7,5},{8,10},{9,11},{10,... | collective-permute-start | bytes 393224 | tf_op jit(solution)/shard_map/ppermute | solution.py:392
  27.5 0.4 collective-permute-done.4.refs_2_
  27.9 1.9 %collective-permute-done.5.refs_3_ = bf16[16,4096]{1,0:T(8,128)(2,1)S(1)} collective-permute-done((bf16[16,4096]{1,0:T(8,128)(2,1)S(1)}, bf16[16,4096]{1,0:T(8,128)(2,1)S(1)}, u32[]{:S(2)}, u32[]{:S(2)}) %collective-permute-start.5) | collective-permute-done | bytes 131104 | tf_op jit(solution)/shard_map/ppermute | solution.py:392
  29.8 3.7 %collective-permute-done.11.refs_6_ = bf16[16,4096]{1,0:T(8,128)(2,1)S(1)} collective-permute-done((bf16[16,4096]{1,0:T(8,128)(2,1)S(1)}, bf16[16,4096]{1,0:T(8,128)(2,1)S(1)}, u32[]{:S(2)}, u32[]{:S(2)}) %collective-permute-start.11) | collective-permute-done | bytes 131104 | tf_op jit(solution)/shard_map/ppermute | solution.py:392
  33.5 1.9 %collective-permute-done.12.refs_7_ = bf16[16,4096]{1,0:T(8,128)(2,1)S(1)} collective-permute-done((bf16[16,4096]{1,0:T(8,128)(2,1)S(1)}, bf16[16,4096]{1,0:T(8,128)(2,1)S(1)}, u32[]{:S(2)}, u32[]{:S(2)}) %collective-permute-start.12) | collective-permute-done | bytes 131104 | tf_op jit(solution)/shard_map/ppermute | solution.py:392
  35.4 8.9 %expert_rows.1 = (bf16[64,768]{1,0:T(8,128)(2,1)S(1)}, bf16[64,768]{1,0:T(8,128)(2,1)S(1)}, bf16[64,768]{1,0:T(8,128)(2,1)S(1)}, bf16[64,4096]{1,0:T(8,128)(2,1)...) custom-call(bf16[16,4096]{1,0:T(8,128)(2,1)S(1)} %get-tuple-element.28.refs_4_.refs_0_, ...), custom_call_target="tpu_custom_call" | custom-call | flops 2013265920 | bytes 18874368 | tf_op jit(solution)/shard_map/expert_rows/pallas_call | solution.py:242
  44.3 5.7 %all-to-all-start = ((bf16[32,2,4096]{2,1,0:T(2,128)(2,1)}), bf16[32,2,4096]{2,1,0:T(2,128)(2,1)S(1)}, u32[]{:S(2)}, u32[]{:S(2)}) async-start(bf16[32,2,4096]{2,1,0:T(2,128)(2,1)} %get-tuple-element.39), calls=%async_computation | async-start | bytes 1048576 | tf_op jit(solution)/shard_map/all_to_all | solution.py:420
  50.0 3.3 %down_grad.1 = bf16[1,768,4096]{2,1,0:T(8,128)(2,1)} custom-call(bf16[64,4096]{1,0:T(8,128)(2,1)S(1)} %get-tuple-element.43.refs_0_, bf16[64,768]{1,0:T(8,128)(2,1)S(1)} %get-tuple-element.44.refs_1_), custom_call_target="tpu_custom_call" | custom-call | flops 402653184 | bytes 6291456 | tf_op jit(solution)/shard_map/down_grad/pallas_call | solution.py:328
  53.4 5.3 %pair_grad.1 = bf16[1,2,4096,768]{3,2,1,0:T(8,128)(2,1)} custom-call(bf16[64,4096]{1,0:T(8,128)(2,1)S(1)} %get-tuple-element.40.refs_0_, bf16[64,768]{1,0:T(8,128)(2,1)S(1)} %get-tuple-element.41.refs_1_, bf16[64,768]{1,0:T(8,128)(2,1)S(1)} %get-tuple-element.42.refs_2_), custom_call_target="tpu_custom_call" | custom-call | flops 805306368 | bytes 12582912 | tf_op jit(solution)/shard_map/pair_grad/pallas_call | solution.py:291
  58.6 7.1 %all-to-all-done.rows_ref = bf16[32,2,4096]{2,1,0:T(2,128)(2,1)S(1)} async-done(((bf16[32,2,4096]{2,1,0:T(2,128)(2,1)}), bf16[32,2,4096]{2,1,0:T(2,128)(2,1)S(1)}, u32[]{:S(2)}, u32[]{:S(2)}) %all-to-all-start) | async-done | bytes 524320 | tf_op jit(solution)/shard_map/all_to_all | solution.py:420
  65.8 1.4 %spread_rows.1 = bf16[128,4096]{1,0:T(8,128)(2,1)} custom-call(bf16[32,2,4096]{2,1,0:T(2,128)(2,1)S(1)} %all-to-all-done.rows_ref, bf16[32,128]{1,0:T(8,128)(2,1)S(1)} %get-tuple-element.26.after.place_ref), custom_call_target="tpu_custom_call" | custom-call | flops 33554432 | bytes 1048576 | tf_op jit(solution)/shard_map/spread_rows/pallas_call | solution.py:363
  (12 shorter events, 1.3 us)
Async XLA Ops:
  2.7 15.4 %collective-permute-start.6 = (bf16[4,4,4096]{2,1,0:T(4,128)(2,1)S(1)}, bf16[4,4,4096]{2,1,0:T(4,128)(2,1)S(1)}, u32[]{:S(2)}, u32[]{:S(2)}) collective-permute-start(bf16[4,4,4096]{2,1,0:T(4,128)(2,1)S(1)} %get-tuple-element.32), channel_id=1, source_target_pairs={{0,8},{1,9},{2,10},{3,11},{4,12},{5,13},{6,14},{7,15},{8,0},{9,1},... | collective-permute-start | bytes 393224 | tf_op jit(solution)/shard_map/ppermute | solution.py:392
  6.8 13.0 %collective-permute-start.7 = (bf16[4,4,4096]{2,1,0:T(4,128)(2,1)S(1)}, bf16[4,4,4096]{2,1,0:T(4,128)(2,1)S(1)}, u32[]{:S(2)}, u32[]{:S(2)}) collective-permute-start(bf16[4,4,4096]{2,1,0:T(4,128)(2,1)S(1)} %get-tuple-element.33), channel_id=1, source_target_pairs={{0,12},{1,13},{2,14},{3,15},{4,8},{5,9},{6,10},{7,11},{8,4},{9,5},... | collective-permute-start | bytes 393224 | tf_op jit(solution)/shard_map/ppermute | solution.py:392
  8.1 12.1 %collective-permute-start.1 = (bf16[4,4,4096]{2,1,0:T(4,128)(2,1)S(1)}, bf16[4,4,4096]{2,1,0:T(4,128)(2,1)S(1)}, u32[]{:S(2)}, u32[]{:S(2)}) collective-permute-start(bf16[4,4,4096]{2,1,0:T(4,128)(2,1)S(1)} %get-tuple-element.24.refs_0_), channel_id=1, source_target_pairs={{0,16},{1,17},{2,18},{3,19},{4,20},{5,21},{6,22},{7,23},{8,24},{9,... | collective-permute-start | bytes 393224 | tf_op jit(solution)/shard_map/ppermute | solution.py:392
  9.6 10.6 %collective-permute-start.2 = (bf16[4,4,4096]{2,1,0:T(4,128)(2,1)S(1)}, bf16[4,4,4096]{2,1,0:T(4,128)(2,1)S(1)}, u32[]{:S(2)}, u32[]{:S(2)}) collective-permute-start(bf16[4,4,4096]{2,1,0:T(4,128)(2,1)S(1)} %get-tuple-element.25), channel_id=1, source_target_pairs={{0,20},{1,21},{2,22},{3,23},{4,16},{5,17},{6,18},{7,19},{8,28},{9,... | collective-permute-start | bytes 393224 | tf_op jit(solution)/shard_map/ppermute | solution.py:392
  9.8 11.3 %collective-permute-start = (bf16[4,4,4096]{2,1,0:T(4,128)(2,1)S(1)}, bf16[4,4,4096]{2,1,0:T(4,128)(2,1)S(1)}, u32[]{:S(2)}, u32[]{:S(2)}) collective-permute-start(bf16[4,4,4096]{2,1,0:T(4,128)(2,1)S(1)} %get-tuple-element.25), channel_id=1, source_target_pairs={{0,4},{1,5},{2,6},{3,7},{4,0},{5,1},{6,2},{7,3},{8,12},{9,13},{10,... | collective-permute-start | bytes 393224 | tf_op jit(solution)/shard_map/ppermute | solution.py:392
  18.1 5.6 %collective-permute-start.8 = (bf16[4,4,4096]{2,1,0:T(4,128)(2,1)S(1)}, bf16[4,4,4096]{2,1,0:T(4,128)(2,1)S(1)}, u32[]{:S(2)}, u32[]{:S(2)}) collective-permute-start(bf16[4,4,4096]{2,1,0:T(4,128)(2,1)S(1)} %collective-permute-done.6.refs_0_), channel_id=1, source_target_pairs={{0,16},{1,17},{2,18},{3,19},{4,20},{5,21},{6,22},{7,23},{8,24},{9,... | collective-permute-start | bytes 393224 | tf_op jit(solution)/shard_map/ppermute | solution.py:392
  19.7 5.5 %collective-permute-start.9 = (bf16[4,4,4096]{2,1,0:T(4,128)(2,1)S(1)}, bf16[4,4,4096]{2,1,0:T(4,128)(2,1)S(1)}, u32[]{:S(2)}, u32[]{:S(2)}) collective-permute-start(bf16[4,4,4096]{2,1,0:T(4,128)(2,1)S(1)} %collective-permute-done.7.refs_1_), channel_id=1, source_target_pairs={{0,16},{1,17},{2,18},{3,19},{4,20},{5,21},{6,22},{7,23},{8,24},{9,... | collective-permute-start | bytes 393224 | tf_op jit(solution)/shard_map/ppermute | solution.py:392
  21.5 5.7 %collective-permute-start.3 = (bf16[16,4096]{1,0:T(8,128)(2,1)S(1)}, bf16[16,4096]{1,0:T(8,128)(2,1)S(1)}, u32[]{:S(2)}, u32[]{:S(2)}) collective-permute-start(bf16[16,4096]{1,0:T(8,128)(2,1)S(1)} %get-tuple-element.29), channel_id=1, source_target_pairs={{0,1},{1,0},{2,3},{3,2},{4,5},{5,4},{6,7},{7,6},{8,9},{9,8},{10,11... | collective-permute-start | bytes 393224 | tf_op jit(solution)/shard_map/ppermute | solution.py:392
  21.5 6.4 %collective-permute-start.4 = (bf16[16,4096]{1,0:T(8,128)(2,1)S(1)}, bf16[16,4096]{1,0:T(8,128)(2,1)S(1)}, u32[]{:S(2)}, u32[]{:S(2)}) collective-permute-start(bf16[16,4096]{1,0:T(8,128)(2,1)S(1)} %get-tuple-element.30), channel_id=1, source_target_pairs={{0,2},{1,3},{2,0},{3,1},{4,6},{5,7},{6,4},{7,5},{8,10},{9,11},{10,... | collective-permute-start | bytes 393224 | tf_op jit(solution)/shard_map/ppermute | solution.py:392
  23.1 6.7 %collective-permute-start.5 = (bf16[16,4096]{1,0:T(8,128)(2,1)S(1)}, bf16[16,4096]{1,0:T(8,128)(2,1)S(1)}, u32[]{:S(2)}, u32[]{:S(2)}) collective-permute-start(bf16[16,4096]{1,0:T(8,128)(2,1)S(1)} %get-tuple-element.31), channel_id=1, source_target_pairs={{0,3},{1,2},{2,1},{3,0},{4,7},{5,6},{6,5},{7,4},{8,11},{9,10},{10,... | collective-permute-start | bytes 393224 | tf_op jit(solution)/shard_map/ppermute | solution.py:392
  25.6 4.3 %collective-permute-start.10 = (bf16[16,4096]{1,0:T(8,128)(2,1)S(1)}, bf16[16,4096]{1,0:T(8,128)(2,1)S(1)}, u32[]{:S(2)}, u32[]{:S(2)}) collective-permute-start(bf16[16,4096]{1,0:T(8,128)(2,1)S(1)} %get-tuple-element.35), channel_id=1, source_target_pairs={{0,1},{1,0},{2,3},{3,2},{4,5},{5,4},{6,7},{7,6},{8,9},{9,8},{10,11... | collective-permute-start | bytes 393224 | tf_op jit(solution)/shard_map/ppermute | solution.py:392
  25.6 7.9 %collective-permute-start.11 = (bf16[16,4096]{1,0:T(8,128)(2,1)S(1)}, bf16[16,4096]{1,0:T(8,128)(2,1)S(1)}, u32[]{:S(2)}, u32[]{:S(2)}) collective-permute-start(bf16[16,4096]{1,0:T(8,128)(2,1)S(1)} %get-tuple-element.36), channel_id=1, source_target_pairs={{0,2},{1,3},{2,0},{3,1},{4,6},{5,7},{6,4},{7,5},{8,10},{9,11},{10,... | collective-permute-start | bytes 393224 | tf_op jit(solution)/shard_map/ppermute | solution.py:392
  27.2 8.2 %collective-permute-start.12 = (bf16[16,4096]{1,0:T(8,128)(2,1)S(1)}, bf16[16,4096]{1,0:T(8,128)(2,1)S(1)}, u32[]{:S(2)}, u32[]{:S(2)}) collective-permute-start(bf16[16,4096]{1,0:T(8,128)(2,1)S(1)} %get-tuple-element.37), channel_id=1, source_target_pairs={{0,3},{1,2},{2,1},{3,0},{4,7},{5,6},{6,5},{7,4},{8,11},{9,10},{10,... | collective-permute-start | bytes 393224 | tf_op jit(solution)/shard_map/ppermute | solution.py:392
  44.3 21.4 %all-to-all-start = ((bf16[32,2,4096]{2,1,0:T(2,128)(2,1)}), bf16[32,2,4096]{2,1,0:T(2,128)(2,1)S(1)}, u32[]{:S(2)}, u32[]{:S(2)}) async-start(bf16[32,2,4096]{2,1,0:T(2,128)(2,1)} %get-tuple-element.39), calls=%async_computation | async-start | bytes 1048576 | tf_op jit(solution)/shard_map/all_to_all | solution.py:420

commit v5 on v4

--- a/solution.py
+++ b/solution.py
@@ -149,6 +149,28 @@
     )(*pieces, *after)
 
 
+def stack_kernel(number, *refs):
+    pieces, out = refs[:number], refs[-1]
+    rows = pieces[0].shape[0] // 2
+    for side in range(2):
+        picked = [piece[side * rows : (side + 1) * rows, :] for piece in pieces]
+        out[side * number * rows : (side + 1) * number * rows, :] = jnp.concatenate(picked, axis=0)
+
+
+def stack(pieces, after=()):
+    number = len(pieces)
+    rows, width = pieces[0].shape
+    return pl.pallas_call(
+        functools.partial(stack_kernel, number),
+        in_specs=[VMEM] * number + [pl.BlockSpec(memory_space=pl.ANY)] * len(after),
+        out_specs=VMEM,
+        out_shape=bf16(number * rows, width),
+        compiler_params=params(16),
+        cost_estimate=cost(0, 4 * number * rows * width),
+        name="stack_rows",
+    )(*pieces, *after)
+
+
 def load_kernel(chunk, pair_hbm, down_hbm, after, pair, down, sems):
     del after
     width = down.shape[1]
@@ -184,13 +206,12 @@
     got, pair, down = refs[:count], refs[count], refs[count + 1]
     gate_out, up_out, hidden_out, tok_all, cot_all, parts_hbm = refs[count + 2 : count + 8]
     parts, acc_gate, acc_up, acc_hid, sems = refs[count + 8 :]
-    half = got[0].shape[0] // 2
     width = got[0].shape[1]
     steps = width // chunk
     for step in range(steps):
         at = slice(step * chunk, (step + 1) * chunk)
-        tok = jnp.concatenate([piece[:half, at] for piece in got], axis=0)
-        cot = jnp.concatenate([piece[half:, at] for piece in got], axis=0)
+        tok = jnp.concatenate([piece[: piece.shape[0] // 2, at] for piece in got], axis=0)
+        cot = jnp.concatenate([piece[piece.shape[0] // 2 :, at] for piece in got], axis=0)
         tok_all[:, at] = tok
         cot_all[:, at] = cot
         gate = dot_nn(tok, pair[0, at, :])
@@ -402,17 +423,23 @@
     arrived = [send(pieces[high], 0, high * near) for high in range(far)]
     early, late = range(far // 2), range(far // 2, far)
     first = [send(pieces[high], group, high * near) for group in range(1, groups) for high in early]
-    second = [send(arrived[high], group, 0) for group in range(1, groups) for high in late]
+    first = merge([arrived[high] for high in early] + first)
     loaded = pltpu.with_memory_space_constraint(down, pltpu.VMEM)
-    first = merge([arrived[high] for high in early] + first, (loaded,))
-    second = merge([arrived[high] for high in late] + second, (first[0],))
-    got = [send(rows[low], 0, low) for rows in (first, second) for low in range(near)]
+    second = merge([arrived[high] for high in late], (loaded,))
+    second = stack([send(second[low], 0, low) for low in range(near)], (first[0],))
+    got = [send(first[low], 0, low) for low in range(near)]
+    got += [send(second, group, 0) for group in range(groups)]
     homes = [
         (group, high * near + low)
-        for part in (early, late)
         for low in range(near)
         for group in range(groups)
-        for high in part
+        for high in early
+    ]
+    homes += [
+        (group, high * near + low)
+        for group in range(groups)
+        for low in range(near)
+        for high in late
     ]
     gate_grad, up_grad, hidden, tok, cot, parts = expert_rows(
         got, homes, pair, down, experts, groups

time: 67.6 us -> 65 us (0.962)
  starting transfers between devices: 20.6 us -> 18.9 us
  waiting for transfers between devices: 17.7 us -> 17 us
    all_to_all x1, starting transfers between devices: 5.7 us -> 4.57 us  [per_device(): lax.all_to_all(parts, ('dp', 'expert'), split_axis=0, concat_axis=0, tile...]
    ppermute x13 -> x12, waiting for transfers between devices: 10.6 us -> 9.83 us  [send(): return lax.ppermute(value, ('dp', 'expert'), pairs)]
    ppermute x13 -> x12, starting transfers between devices: 14.9 us -> 14.3 us  [send(): return lax.ppermute(value, ('dp', 'expert'), pairs)]
  transfers between devices with their start and end apart: 14 -> 13, of which waited for: 8 -> 6; matrix products, arithmetic and copies ran while one was open for 0% -> 0% of each run, Pallas kernels for 24% -> 24%
where the time goes in v5:
time: 65 us; the launch traced here: 64.7 us
  Pallas kernels  28 us (43%)
  starting transfers between devices  18.9 us (29%)
  waiting for transfers between devices  17 us (26%)
  between operations  0.9 us (1%)
    ppermute x12, starting transfers between devices, send(): return lax.ppermute(value, ('dp', 'expert'), pairs)  14.3 us
    ppermute x12, waiting for transfers between devices, send(): return lax.ppermute(value, ('dp', 'expert'), pairs)  9.83 us
    pallas_call x1, Pallas kernels, expert_rows(): pl.pallas_call(functools.partial(expert_kernel, homes, experts, groups, c...  8.89 us
    all_to_all x1, waiting for transfers between devices, per_device(): lax.all_to_all(parts, ('dp', 'expert'), split_axis=0, concat_axis=0, tile...  7.14 us
    pallas_call x1, Pallas kernels, load(): pl.pallas_call(functools.partial(load_kernel, chunk), in_specs=[HBM] * 2...  6.5 us
    pallas_call x1, Pallas kernels, pair_grad(): pl.pallas_call(functools.partial(pair_grad_kernel, blocks, chunk), in_spe...  5.26 us
    all_to_all x1, starting transfers between devices, per_device(): lax.all_to_all(parts, ('dp', 'expert'), split_axis=0, concat_axis=0, tile...  4.57 us
    pallas_call x1, Pallas kernels, down_grad(): pl.pallas_call(functools.partial(down_grad_kernel, blocks, chunk), in_spe...  3.32 us
  transfers between devices with their start and end apart: 13, of which 6 were waited for; matrix products, arithmetic and copies ran while one was open for 0% of the time, Pallas kernels for 24%

profile of v5, /device:TPU:0, one launch (start us, length us, event | category | flops | bytes accessed | tf_op | source)
XLA Modules:
  0.0 64.7 jit_solution(9622563411692372342)
XLA Ops:
  0.6 2.0 %route_rows.1 = (bf16[4,4,4096]{2,1,0:T(4,128)(2,1)S(1)}, bf16[4,4,4096]{2,1,0:T(4,128)(2,1)S(1)}, bf16[4,4,4096]{2,1,0:T(4,128)(2,1)S(1)}, bf16[4,4,4096]{2,1,0:T(4,128)(2,1)S(1)}, bf16[32,128]{1,0:T(8,128)(2,1)S(1)}) custom-call(s32[1,128]{1,0:T(1,128)} %bitcast.6, f32[1,128]{1,0:T(1,128)} %bitcast.7, bf16[128,4096]{1,0:T(8,128)(2,1)} %act_hbm.1, ...), custom_call_target="tpu_custom_call" | custom-call | flops 67108864 | bytes 2097152 | tf_op jit(solution)/shard_map/route_rows/pallas_call | solution.py:111
  2.7 4.1 %collective-permute-start.6 = (bf16[4,4,4096]{2,1,0:T(4,128)(2,1)S(1)}, bf16[4,4,4096]{2,1,0:T(4,128)(2,1)S(1)}, u32[]{:S(2)}, u32[]{:S(2)}) collective-permute-start(bf16[4,4,4096]{2,1,0:T(4,128)(2,1)S(1)} %get-tuple-element.30), channel_id=1, source_target_pairs={{0,8},{1,9},{2,10},{3,11},{4,12},{5,13},{6,14},{7,15},{8,0},{9,1},... | collective-permute-start | bytes 393224 | tf_op jit(solution)/shard_map/ppermute | solution.py:413
  6.8 1.4 %collective-permute-start.7 = (bf16[4,4,4096]{2,1,0:T(4,128)(2,1)S(1)}, bf16[4,4,4096]{2,1,0:T(4,128)(2,1)S(1)}, u32[]{:S(2)}, u32[]{:S(2)}) collective-permute-start(bf16[4,4,4096]{2,1,0:T(4,128)(2,1)S(1)} %get-tuple-element.31), channel_id=1, source_target_pairs={{0,12},{1,13},{2,14},{3,15},{4,8},{5,9},{6,10},{7,11},{8,4},{9,5},... | collective-permute-start | bytes 393224 | tf_op jit(solution)/shard_map/ppermute | solution.py:413
  8.1 1.5 %collective-permute-start.1 = (bf16[4,4,4096]{2,1,0:T(4,128)(2,1)S(1)}, bf16[4,4,4096]{2,1,0:T(4,128)(2,1)S(1)}, u32[]{:S(2)}, u32[]{:S(2)}) collective-permute-start(bf16[4,4,4096]{2,1,0:T(4,128)(2,1)S(1)} %get-tuple-element.24.refs_0_), channel_id=1, source_target_pairs={{0,16},{1,17},{2,18},{3,19},{4,20},{5,21},{6,22},{7,23},{8,24},{9,... | collective-permute-start | bytes 393224 | tf_op jit(solution)/shard_map/ppermute | solution.py:413
  9.8 1.8 %collective-permute-start = (bf16[4,4,4096]{2,1,0:T(4,128)(2,1)S(1)}, bf16[4,4,4096]{2,1,0:T(4,128)(2,1)S(1)}, u32[]{:S(2)}, u32[]{:S(2)}) collective-permute-start(bf16[4,4,4096]{2,1,0:T(4,128)(2,1)S(1)} %get-tuple-element.25), channel_id=1, source_target_pairs={{0,4},{1,5},{2,6},{3,7},{4,0},{5,1},{6,2},{7,3},{8,12},{9,13},{10,... | collective-permute-start | bytes 393224 | tf_op jit(solution)/shard_map/ppermute | solution.py:413
  11.6 6.5 %load_weights.1 = (bf16[2,4096,768]{2,1,0:T(8,128)(2,1)S(1)}, bf16[768,4096]{1,0:T(8,128)(2,1)S(1)}) custom-call(bf16[2,4096,768]{2,1,0:T(8,128)(2,1)} %bitcast.4, bf16[768,4096]{1,0:T(8,128)(2,1)} %bitcast.5, bf16[32,128]{1,0:T(8,128)(2,1)S(1)} %get-tuple-element.32.after.place_ref), custom_call_target="tpu_custom_call" | custom-call | bytes 18874368 | tf_op jit(solution)/shard_map/load_weights/pallas_call | solution.py:193
  18.1 0.2 merge_rows.3
  18.4 1.6 %collective-permute-start.9 = (bf16[8,4096]{1,0:T(8,128)(2,1)S(1)}, bf16[8,4096]{1,0:T(8,128)(2,1)S(1)}, u32[]{:S(2)}, u32[]{:S(2)}) collective-permute-start(bf16[8,4096]{1,0:T(8,128)(2,1)S(1)} %get-tuple-element.36), channel_id=1, source_target_pairs={{0,2},{1,3},{2,0},{3,1},{4,6},{5,7},{6,4},{7,5},{8,10},{9,11},{10,... | collective-permute-start | bytes 196616 | tf_op jit(solution)/shard_map/ppermute | solution.py:413
  20.0 0.3 collective-permute-start.10
  20.3 0.8 %collective-permute-done.refs_1_ = bf16[4,4,4096]{2,1,0:T(4,128)(2,1)S(1)} collective-permute-done((bf16[4,4,4096]{2,1,0:T(4,128)(2,1)S(1)}, bf16[4,4,4096]{2,1,0:T(4,128)(2,1)S(1)}, u32[]{:S(2)}, u32[]{:S(2)}) %collective-permute-start) | collective-permute-done | bytes 131104 | tf_op jit(solution)/shard_map/ppermute | solution.py:413
  21.1 0.4 merge_rows.2
  21.5 1.4 %collective-permute-done.9.refs_2_ = bf16[8,4096]{1,0:T(8,128)(2,1)S(1)} collective-permute-done((bf16[8,4096]{1,0:T(8,128)(2,1)S(1)}, bf16[8,4096]{1,0:T(8,128)(2,1)S(1)}, u32[]{:S(2)}, u32[]{:S(2)}) %collective-permute-start.9) | collective-permute-done | bytes 65568 | tf_op jit(solution)/shard_map/ppermute | solution.py:413
  22.9 1.1 %collective-permute-done.10.refs_3_ = bf16[8,4096]{1,0:T(8,128)(2,1)S(1)} collective-permute-done((bf16[8,4096]{1,0:T(8,128)(2,1)S(1)}, bf16[8,4096]{1,0:T(8,128)(2,1)S(1)}, u32[]{:S(2)}, u32[]{:S(2)}) %collective-permute-start.10) | collective-permute-done | bytes 65568 | tf_op jit(solution)/shard_map/ppermute | solution.py:413
  24.1 1.6 %collective-permute-start.11 = (bf16[32,4096]{1,0:T(8,128)(2,1)S(1)}, bf16[32,4096]{1,0:T(8,128)(2,1)S(1)}, u32[]{:S(2)}, u32[]{:S(2)}) collective-permute-start(bf16[32,4096]{1,0:T(8,128)(2,1)S(1)} %stack_rows.1.refs_4_), channel_id=1, source_target_pairs={{0,16},{1,17},{2,18},{3,19},{4,20},{5,21},{6,22},{7,23},{8,24},{9,... | collective-permute-start | bytes 786440 | tf_op jit(solution)/shard_map/ppermute | solution.py:413
  25.7 1.3 %collective-permute-start.4 = (bf16[16,4096]{1,0:T(8,128)(2,1)S(1)}, bf16[16,4096]{1,0:T(8,128)(2,1)S(1)}, u32[]{:S(2)}, u32[]{:S(2)}) collective-permute-start(bf16[16,4096]{1,0:T(8,128)(2,1)S(1)} %get-tuple-element.28), channel_id=1, source_target_pairs={{0,2},{1,3},{2,0},{3,1},{4,6},{5,7},{6,4},{7,5},{8,10},{9,11},{10,... | collective-permute-start | bytes 393224 | tf_op jit(solution)/shard_map/ppermute | solution.py:413
  27.0 0.5 collective-permute-start.5
  27.6 4.4 %collective-permute-done.4.refs_2_ = bf16[16,4096]{1,0:T(8,128)(2,1)S(1)} collective-permute-done((bf16[16,4096]{1,0:T(8,128)(2,1)S(1)}, bf16[16,4096]{1,0:T(8,128)(2,1)S(1)}, u32[]{:S(2)}, u32[]{:S(2)}) %collective-permute-start.4) | collective-permute-done | bytes 131104 | tf_op jit(solution)/shard_map/ppermute | solution.py:413
  32.0 2.0 %collective-permute-done.5.refs_3_ = bf16[16,4096]{1,0:T(8,128)(2,1)S(1)} collective-permute-done((bf16[16,4096]{1,0:T(8,128)(2,1)S(1)}, bf16[16,4096]{1,0:T(8,128)(2,1)S(1)}, u32[]{:S(2)}, u32[]{:S(2)}) %collective-permute-start.5) | collective-permute-done | bytes 131104 | tf_op jit(solution)/shard_map/ppermute | solution.py:413
  34.0 8.9 %expert_rows.1 = (bf16[64,768]{1,0:T(8,128)(2,1)S(1)}, bf16[64,768]{1,0:T(8,128)(2,1)S(1)}, bf16[64,768]{1,0:T(8,128)(2,1)S(1)}, bf16[64,4096]{1,0:T(8,128)(2,1)...) custom-call(bf16[16,4096]{1,0:T(8,128)(2,1)S(1)} %get-tuple-element.26.refs_4_.refs_0_, ...), custom_call_target="tpu_custom_call" | custom-call | flops 2013265920 | bytes 18874368 | tf_op jit(solution)/shard_map/expert_rows/pallas_call | solution.py:263
  42.9 4.6 %all-to-all-start = ((bf16[32,2,4096]{2,1,0:T(2,128)(2,1)}), bf16[32,2,4096]{2,1,0:T(2,128)(2,1)S(1)}, u32[]{:S(2)}, u32[]{:S(2)}) async-start(bf16[32,2,4096]{2,1,0:T(2,128)(2,1)} %get-tuple-element.39), calls=%async_computation | async-start | bytes 1048576 | tf_op jit(solution)/shard_map/all_to_all | solution.py:447
  47.5 3.3 %down_grad.1 = bf16[1,768,4096]{2,1,0:T(8,128)(2,1)} custom-call(bf16[64,4096]{1,0:T(8,128)(2,1)S(1)} %get-tuple-element.43.refs_0_, bf16[64,768]{1,0:T(8,128)(2,1)S(1)} %get-tuple-element.44.refs_1_), custom_call_target="tpu_custom_call" | custom-call | flops 402653184 | bytes 6291456 | tf_op jit(solution)/shard_map/down_grad/pallas_call | solution.py:349
  50.8 5.3 %pair_grad.1 = bf16[1,2,4096,768]{3,2,1,0:T(8,128)(2,1)} custom-call(bf16[64,4096]{1,0:T(8,128)(2,1)S(1)} %get-tuple-element.40.refs_0_, bf16[64,768]{1,0:T(8,128)(2,1)S(1)} %get-tuple-element.41.refs_1_, bf16[64,768]{1,0:T(8,128)(2,1)S(1)} %get-tuple-element.42.refs_2_), custom_call_target="tpu_custom_call" | custom-call | flops 805306368 | bytes 12582912 | tf_op jit(solution)/shard_map/pair_grad/pallas_call | solution.py:312
  56.1 7.1 %all-to-all-done.rows_ref = bf16[32,2,4096]{2,1,0:T(2,128)(2,1)S(1)} async-done(((bf16[32,2,4096]{2,1,0:T(2,128)(2,1)}), bf16[32,2,4096]{2,1,0:T(2,128)(2,1)S(1)}, u32[]{:S(2)}, u32[]{:S(2)}) %all-to-all-start) | async-done | bytes 524320 | tf_op jit(solution)/shard_map/all_to_all | solution.py:447
  63.2 1.3 %spread_rows.1 = bf16[128,4096]{1,0:T(8,128)(2,1)} custom-call(bf16[32,2,4096]{2,1,0:T(2,128)(2,1)S(1)} %all-to-all-done.rows_ref, bf16[32,128]{1,0:T(8,128)(2,1)S(1)} %get-tuple-element.32.after.place_ref), custom_call_target="tpu_custom_call" | custom-call | flops 33554432 | bytes 1048576 | tf_op jit(solution)/shard_map/spread_rows/pallas_call | solution.py:384
  (11 shorter events, 0.4 us)
Async XLA Ops:
  2.7 15.4 %collective-permute-start.6 = (bf16[4,4,4096]{2,1,0:T(4,128)(2,1)S(1)}, bf16[4,4,4096]{2,1,0:T(4,128)(2,1)S(1)}, u32[]{:S(2)}, u32[]{:S(2)}) collective-permute-start(bf16[4,4,4096]{2,1,0:T(4,128)(2,1)S(1)} %get-tuple-element.30), channel_id=1, source_target_pairs={{0,8},{1,9},{2,10},{3,11},{4,12},{5,13},{6,14},{7,15},{8,0},{9,1},... | collective-permute-start | bytes 393224 | tf_op jit(solution)/shard_map/ppermute | solution.py:413
  6.8 11.4 %collective-permute-start.7 = (bf16[4,4,4096]{2,1,0:T(4,128)(2,1)S(1)}, bf16[4,4,4096]{2,1,0:T(4,128)(2,1)S(1)}, u32[]{:S(2)}, u32[]{:S(2)}) collective-permute-start(bf16[4,4,4096]{2,1,0:T(4,128)(2,1)S(1)} %get-tuple-element.31), channel_id=1, source_target_pairs={{0,12},{1,13},{2,14},{3,15},{4,8},{5,9},{6,10},{7,11},{8,4},{9,5},... | collective-permute-start | bytes 393224 | tf_op jit(solution)/shard_map/ppermute | solution.py:413
  8.1 11.8 %collective-permute-start.1 = (bf16[4,4,4096]{2,1,0:T(4,128)(2,1)S(1)}, bf16[4,4,4096]{2,1,0:T(4,128)(2,1)S(1)}, u32[]{:S(2)}, u32[]{:S(2)}) collective-permute-start(bf16[4,4,4096]{2,1,0:T(4,128)(2,1)S(1)} %get-tuple-element.24.refs_0_), channel_id=1, source_target_pairs={{0,16},{1,17},{2,18},{3,19},{4,20},{5,21},{6,22},{7,23},{8,24},{9,... | collective-permute-start | bytes 393224 | tf_op jit(solution)/shard_map/ppermute | solution.py:413
  9.6 10.6 %collective-permute-start.2 = (bf16[4,4,4096]{2,1,0:T(4,128)(2,1)S(1)}, bf16[4,4,4096]{2,1,0:T(4,128)(2,1)S(1)}, u32[]{:S(2)}, u32[]{:S(2)}) collective-permute-start(bf16[4,4,4096]{2,1,0:T(4,128)(2,1)S(1)} %get-tuple-element.25), channel_id=1, source_target_pairs={{0,20},{1,21},{2,22},{3,23},{4,16},{5,17},{6,18},{7,19},{8,28},{9,... | collective-permute-start | bytes 393224 | tf_op jit(solution)/shard_map/ppermute | solution.py:413
  9.8 11.3 %collective-permute-start = (bf16[4,4,4096]{2,1,0:T(4,128)(2,1)S(1)}, bf16[4,4,4096]{2,1,0:T(4,128)(2,1)S(1)}, u32[]{:S(2)}, u32[]{:S(2)}) collective-permute-start(bf16[4,4,4096]{2,1,0:T(4,128)(2,1)S(1)} %get-tuple-element.25), channel_id=1, source_target_pairs={{0,4},{1,5},{2,6},{3,7},{4,0},{5,1},{6,2},{7,3},{8,12},{9,13},{10,... | collective-permute-start | bytes 393224 | tf_op jit(solution)/shard_map/ppermute | solution.py:413
  18.3 3.1 %collective-permute-start.8 = (bf16[8,4096]{1,0:T(8,128)(2,1)S(1)}, bf16[8,4096]{1,0:T(8,128)(2,1)S(1)}, u32[]{:S(2)}, u32[]{:S(2)}) collective-permute-start(bf16[8,4096]{1,0:T(8,128)(2,1)S(1)} %get-tuple-element.35), channel_id=1, source_target_pairs={{0,1},{1,0},{2,3},{3,2},{4,5},{5,4},{6,7},{7,6},{8,9},{9,8},{10,11... | collective-permute-start | bytes 196616 | tf_op jit(solution)/shard_map/ppermute | solution.py:413
  18.4 4.5 %collective-permute-start.9 = (bf16[8,4096]{1,0:T(8,128)(2,1)S(1)}, bf16[8,4096]{1,0:T(8,128)(2,1)S(1)}, u32[]{:S(2)}, u32[]{:S(2)}) collective-permute-start(bf16[8,4096]{1,0:T(8,128)(2,1)S(1)} %get-tuple-element.36), channel_id=1, source_target_pairs={{0,2},{1,3},{2,0},{3,1},{4,6},{5,7},{6,4},{7,5},{8,10},{9,11},{10,... | collective-permute-start | bytes 196616 | tf_op jit(solution)/shard_map/ppermute | solution.py:413
  20.0 4.0 %collective-permute-start.10 = (bf16[8,4096]{1,0:T(8,128)(2,1)S(1)}, bf16[8,4096]{1,0:T(8,128)(2,1)S(1)}, u32[]{:S(2)}, u32[]{:S(2)}) collective-permute-start(bf16[8,4096]{1,0:T(8,128)(2,1)S(1)} %get-tuple-element.37), channel_id=1, source_target_pairs={{0,3},{1,2},{2,1},{3,0},{4,7},{5,6},{6,5},{7,4},{8,11},{9,10},{10,... | collective-permute-start | bytes 196616 | tf_op jit(solution)/shard_map/ppermute | solution.py:413
  24.1 9.9 %collective-permute-start.11 = (bf16[32,4096]{1,0:T(8,128)(2,1)S(1)}, bf16[32,4096]{1,0:T(8,128)(2,1)S(1)}, u32[]{:S(2)}, u32[]{:S(2)}) collective-permute-start(bf16[32,4096]{1,0:T(8,128)(2,1)S(1)} %stack_rows.1.refs_4_), channel_id=1, source_target_pairs={{0,16},{1,17},{2,18},{3,19},{4,20},{5,21},{6,22},{7,23},{8,24},{9,... | collective-permute-start | bytes 786440 | tf_op jit(solution)/shard_map/ppermute | solution.py:413
  25.7 1.9 %collective-permute-start.3 = (bf16[16,4096]{1,0:T(8,128)(2,1)S(1)}, bf16[16,4096]{1,0:T(8,128)(2,1)S(1)}, u32[]{:S(2)}, u32[]{:S(2)}) collective-permute-start(bf16[16,4096]{1,0:T(8,128)(2,1)S(1)} %get-tuple-element.27), channel_id=1, source_target_pairs={{0,1},{1,0},{2,3},{3,2},{4,5},{5,4},{6,7},{7,6},{8,9},{9,8},{10,11... | collective-permute-start | bytes 393224 | tf_op jit(solution)/shard_map/ppermute | solution.py:413
  25.7 6.3 %collective-permute-start.4 = (bf16[16,4096]{1,0:T(8,128)(2,1)S(1)}, bf16[16,4096]{1,0:T(8,128)(2,1)S(1)}, u32[]{:S(2)}, u32[]{:S(2)}) collective-permute-start(bf16[16,4096]{1,0:T(8,128)(2,1)S(1)} %get-tuple-element.28), channel_id=1, source_target_pairs={{0,2},{1,3},{2,0},{3,1},{4,6},{5,7},{6,4},{7,5},{8,10},{9,11},{10,... | collective-permute-start | bytes 393224 | tf_op jit(solution)/shard_map/ppermute | solution.py:413
  27.0 7.0 %collective-permute-start.5 = (bf16[16,4096]{1,0:T(8,128)(2,1)S(1)}, bf16[16,4096]{1,0:T(8,128)(2,1)S(1)}, u32[]{:S(2)}, u32[]{:S(2)}) collective-permute-start(bf16[16,4096]{1,0:T(8,128)(2,1)S(1)} %get-tuple-element.29), channel_id=1, source_target_pairs={{0,3},{1,2},{2,1},{3,0},{4,7},{5,6},{6,5},{7,4},{8,11},{9,10},{10,... | collective-permute-start | bytes 393224 | tf_op jit(solution)/shard_map/ppermute | solution.py:413
  42.9 20.3 %all-to-all-start = ((bf16[32,2,4096]{2,1,0:T(2,128)(2,1)}), bf16[32,2,4096]{2,1,0:T(2,128)(2,1)S(1)}, u32[]{:S(2)}, u32[]{:S(2)}) async-start(bf16[32,2,4096]{2,1,0:T(2,128)(2,1)} %get-tuple-element.39), calls=%async_computation | async-start | bytes 1048576 | tf_op jit(solution)/shard_map/all_to_all | solution.py:447

commit v6 on v5

--- a/solution.py
+++ b/solution.py
@@ -426,9 +426,11 @@
     first = merge([arrived[high] for high in early] + first)
     loaded = pltpu.with_memory_space_constraint(down, pltpu.VMEM)
     second = merge([arrived[high] for high in late], (loaded,))
-    second = stack([send(second[low], 0, low) for low in range(near)], (first[0],))
+    mine = [send(second[low], 0, low) for low in range(near)]
+    second = [stack(mine[: near // 2])]
+    second.append(stack(mine[near // 2 :], (second[0],)))
     got = [send(first[low], 0, low) for low in range(near)]
-    got += [send(second, group, 0) for group in range(groups)]
+    got += [send(part, group, 0) for group in range(groups) for part in second]
     homes = [
         (group, high * near + low)
         for low in range(near)

time: 65 us -> 65 us (level)
  starting transfers between devices: 18.9 us -> 21 us
  waiting for transfers between devices: 17 us -> 14.9 us
    ppermute x12 -> x13, waiting for transfers between devices: 9.83 us -> 7.72 us  [send(): return lax.ppermute(value, ('dp', 'expert'), pairs)]
    all_to_all x1, starting transfers between devices: 4.57 us -> 6.08 us  [per_device(): lax.all_to_all(parts, ('dp', 'expert'), split_axis=0, concat_axis=0, tile...]
    ppermute x12 -> x13, starting transfers between devices: 14.3 us -> 14.9 us  [send(): return lax.ppermute(value, ('dp', 'expert'), pairs)]
  transfers between devices with their start and end apart: 13 -> 14, of which waited for: 6 -> 7; matrix products, arithmetic and copies ran while one was open for 0% -> 0% of each run, Pallas kernels for 24% -> 24%
where the time goes in v6:
time: 65 us; the launch traced here: 64.7 us
  Pallas kernels  28 us (43%)
  starting transfers between devices  21 us (32%)
  waiting for transfers between devices  14.9 us (23%)
  between operations  0.91 us (1%)
    ppermute x13, starting transfers between devices, send(): return lax.ppermute(value, ('dp', 'expert'), pairs)  14.9 us
    pallas_call x1, Pallas kernels, expert_rows(): pl.pallas_call(functools.partial(expert_kernel, homes, experts, groups, c...  8.87 us
    ppermute x13, waiting for transfers between devices, send(): return lax.ppermute(value, ('dp', 'expert'), pairs)  7.72 us
    all_to_all x1, waiting for transfers between devices, per_device(): lax.all_to_all(parts, ('dp', 'expert'), split_axis=0, concat_axis=0, tile...  7.14 us
    pallas_call x1, Pallas kernels, load(): pl.pallas_call(functools.partial(load_kernel, chunk), in_specs=[HBM] * 2...  6.5 us
    all_to_all x1, starting transfers between devices, per_device(): lax.all_to_all(parts, ('dp', 'expert'), split_axis=0, concat_axis=0, tile...  6.08 us
    pallas_call x1, Pallas kernels, pair_grad(): pl.pallas_call(functools.partial(pair_grad_kernel, blocks, chunk), in_spe...  5.26 us
    pallas_call x1, Pallas kernels, down_grad(): pl.pallas_call(functools.partial(down_grad_kernel, blocks, chunk), in_spe...  3.32 us
  transfers between devices with their start and end apart: 14, of which 7 were waited for; matrix products, arithmetic and copies ran while one was open for 0% of the time, Pallas kernels for 24%

profile of v6, /device:TPU:0, one launch (start us, length us, event | category | flops | bytes accessed | tf_op | source)
XLA Modules:
  0.0 64.7 jit_solution(9361301483769973576)
XLA Ops:
  0.6 2.0 %route_rows.1 = (bf16[4,4,4096]{2,1,0:T(4,128)(2,1)S(1)}, bf16[4,4,4096]{2,1,0:T(4,128)(2,1)S(1)}, bf16[4,4,4096]{2,1,0:T(4,128)(2,1)S(1)}, bf16[4,4,4096]{2,1,0:T(4,128)(2,1)S(1)}, bf16[32,128]{1,0:T(8,128)(2,1)S(1)}) custom-call(s32[1,128]{1,0:T(1,128)} %bitcast.6, f32[1,128]{1,0:T(1,128)} %bitcast.7, bf16[128,4096]{1,0:T(8,128)(2,1)} %act_hbm.1, ...), custom_call_target="tpu_custom_call" | custom-call | flops 67108864 | bytes 2097152 | tf_op jit(solution)/shard_map/route_rows/pallas_call | solution.py:111
  2.7 4.1 %collective-permute-start.6 = (bf16[4,4,4096]{2,1,0:T(4,128)(2,1)S(1)}, bf16[4,4,4096]{2,1,0:T(4,128)(2,1)S(1)}, u32[]{:S(2)}, u32[]{:S(2)}) collective-permute-start(bf16[4,4,4096]{2,1,0:T(4,128)(2,1)S(1)} %get-tuple-element.30), channel_id=1, source_target_pairs={{0,8},{1,9},{2,10},{3,11},{4,12},{5,13},{6,14},{7,15},{8,0},{9,1},... | collective-permute-start | bytes 393224 | tf_op jit(solution)/shard_map/ppermute | solution.py:413
  6.8 1.4 %collective-permute-start.7 = (bf16[4,4,4096]{2,1,0:T(4,128)(2,1)S(1)}, bf16[4,4,4096]{2,1,0:T(4,128)(2,1)S(1)}, u32[]{:S(2)}, u32[]{:S(2)}) collective-permute-start(bf16[4,4,4096]{2,1,0:T(4,128)(2,1)S(1)} %get-tuple-element.31), channel_id=1, source_target_pairs={{0,12},{1,13},{2,14},{3,15},{4,8},{5,9},{6,10},{7,11},{8,4},{9,5},... | collective-permute-start | bytes 393224 | tf_op jit(solution)/shard_map/ppermute | solution.py:413
  8.1 1.5 %collective-permute-start.1 = (bf16[4,4,4096]{2,1,0:T(4,128)(2,1)S(1)}, bf16[4,4,4096]{2,1,0:T(4,128)(2,1)S(1)}, u32[]{:S(2)}, u32[]{:S(2)}) collective-permute-start(bf16[4,4,4096]{2,1,0:T(4,128)(2,1)S(1)} %get-tuple-element.24.refs_0_), channel_id=1, source_target_pairs={{0,16},{1,17},{2,18},{3,19},{4,20},{5,21},{6,22},{7,23},{8,24},{9,... | collective-permute-start | bytes 393224 | tf_op jit(solution)/shard_map/ppermute | solution.py:413
  9.8 1.8 %collective-permute-start = (bf16[4,4,4096]{2,1,0:T(4,128)(2,1)S(1)}, bf16[4,4,4096]{2,1,0:T(4,128)(2,1)S(1)}, u32[]{:S(2)}, u32[]{:S(2)}) collective-permute-start(bf16[4,4,4096]{2,1,0:T(4,128)(2,1)S(1)} %get-tuple-element.25), channel_id=1, source_target_pairs={{0,4},{1,5},{2,6},{3,7},{4,0},{5,1},{6,2},{7,3},{8,12},{9,13},{10,... | collective-permute-start | bytes 393224 | tf_op jit(solution)/shard_map/ppermute | solution.py:413
  11.6 6.5 %load_weights.1 = (bf16[2,4096,768]{2,1,0:T(8,128)(2,1)S(1)}, bf16[768,4096]{1,0:T(8,128)(2,1)S(1)}) custom-call(bf16[2,4096,768]{2,1,0:T(8,128)(2,1)} %bitcast.4, bf16[768,4096]{1,0:T(8,128)(2,1)} %bitcast.5, bf16[32,128]{1,0:T(8,128)(2,1)S(1)} %get-tuple-element.32.after.place_ref), custom_call_target="tpu_custom_call" | custom-call | bytes 18874368 | tf_op jit(solution)/shard_map/load_weights/pallas_call | solution.py:193
  18.4 1.6 %collective-permute-start.9 = (bf16[8,4096]{1,0:T(8,128)(2,1)S(1)}, bf16[8,4096]{1,0:T(8,128)(2,1)S(1)}, u32[]{:S(2)}, u32[]{:S(2)}) collective-permute-start(bf16[8,4096]{1,0:T(8,128)(2,1)S(1)} %get-tuple-element.36), channel_id=1, source_target_pairs={{0,2},{1,3},{2,0},{3,1},{4,6},{5,7},{6,4},{7,5},{8,10},{9,11},{10,... | collective-permute-start | bytes 196616 | tf_op jit(solution)/shard_map/ppermute | solution.py:413
  20.0 0.3 collective-permute-start.10
  20.3 0.8 %collective-permute-done.refs_1_ = bf16[4,4,4096]{2,1,0:T(4,128)(2,1)S(1)} collective-permute-done((bf16[4,4,4096]{2,1,0:T(4,128)(2,1)S(1)}, bf16[4,4,4096]{2,1,0:T(4,128)(2,1)S(1)}, u32[]{:S(2)}, u32[]{:S(2)}) %collective-permute-start) | collective-permute-done | bytes 131104 | tf_op jit(solution)/shard_map/ppermute | solution.py:413
  21.1 0.4 merge_rows.2
  21.5 1.6 %collective-permute-start.4 = (bf16[16,4096]{1,0:T(8,128)(2,1)S(1)}, bf16[16,4096]{1,0:T(8,128)(2,1)S(1)}, u32[]{:S(2)}, u32[]{:S(2)}) collective-permute-start(bf16[16,4096]{1,0:T(8,128)(2,1)S(1)} %get-tuple-element.28), channel_id=1, source_target_pairs={{0,2},{1,3},{2,0},{3,1},{4,6},{5,7},{6,4},{7,5},{8,10},{9,11},{10,... | collective-permute-start | bytes 393224 | tf_op jit(solution)/shard_map/ppermute | solution.py:413
  23.5 0.6 collective-permute-done.10.refs_1_
  24.1 1.6 %collective-permute-start.12 = (bf16[16,4096]{1,0:T(8,128)(2,1)S(1)}, bf16[16,4096]{1,0:T(8,128)(2,1)S(1)}, u32[]{:S(2)}, u32[]{:S(2)}) collective-permute-start(bf16[16,4096]{1,0:T(8,128)(2,1)S(1)} %stack_rows.3.refs_5_), channel_id=1, source_target_pairs={{0,16},{1,17},{2,18},{3,19},{4,20},{5,21},{6,22},{7,23},{8,24},{9,... | collective-permute-start | bytes 393224 | tf_op jit(solution)/shard_map/ppermute | solution.py:413
  25.6 0.5 collective-permute-start.11
  26.2 1.7 %collective-permute-done.4.refs_2_ = bf16[16,4096]{1,0:T(8,128)(2,1)S(1)} collective-permute-done((bf16[16,4096]{1,0:T(8,128)(2,1)S(1)}, bf16[16,4096]{1,0:T(8,128)(2,1)S(1)}, u32[]{:S(2)}, u32[]{:S(2)}) %collective-permute-start.4) | collective-permute-done | bytes 131104 | tf_op jit(solution)/shard_map/ppermute | solution.py:413
  27.9 1.9 %collective-permute-done.5.refs_3_ = bf16[16,4096]{1,0:T(8,128)(2,1)S(1)} collective-permute-done((bf16[16,4096]{1,0:T(8,128)(2,1)S(1)}, bf16[16,4096]{1,0:T(8,128)(2,1)S(1)}, u32[]{:S(2)}, u32[]{:S(2)}) %collective-permute-start.5) | collective-permute-done | bytes 131104 | tf_op jit(solution)/shard_map/ppermute | solution.py:413
  29.8 0.7 %collective-permute-done.12.refs_7_ = bf16[16,4096]{1,0:T(8,128)(2,1)S(1)} collective-permute-done((bf16[16,4096]{1,0:T(8,128)(2,1)S(1)}, bf16[16,4096]{1,0:T(8,128)(2,1)S(1)}, u32[]{:S(2)}, u32[]{:S(2)}) %collective-permute-start.12) | collective-permute-done | bytes 131104 | tf_op jit(solution)/shard_map/ppermute | solution.py:413
  30.5 2.0 %collective-permute-done.11.refs_6_ = bf16[16,4096]{1,0:T(8,128)(2,1)S(1)} collective-permute-done((bf16[16,4096]{1,0:T(8,128)(2,1)S(1)}, bf16[16,4096]{1,0:T(8,128)(2,1)S(1)}, u32[]{:S(2)}, u32[]{:S(2)}) %collective-permute-start.11) | collective-permute-done | bytes 131104 | tf_op jit(solution)/shard_map/ppermute | solution.py:413
  32.5 8.9 %expert_rows.1 = (bf16[64,768]{1,0:T(8,128)(2,1)S(1)}, bf16[64,768]{1,0:T(8,128)(2,1)S(1)}, bf16[64,768]{1,0:T(8,128)(2,1)S(1)}, bf16[64,4096]{1,0:T(8,128)(2,1)...) custom-call(bf16[16,4096]{1,0:T(8,128)(2,1)S(1)} %get-tuple-element.26.refs_0_, ...), custom_call_target="tpu_custom_call" | custom-call | flops 2013265920 | bytes 18874368 | tf_op jit(solution)/shard_map/expert_rows/pallas_call | solution.py:263
  41.4 6.1 %all-to-all-start = ((bf16[32,2,4096]{2,1,0:T(2,128)(2,1)}), bf16[32,2,4096]{2,1,0:T(2,128)(2,1)S(1)}, u32[]{:S(2)}, u32[]{:S(2)}) async-start(bf16[32,2,4096]{2,1,0:T(2,128)(2,1)} %get-tuple-element.39), calls=%async_computation | async-start | bytes 1048576 | tf_op jit(solution)/shard_map/all_to_all | solution.py:449
  47.5 3.3 %down_grad.1 = bf16[1,768,4096]{2,1,0:T(8,128)(2,1)} custom-call(bf16[64,4096]{1,0:T(8,128)(2,1)S(1)} %get-tuple-element.43.refs_0_, bf16[64,768]{1,0:T(8,128)(2,1)S(1)} %get-tuple-element.44.refs_1_), custom_call_target="tpu_custom_call" | custom-call | flops 402653184 | bytes 6291456 | tf_op jit(solution)/shard_map/down_grad/pallas_call | solution.py:349
  50.8 5.3 %pair_grad.1 = bf16[1,2,4096,768]{3,2,1,0:T(8,128)(2,1)} custom-call(bf16[64,4096]{1,0:T(8,128)(2,1)S(1)} %get-tuple-element.40.refs_0_, bf16[64,768]{1,0:T(8,128)(2,1)S(1)} %get-tuple-element.41.refs_1_, bf16[64,768]{1,0:T(8,128)(2,1)S(1)} %get-tuple-element.42.refs_2_), custom_call_target="tpu_custom_call" | custom-call | flops 805306368 | bytes 12582912 | tf_op jit(solution)/shard_map/pair_grad/pallas_call | solution.py:312
  56.1 7.1 %all-to-all-done.rows_ref = bf16[32,2,4096]{2,1,0:T(2,128)(2,1)S(1)} async-done(((bf16[32,2,4096]{2,1,0:T(2,128)(2,1)}), bf16[32,2,4096]{2,1,0:T(2,128)(2,1)S(1)}, u32[]{:S(2)}, u32[]{:S(2)}) %all-to-all-start) | async-done | bytes 524320 | tf_op jit(solution)/shard_map/all_to_all | solution.py:449
  63.2 1.3 %spread_rows.1 = bf16[128,4096]{1,0:T(8,128)(2,1)} custom-call(bf16[32,2,4096]{2,1,0:T(2,128)(2,1)S(1)} %all-to-all-done.rows_ref, bf16[32,128]{1,0:T(8,128)(2,1)S(1)} %get-tuple-element.32.after.place_ref), custom_call_target="tpu_custom_call" | custom-call | flops 33554432 | bytes 1048576 | tf_op jit(solution)/shard_map/spread_rows/pallas_call | solution.py:384
  (14 shorter events, 0.9 us)
Async XLA Ops:
  2.7 15.4 %collective-permute-start.6 = (bf16[4,4,4096]{2,1,0:T(4,128)(2,1)S(1)}, bf16[4,4,4096]{2,1,0:T(4,128)(2,1)S(1)}, u32[]{:S(2)}, u32[]{:S(2)}) collective-permute-start(bf16[4,4,4096]{2,1,0:T(4,128)(2,1)S(1)} %get-tuple-element.30), channel_id=1, source_target_pairs={{0,8},{1,9},{2,10},{3,11},{4,12},{5,13},{6,14},{7,15},{8,0},{9,1},... | collective-permute-start | bytes 393224 | tf_op jit(solution)/shard_map/ppermute | solution.py:413
  6.8 11.4 %collective-permute-start.7 = (bf16[4,4,4096]{2,1,0:T(4,128)(2,1)S(1)}, bf16[4,4,4096]{2,1,0:T(4,128)(2,1)S(1)}, u32[]{:S(2)}, u32[]{:S(2)}) collective-permute-start(bf16[4,4,4096]{2,1,0:T(4,128)(2,1)S(1)} %get-tuple-element.31), channel_id=1, source_target_pairs={{0,12},{1,13},{2,14},{3,15},{4,8},{5,9},{6,10},{7,11},{8,4},{9,5},... | collective-permute-start | bytes 393224 | tf_op jit(solution)/shard_map/ppermute | solution.py:413
  8.1 11.8 %collective-permute-start.1 = (bf16[4,4,4096]{2,1,0:T(4,128)(2,1)S(1)}, bf16[4,4,4096]{2,1,0:T(4,128)(2,1)S(1)}, u32[]{:S(2)}, u32[]{:S(2)}) collective-permute-start(bf16[4,4,4096]{2,1,0:T(4,128)(2,1)S(1)} %get-tuple-element.24.refs_0_), channel_id=1, source_target_pairs={{0,16},{1,17},{2,18},{3,19},{4,20},{5,21},{6,22},{7,23},{8,24},{9,... | collective-permute-start | bytes 393224 | tf_op jit(solution)/shard_map/ppermute | solution.py:413
  9.6 10.6 %collective-permute-start.2 = (bf16[4,4,4096]{2,1,0:T(4,128)(2,1)S(1)}, bf16[4,4,4096]{2,1,0:T(4,128)(2,1)S(1)}, u32[]{:S(2)}, u32[]{:S(2)}) collective-permute-start(bf16[4,4,4096]{2,1,0:T(4,128)(2,1)S(1)} %get-tuple-element.25), channel_id=1, source_target_pairs={{0,20},{1,21},{2,22},{3,23},{4,16},{5,17},{6,18},{7,19},{8,28},{9,... | collective-permute-start | bytes 393224 | tf_op jit(solution)/shard_map/ppermute | solution.py:413
  9.8 11.3 %collective-permute-start = (bf16[4,4,4096]{2,1,0:T(4,128)(2,1)S(1)}, bf16[4,4,4096]{2,1,0:T(4,128)(2,1)S(1)}, u32[]{:S(2)}, u32[]{:S(2)}) collective-permute-start(bf16[4,4,4096]{2,1,0:T(4,128)(2,1)S(1)} %get-tuple-element.25), channel_id=1, source_target_pairs={{0,4},{1,5},{2,6},{3,7},{4,0},{5,1},{6,2},{7,3},{8,12},{9,13},{10,... | collective-permute-start | bytes 393224 | tf_op jit(solution)/shard_map/ppermute | solution.py:413
  18.3 4.8 %collective-permute-start.8 = (bf16[8,4096]{1,0:T(8,128)(2,1)S(1)}, bf16[8,4096]{1,0:T(8,128)(2,1)S(1)}, u32[]{:S(2)}, u32[]{:S(2)}) collective-permute-start(bf16[8,4096]{1,0:T(8,128)(2,1)S(1)} %get-tuple-element.35), channel_id=1, source_target_pairs={{0,1},{1,0},{2,3},{3,2},{4,5},{5,4},{6,7},{7,6},{8,9},{9,8},{10,11... | collective-permute-start | bytes 196616 | tf_op jit(solution)/shard_map/ppermute | solution.py:413
  18.4 5.0 %collective-permute-start.9 = (bf16[8,4096]{1,0:T(8,128)(2,1)S(1)}, bf16[8,4096]{1,0:T(8,128)(2,1)S(1)}, u32[]{:S(2)}, u32[]{:S(2)}) collective-permute-start(bf16[8,4096]{1,0:T(8,128)(2,1)S(1)} %get-tuple-element.36), channel_id=1, source_target_pairs={{0,2},{1,3},{2,0},{3,1},{4,6},{5,7},{6,4},{7,5},{8,10},{9,11},{10,... | collective-permute-start | bytes 196616 | tf_op jit(solution)/shard_map/ppermute | solution.py:413
  20.0 4.0 %collective-permute-start.10 = (bf16[8,4096]{1,0:T(8,128)(2,1)S(1)}, bf16[8,4096]{1,0:T(8,128)(2,1)S(1)}, u32[]{:S(2)}, u32[]{:S(2)}) collective-permute-start(bf16[8,4096]{1,0:T(8,128)(2,1)S(1)} %get-tuple-element.37), channel_id=1, source_target_pairs={{0,3},{1,2},{2,1},{3,0},{4,7},{5,6},{6,5},{7,4},{8,11},{9,10},{10,... | collective-permute-start | bytes 196616 | tf_op jit(solution)/shard_map/ppermute | solution.py:413
  21.5 4.7 %collective-permute-start.3 = (bf16[16,4096]{1,0:T(8,128)(2,1)S(1)}, bf16[16,4096]{1,0:T(8,128)(2,1)S(1)}, u32[]{:S(2)}, u32[]{:S(2)}) collective-permute-start(bf16[16,4096]{1,0:T(8,128)(2,1)S(1)} %get-tuple-element.27), channel_id=1, source_target_pairs={{0,1},{1,0},{2,3},{3,2},{4,5},{5,4},{6,7},{7,6},{8,9},{9,8},{10,11... | collective-permute-start | bytes 393224 | tf_op jit(solution)/shard_map/ppermute | solution.py:413
  21.5 6.4 %collective-permute-start.4 = (bf16[16,4096]{1,0:T(8,128)(2,1)S(1)}, bf16[16,4096]{1,0:T(8,128)(2,1)S(1)}, u32[]{:S(2)}, u32[]{:S(2)}) collective-permute-start(bf16[16,4096]{1,0:T(8,128)(2,1)S(1)} %get-tuple-element.28), channel_id=1, source_target_pairs={{0,2},{1,3},{2,0},{3,1},{4,6},{5,7},{6,4},{7,5},{8,10},{9,11},{10,... | collective-permute-start | bytes 393224 | tf_op jit(solution)/shard_map/ppermute | solution.py:413
  23.1 6.7 %collective-permute-start.5 = (bf16[16,4096]{1,0:T(8,128)(2,1)S(1)}, bf16[16,4096]{1,0:T(8,128)(2,1)S(1)}, u32[]{:S(2)}, u32[]{:S(2)}) collective-permute-start(bf16[16,4096]{1,0:T(8,128)(2,1)S(1)} %get-tuple-element.29), channel_id=1, source_target_pairs={{0,3},{1,2},{2,1},{3,0},{4,7},{5,6},{6,5},{7,4},{8,11},{9,10},{10,... | collective-permute-start | bytes 393224 | tf_op jit(solution)/shard_map/ppermute | solution.py:413
  24.1 6.4 %collective-permute-start.12 = (bf16[16,4096]{1,0:T(8,128)(2,1)S(1)}, bf16[16,4096]{1,0:T(8,128)(2,1)S(1)}, u32[]{:S(2)}, u32[]{:S(2)}) collective-permute-start(bf16[16,4096]{1,0:T(8,128)(2,1)S(1)} %stack_rows.3.refs_5_), channel_id=1, source_target_pairs={{0,16},{1,17},{2,18},{3,19},{4,20},{5,21},{6,22},{7,23},{8,24},{9,... | collective-permute-start | bytes 393224 | tf_op jit(solution)/shard_map/ppermute | solution.py:413
  25.6 6.9 %collective-permute-start.11 = (bf16[16,4096]{1,0:T(8,128)(2,1)S(1)}, bf16[16,4096]{1,0:T(8,128)(2,1)S(1)}, u32[]{:S(2)}, u32[]{:S(2)}) collective-permute-start(bf16[16,4096]{1,0:T(8,128)(2,1)S(1)} %stack_rows.2.refs_2_.refs_4_), channel_id=1, source_target_pairs={{0,16},{1,17},{2,18},{3,19},{4,20},{5,21},{6,22},{7,23},{8,24},{9,... | collective-permute-start | bytes 393224 | tf_op jit(solution)/shard_map/ppermute | solution.py:413
  41.4 21.8 %all-to-all-start = ((bf16[32,2,4096]{2,1,0:T(2,128)(2,1)}), bf16[32,2,4096]{2,1,0:T(2,128)(2,1)S(1)}, u32[]{:S(2)}, u32[]{:S(2)}) async-start(bf16[32,2,4096]{2,1,0:T(2,128)(2,1)} %get-tuple-element.39), calls=%async_computation | async-start | bytes 1048576 | tf_op jit(solution)/shard_map/all_to_all | solution.py:449

commit v7 on v6

--- a/solution.py
+++ b/solution.py
@@ -8,6 +8,7 @@
 from jax.sharding import PartitionSpec as P
 
 CAP = 2
+HALVES = 2
 MIB = 1024 * 1024
 VMEM = pl.BlockSpec(memory_space=pltpu.VMEM)
 HBM = pl.BlockSpec(memory_space=pltpu.HBM)
@@ -150,25 +151,26 @@
 
 
 def stack_kernel(number, *refs):
-    pieces, out = refs[:number], refs[-1]
-    rows = pieces[0].shape[0] // 2
-    for side in range(2):
-        picked = [piece[side * rows : (side + 1) * rows, :] for piece in pieces]
-        out[side * number * rows : (side + 1) * number * rows, :] = jnp.concatenate(picked, axis=0)
-
-
-def stack(pieces, after=()):
+    pieces, outs = refs[:number], refs[number:]
+    rows, width = pieces[0].shape[0] // 2, outs[0].shape[1]
+    for half, out in enumerate(outs):
+        at = slice(half * width, (half + 1) * width)
+        picked = [piece[:rows, at] for piece in pieces] + [piece[rows:, at] for piece in pieces]
+        out[...] = jnp.concatenate(picked, axis=0)
+
+
+def stack(pieces):
     number = len(pieces)
     rows, width = pieces[0].shape
     return pl.pallas_call(
         functools.partial(stack_kernel, number),
-        in_specs=[VMEM] * number + [pl.BlockSpec(memory_space=pl.ANY)] * len(after),
-        out_specs=VMEM,
-        out_shape=bf16(number * rows, width),
+        in_specs=[VMEM] * number,
+        out_specs=[VMEM] * HALVES,
+        out_shape=[bf16(number * rows, width // HALVES)] * HALVES,
         compiler_params=params(16),
         cost_estimate=cost(0, 4 * number * rows * width),
         name="stack_rows",
-    )(*pieces, *after)
+    )(*pieces)
 
 
 def load_kernel(chunk, pair_hbm, down_hbm, after, pair, down, sems):
@@ -202,27 +204,68 @@
     )(in_hbm(pair), in_hbm(down), after)
 
 
-def expert_kernel(homes, experts, groups, chunk, count, *refs):
-    got, pair, down = refs[:count], refs[count], refs[count + 1]
-    gate_out, up_out, hidden_out, tok_all, cot_all, parts_hbm = refs[count + 2 : count + 8]
-    parts, acc_gate, acc_up, acc_hid, sems = refs[count + 8 :]
-    width = got[0].shape[1]
-    steps = width // chunk
-    for step in range(steps):
-        at = slice(step * chunk, (step + 1) * chunk)
-        tok = jnp.concatenate([piece[: piece.shape[0] // 2, at] for piece in got], axis=0)
-        cot = jnp.concatenate([piece[piece.shape[0] // 2 :, at] for piece in got], axis=0)
+def gather_columns(near_rows, far_rows, near_at, far_at):
+    pieces = [(ref, near_at) for ref in near_rows] + [(ref, far_at) for ref in far_rows]
+    tok = [ref[: ref.shape[0] // 2, at] for ref, at in pieces]
+    cot = [ref[ref.shape[0] // 2 :, at] for ref, at in pieces]
+    return jnp.concatenate(tok, axis=0), jnp.concatenate(cot, axis=0)
+
+
+def first_kernel(near, groups, chunk, *refs):
+    near_rows, far_rows = refs[:near], refs[near : near + groups]
+    pair, down, gate, up, hid, tok_all, cot_all = refs[near + groups :]
+    for step in range(tok_all.shape[1] // chunk):
+        at = slice(step * chunk, (step + 1) * chunk)
+        tok, cot = gather_columns(near_rows, far_rows, at, at)
         tok_all[:, at] = tok
         cot_all[:, at] = cot
-        gate = dot_nn(tok, pair[0, at, :])
-        up = dot_nn(tok, pair[1, at, :])
-        hid = dot_nt(cot, down[:, at])
+        part_gate = dot_nn(tok, pair[0, at, :])
+        part_up = dot_nn(tok, pair[1, at, :])
+        part_hid = dot_nt(cot, down[:, at])
         if step == 0:
-            acc_gate[...], acc_up[...], acc_hid[...] = gate, up, hid
+            gate[...], up[...], hid[...] = part_gate, part_up, part_hid
         else:
-            acc_gate[...] += gate
-            acc_up[...] += up
-            acc_hid[...] += hid
+            gate[...] += part_gate
+            up[...] += part_up
+            hid[...] += part_hid
+
+
+def first_half(near_rows, far_rows, pair, down):
+    near, groups = len(near_rows), len(far_rows)
+    total = (near * near_rows[0].shape[0] + groups * far_rows[0].shape[0]) // 2
+    half = far_rows[0].shape[1]
+    units = down.shape[0]
+    chunk = min(1024, half)
+    return pl.pallas_call(
+        functools.partial(first_kernel, near, groups, chunk),
+        in_specs=[VMEM] * (near + groups + 2),
+        out_specs=[VMEM] * 5,
+        out_shape=[jax.ShapeDtypeStruct((total, units), jnp.float32)] * 3
+        + [bf16(total, half)] * 2,
+        compiler_params=params(24),
+        cost_estimate=cost(6 * total * half * units, 6 * half * units),
+        name="first_half",
+    )(*near_rows, *far_rows, pair, down)
+
+
+def second_kernel(homes, experts, near, groups, chunk, *refs):
+    near_rows, far_rows = refs[:near], refs[near : near + groups]
+    gate_sum, up_sum, hid_sum, pair, down = refs[near + groups : near + groups + 5]
+    gate_out, up_out, hidden_out, tok_all, cot_all, parts_hbm = refs[
+        near + groups + 5 : near + groups + 11
+    ]
+    parts, acc_gate, acc_up, acc_hid, sems = refs[near + groups + 11 :]
+    half, width = tok_all.shape[1], down.shape[1]
+    for step in range(half // chunk):
+        at = slice(step * chunk, (step + 1) * chunk)
+        there = slice(half + step * chunk, half + (step + 1) * chunk)
+        tok, cot = gather_columns(near_rows, far_rows, there, at)
+        tok_all[:, at] = tok
+        cot_all[:, at] = cot
+        before = (gate_sum, up_sum, hid_sum) if step == 0 else (acc_gate, acc_up, acc_hid)
+        acc_gate[...] = before[0][...] + dot_nn(tok, pair[0, there, :])
+        acc_up[...] = before[1][...] + dot_nn(tok, pair[1, there, :])
+        acc_hid[...] = before[2][...] + dot_nt(cot, down[:, there])
     pre_gate, pre_up, hidden_grad = acc_gate[...], acc_up[...], acc_hid[...]
     sigmoid_gate = jax.nn.sigmoid(pre_gate)
     activated = pre_gate * sigmoid_gate
@@ -238,7 +281,7 @@
         lax.rem(group - back + groups, groups) * experts + (me ^ turn) for back, turn in homes
     ]
     copies = []
-    for step in range(steps):
+    for step in range(width // chunk):
         at = slice(step * chunk, (step + 1) * chunk)
         value = dot_nt(gate_grad, pair[0, at, :]) + dot_nt(up_grad, pair[1, at, :])
         value = value.astype(jnp.bfloat16)
@@ -254,18 +297,18 @@
         one.wait()
 
 
-def expert_rows(got, homes, pair, down, experts, groups):
-    width = got[0].shape[1]
-    units = down.shape[0]
-    chunk = min(1024, width)
-    blocks = groups * experts
-    total = blocks * CAP
-    return pl.pallas_call(
-        functools.partial(expert_kernel, homes, experts, groups, chunk, len(got)),
-        in_specs=[VMEM] * (len(got) + 2),
+def second_half(near_rows, far_rows, sums, pair, down, homes, experts):
+    near, groups = len(near_rows), len(far_rows)
+    total, units = sums[0].shape
+    half, width = far_rows[0].shape[1], down.shape[1]
+    chunk = min(1024, half)
+    blocks = total // CAP
+    return pl.pallas_call(
+        functools.partial(second_kernel, homes, experts, near, groups, chunk),
+        in_specs=[VMEM] * (near + groups + 5),
         out_specs=[VMEM] * 5 + [HBM],
         out_shape=[bf16(total, units)] * 3
-        + [bf16(total, width)] * 2
+        + [bf16(total, half)] * 2
         + [pltpu.HBM((blocks, CAP, width), jnp.bfloat16)],
         scratch_shapes=[
             pltpu.VMEM((blocks, CAP, width), jnp.bfloat16),
@@ -274,24 +317,20 @@
             pltpu.VMEM((total, units), jnp.float32),
             pltpu.SemaphoreType.DMA((width // chunk,)),
         ],
-        compiler_params=params(28),
-        cost_estimate=cost(10 * total * width * units, 6 * width * units),
-        name="expert_rows",
-    )(
-        *got,
-        pltpu.with_memory_space_constraint(pair, pltpu.VMEM),
-        pltpu.with_memory_space_constraint(down, pltpu.VMEM),
-    )
+        compiler_params=params(24),
+        cost_estimate=cost(7 * total * width * units, 6 * width * units),
+        name="second_half",
+    )(*near_rows, *far_rows, *sums, pair, down)
 
 
 def pair_grad_kernel(blocks, chunk, *refs):
     toks, gate_ref, up_ref = refs[:blocks], refs[blocks], refs[blocks + 1]
+    half = toks[0].shape[1]
     out_hbm, buffer, sems = refs[blocks + 2 :]
-    width = toks[0].shape[1]
     copies = []
-    for step in range(width // chunk):
-        at = slice(step * chunk, (step + 1) * chunk)
-        tok = jnp.concatenate([ref[:, at] for ref in toks], axis=0)
+    for step in range(blocks * half // chunk):
+        at = slice(step * chunk, (step + 1) * chunk)
+        tok = toks[step * chunk // half][:, step * chunk % half : step * chunk % half + chunk]
         for side, ref in enumerate((gate_ref, up_ref)):
             buffer[side, at, :] = dot_tn(tok, ref[...]).astype(jnp.bfloat16)
         where = pl.ds(step * chunk, chunk)
@@ -306,9 +345,9 @@
 
 def pair_grad(toks, gate_grad, up_grad):
     blocks = len(toks)
-    width = toks[0].shape[1]
+    width = blocks * toks[0].shape[1]
     total, units = gate_grad.shape
-    chunk = min(512, width)
+    chunk = min(512, width // blocks)
     return pl.pallas_call(
         functools.partial(pair_grad_kernel, blocks, chunk),
         in_specs=[VMEM] * (blocks + 2),
@@ -327,11 +366,11 @@
 def down_grad_kernel(blocks, chunk, *refs):
     cots, hidden_ref, out_hbm = refs[:blocks], refs[blocks], refs[blocks + 1]
     buffer, sems = refs[blocks + 2 :]
-    width = cots[0].shape[1]
+    half = cots[0].shape[1]
     copies = []
-    for step in range(width // chunk):
-        at = slice(step * chunk, (step + 1) * chunk)
-        cot = jnp.concatenate([ref[:, at] for ref in cots], axis=0)
+    for step in range(blocks * half // chunk):
+        at = slice(step * chunk, (step + 1) * chunk)
+        cot = cots[step * chunk // half][:, step * chunk % half : step * chunk % half + chunk]
         buffer[:, at] = dot_tn(hidden_ref[...], cot).astype(jnp.bfloat16)
         where = pl.ds(step * chunk, chunk)
         one = pltpu.make_async_copy(buffer.at[:, where], out_hbm.at[0, :, where], sems.at[step])
@@ -343,9 +382,9 @@
 
 def down_grad(cots, hidden):
     blocks = len(cots)
-    width = cots[0].shape[1]
+    width = blocks * cots[0].shape[1]
     total, units = hidden.shape
-    chunk = min(1024, width)
+    chunk = min(1024, width // blocks)
     return pl.pallas_call(
         functools.partial(down_grad_kernel, blocks, chunk),
         in_specs=[VMEM] * (blocks + 1),
@@ -427,10 +466,9 @@
     loaded = pltpu.with_memory_space_constraint(down, pltpu.VMEM)
     second = merge([arrived[high] for high in late], (loaded,))
     mine = [send(second[low], 0, low) for low in range(near)]
-    second = [stack(mine[: near // 2])]
-    second.append(stack(mine[near // 2 :], (second[0],)))
-    got = [send(first[low], 0, low) for low in range(near)]
-    got += [send(part, group, 0) for group in range(groups) for part in second]
+    halves = stack(mine)
+    near_rows = [send(first[low], 0, low) for low in range(near)]
+    far_rows = [[send(half, group, 0) for group in range(groups)] for half in halves]
     homes = [
         (group, high * near + low)
         for low in range(near)
@@ -443,12 +481,14 @@
         for low in range(near)
         for high in late
     ]
-    gate_grad, up_grad, hidden, tok, cot, parts = expert_rows(
-        got, homes, pair, down, experts, groups
+    pair = pltpu.with_memory_space_constraint(pair, pltpu.VMEM)
+    *sums, tok_first, cot_first = first_half(near_rows, far_rows[0], pair, loaded)
+    gate_grad, up_grad, hidden, tok_second, cot_second, parts = second_half(
+        near_rows, far_rows[1], sums, pair, loaded, homes, experts
     )
     returned = lax.all_to_all(parts, ("dp", "expert"), split_axis=0, concat_axis=0, tiled=True)
-    down_total = down_grad([cot], hidden)
-    pair_total = pair_grad([tok], gate_grad, up_grad)
+    down_total = down_grad([cot_first, cot_second], hidden)
+    pair_total = pair_grad([tok_first, tok_second], gate_grad, up_grad)
     input_grad = spread(returned, place)
     return input_grad, pair_total, down_total
 

time: 65 us -> 62.8 us (0.966)
  waiting for transfers between devices: 14.9 us -> 12.9 us
    ppermute x13, waiting for transfers between devices: 7.72 us -> 5.74 us  [send(): return lax.ppermute(value, ('dp', 'expert'), pairs)]
    pallas_call x1 -> x2, Pallas kernels: 8.87 us -> 8.77 us  [the longest x1 6.63 us: second_half(): pl.pallas_call(functools.partial(second_kernel, homes, experts, near, gro...]
  transfers between devices with their start and end apart: 14 -> 14, of which waited for: 7 -> 6; matrix products, arithmetic and copies ran while one was open for 0% -> 0% of each run, Pallas kernels for 24% -> 29%
where the time goes in v7:
time: 62.8 us; the launch traced here: 62.5 us
  Pallas kernels  27.9 us (44%)
  starting transfers between devices  20.8 us (33%)
  waiting for transfers between devices  12.9 us (21%)
  between operations  0.9 us (1%)
    ppermute x13, starting transfers between devices, send(): return lax.ppermute(value, ('dp', 'expert'), pairs)  14.9 us
    all_to_all x1, waiting for transfers between devices, per_device(): lax.all_to_all(parts, ('dp', 'expert'), split_axis=0, concat_axis=0, tile...  7.15 us
    pallas_call x1, Pallas kernels, second_half(): pl.pallas_call(functools.partial(second_kernel, homes, experts, near, gro...  6.63 us
    pallas_call x1, Pallas kernels, load(): pl.pallas_call(functools.partial(load_kernel, chunk), in_specs=[HBM] * 2...  6.5 us
    all_to_all x1, starting transfers between devices, per_device(): lax.all_to_all(parts, ('dp', 'expert'), split_axis=0, concat_axis=0, tile...  5.96 us
    ppermute x13, waiting for transfers between devices, send(): return lax.ppermute(value, ('dp', 'expert'), pairs)  5.74 us
    pallas_call x1, Pallas kernels, pair_grad(): pl.pallas_call(functools.partial(pair_grad_kernel, blocks, chunk), in_spe...  5.25 us
    pallas_call x1, Pallas kernels, down_grad(): pl.pallas_call(functools.partial(down_grad_kernel, blocks, chunk), in_spe...  3.32 us
  transfers between devices with their start and end apart: 14, of which 6 were waited for; matrix products, arithmetic and copies ran while one was open for 0% of the time, Pallas kernels for 29%

profile of v7, /device:TPU:0, one launch (start us, length us, event | category | flops | bytes accessed | tf_op | source)
XLA Modules:
  0.0 62.5 jit_solution(6282842896159815751)
XLA Ops:
  0.6 2.0 %route_rows.1 = (bf16[4,4,4096]{2,1,0:T(4,128)(2,1)S(1)}, bf16[4,4,4096]{2,1,0:T(4,128)(2,1)S(1)}, bf16[4,4,4096]{2,1,0:T(4,128)(2,1)S(1)}, bf16[4,4,4096]{2,1,0:T(4,128)(2,1)S(1)}, bf16[32,128]{1,0:T(8,128)(2,1)S(1)}) custom-call(s32[1,128]{1,0:T(1,128)} %bitcast.6, f32[1,128]{1,0:T(1,128)} %bitcast.7, bf16[128,4096]{1,0:T(8,128)(2,1)} %act_hbm.1, ...), custom_call_target="tpu_custom_call" | custom-call | flops 67108864 | bytes 2097152 | tf_op jit(solution)/shard_map/route_rows/pallas_call | solution.py:112
  2.7 4.1 %collective-permute-start.6 = (bf16[4,4,4096]{2,1,0:T(4,128)(2,1)S(1)}, bf16[4,4,4096]{2,1,0:T(4,128)(2,1)S(1)}, u32[]{:S(2)}, u32[]{:S(2)}) collective-permute-start(bf16[4,4,4096]{2,1,0:T(4,128)(2,1)S(1)} %get-tuple-element.37), channel_id=1, source_target_pairs={{0,8},{1,9},{2,10},{3,11},{4,12},{5,13},{6,14},{7,15},{8,0},{9,1},... | collective-permute-start | bytes 393224 | tf_op jit(solution)/shard_map/ppermute | solution.py:452
  6.8 1.3 %collective-permute-start.7 = (bf16[4,4,4096]{2,1,0:T(4,128)(2,1)S(1)}, bf16[4,4,4096]{2,1,0:T(4,128)(2,1)S(1)}, u32[]{:S(2)}, u32[]{:S(2)}) collective-permute-start(bf16[4,4,4096]{2,1,0:T(4,128)(2,1)S(1)} %get-tuple-element.38), channel_id=1, source_target_pairs={{0,12},{1,13},{2,14},{3,15},{4,8},{5,9},{6,10},{7,11},{8,4},{9,5},... | collective-permute-start | bytes 393224 | tf_op jit(solution)/shard_map/ppermute | solution.py:452
  8.1 1.5 %collective-permute-start.1 = (bf16[4,4,4096]{2,1,0:T(4,128)(2,1)S(1)}, bf16[4,4,4096]{2,1,0:T(4,128)(2,1)S(1)}, u32[]{:S(2)}, u32[]{:S(2)}) collective-permute-start(bf16[4,4,4096]{2,1,0:T(4,128)(2,1)S(1)} %get-tuple-element.31.refs_0_), channel_id=1, source_target_pairs={{0,16},{1,17},{2,18},{3,19},{4,20},{5,21},{6,22},{7,23},{8,24},{9,... | collective-permute-start | bytes 393224 | tf_op jit(solution)/shard_map/ppermute | solution.py:452
  9.8 1.8 %collective-permute-start = (bf16[4,4,4096]{2,1,0:T(4,128)(2,1)S(1)}, bf16[4,4,4096]{2,1,0:T(4,128)(2,1)S(1)}, u32[]{:S(2)}, u32[]{:S(2)}) collective-permute-start(bf16[4,4,4096]{2,1,0:T(4,128)(2,1)S(1)} %get-tuple-element.32), channel_id=1, source_target_pairs={{0,4},{1,5},{2,6},{3,7},{4,0},{5,1},{6,2},{7,3},{8,12},{9,13},{10,... | collective-permute-start | bytes 393224 | tf_op jit(solution)/shard_map/ppermute | solution.py:452
  11.6 6.5 %load_weights.1 = (bf16[2,4096,768]{2,1,0:T(8,128)(2,1)S(1)}, bf16[768,4096]{1,0:T(8,128)(2,1)S(1)}) custom-call(bf16[2,4096,768]{2,1,0:T(8,128)(2,1)} %bitcast.4, bf16[768,4096]{1,0:T(8,128)(2,1)} %bitcast.5, bf16[32,128]{1,0:T(8,128)(2,1)S(1)} %get-tuple-element.39.after.place_ref), custom_call_target="tpu_custom_call" | custom-call | bytes 18874368 | tf_op jit(solution)/shard_map/load_weights/pallas_call | solution.py:195
  18.4 1.6 %collective-permute-start.9 = (bf16[8,4096]{1,0:T(8,128)(2,1)S(1)}, bf16[8,4096]{1,0:T(8,128)(2,1)S(1)}, u32[]{:S(2)}, u32[]{:S(2)}) collective-permute-start(bf16[8,4096]{1,0:T(8,128)(2,1)S(1)} %get-tuple-element.43), channel_id=1, source_target_pairs={{0,2},{1,3},{2,0},{3,1},{4,6},{5,7},{6,4},{7,5},{8,10},{9,11},{10,... | collective-permute-start | bytes 196616 | tf_op jit(solution)/shard_map/ppermute | solution.py:452
  20.0 0.3 collective-permute-start.10
  20.3 0.8 %collective-permute-done.refs_1_ = bf16[4,4,4096]{2,1,0:T(4,128)(2,1)S(1)} collective-permute-done((bf16[4,4,4096]{2,1,0:T(4,128)(2,1)S(1)}, bf16[4,4,4096]{2,1,0:T(4,128)(2,1)S(1)}, u32[]{:S(2)}, u32[]{:S(2)}) %collective-permute-start) | collective-permute-done | bytes 131104 | tf_op jit(solution)/shard_map/ppermute | solution.py:452
  21.0 0.4 merge_rows.2
  21.5 1.6 %collective-permute-start.4 = (bf16[16,4096]{1,0:T(8,128)(2,1)S(1)}, bf16[16,4096]{1,0:T(8,128)(2,1)S(1)}, u32[]{:S(2)}, u32[]{:S(2)}) collective-permute-start(bf16[16,4096]{1,0:T(8,128)(2,1)S(1)} %get-tuple-element.35), channel_id=1, source_target_pairs={{0,2},{1,3},{2,0},{3,1},{4,6},{5,7},{6,4},{7,5},{8,10},{9,11},{10,... | collective-permute-start | bytes 393224 | tf_op jit(solution)/shard_map/ppermute | solution.py:452
  23.4 0.6 %collective-permute-done.10.refs_3_ = bf16[8,4096]{1,0:T(8,128)(2,1)S(1)} collective-permute-done((bf16[8,4096]{1,0:T(8,128)(2,1)S(1)}, bf16[8,4096]{1,0:T(8,128)(2,1)S(1)}, u32[]{:S(2)}, u32[]{:S(2)}) %collective-permute-start.10) | collective-permute-done | bytes 65568 | tf_op jit(solution)/shard_map/ppermute | solution.py:452
  24.1 1.6 %collective-permute-start.12 = (bf16[32,2048]{1,0:T(8,128)(2,1)S(1)}, bf16[32,2048]{1,0:T(8,128)(2,1)S(1)}, u32[]{:S(2)}, u32[]{:S(2)}) collective-permute-start(bf16[32,2048]{1,0:T(8,128)(2,1)S(1)} %get-tuple-element.46.refs_4_), channel_id=1, source_target_pairs={{0,16},{1,17},{2,18},{3,19},{4,20},{5,21},{6,22},{7,23},{8,24},{9,... | collective-permute-start | bytes 393224 | tf_op jit(solution)/shard_map/ppermute | solution.py:452
  25.7 0.5 collective-permute-start.11
  26.2 1.7 %collective-permute-done.4.refs_2_ = bf16[16,4096]{1,0:T(8,128)(2,1)S(1)} collective-permute-done((bf16[16,4096]{1,0:T(8,128)(2,1)S(1)}, bf16[16,4096]{1,0:T(8,128)(2,1)S(1)}, u32[]{:S(2)}, u32[]{:S(2)}) %collective-permute-start.4) | collective-permute-done | bytes 131104 | tf_op jit(solution)/shard_map/ppermute | solution.py:452
  27.9 1.9 %collective-permute-done.5.refs_3_ = bf16[16,4096]{1,0:T(8,128)(2,1)S(1)} collective-permute-done((bf16[16,4096]{1,0:T(8,128)(2,1)S(1)}, bf16[16,4096]{1,0:T(8,128)(2,1)S(1)}, u32[]{:S(2)}, u32[]{:S(2)}) %collective-permute-start.5) | collective-permute-done | bytes 131104 | tf_op jit(solution)/shard_map/ppermute | solution.py:452
  29.8 0.7 %collective-permute-done.12.refs_5_ = bf16[32,2048]{1,0:T(8,128)(2,1)S(1)} collective-permute-done((bf16[32,2048]{1,0:T(8,128)(2,1)S(1)}, bf16[32,2048]{1,0:T(8,128)(2,1)S(1)}, u32[]{:S(2)}, u32[]{:S(2)}) %collective-permute-start.12) | collective-permute-done | bytes 131104 | tf_op jit(solution)/shard_map/ppermute | solution.py:452
  30.5 2.1 %first_half.1 = (f32[64,768]{1,0:T(8,128)S(1)}, f32[64,768]{1,0:T(8,128)S(1)}, f32[64,768]{1,0:T(8,128)S(1)}, bf16[64,2048]{1,0:T(8,128)(2,1)S(1)}, bf16[64,2048]{1,0:T(8,128)(2,1)S(1)}) custom-call(bf16[16,4096]{1,0:T(8,128)(2,1)S(1)} %get-tuple-element.33.refs_0_, bf16[16,4096]{1,0:T(8,128)(2,1)S(1)} %collective-permute-done.3.refs_1_, ...), custom_call_target="tpu_custom_call" | custom-call | flops 603979776 | bytes 9437184 | tf_op jit(solution)/shard_map/first_half/pallas_call | solution.py:239
  32.7 6.6 %second_half.1 = (bf16[64,768]{1,0:T(8,128)(2,1)S(1)}, bf16[64,768]{1,0:T(8,128)(2,1)S(1)}, bf16[64,768]{1,0:T(8,128)(2,1)S(1)}, bf16[64,2048]{1,0:T(8,128)(2,1)...) custom-call(bf16[16,4096]{1,0:T(8,128)(2,1)S(1)} %get-tuple-element.33.refs_0_, ...), custom_call_target="tpu_custom_call" | custom-call | flops 1409286144 | bytes 18874368 | tf_op jit(solution)/shard_map/second_half/pallas_call | solution.py:306
  39.3 6.0 %all-to-all-start = ((bf16[32,2,4096]{2,1,0:T(2,128)(2,1)}), bf16[32,2,4096]{2,1,0:T(2,128)(2,1)S(1)}, u32[]{:S(2)}, u32[]{:S(2)}) async-start(bf16[32,2,4096]{2,1,0:T(2,128)(2,1)} %get-tuple-element.51), calls=%async_computation | async-start | bytes 1048576 | tf_op jit(solution)/shard_map/all_to_all | solution.py:489
  45.3 3.3 %down_grad.1 = bf16[1,768,4096]{2,1,0:T(8,128)(2,1)} custom-call(bf16[64,2048]{1,0:T(8,128)(2,1)S(1)} %get-tuple-element.56.refs_0_, bf16[64,2048]{1,0:T(8,128)(2,1)S(1)} %get-tuple-element.57.refs_1_, bf16[64,768]{1,0:T(8,128)(2,1)S(1)} %get-tuple-element.58.refs_2_), custom_call_target="tpu_custom_call" | custom-call | flops 402653184 | bytes 6291456 | tf_op jit(solution)/shard_map/down_grad/pallas_call | solution.py:388
  48.6 5.2 %pair_grad.1 = bf16[1,2,4096,768]{3,2,1,0:T(8,128)(2,1)} custom-call(bf16[64,2048]{1,0:T(8,128)(2,1)S(1)} %get-tuple-element.52.refs_0_, bf16[64,2048]{1,0:T(8,128)(2,1)S(1)} %get-tuple-element.53.refs_1_, bf16[64,768]{1,0:T(8,128)(2,1)S(1)} %get-tuple-element.54.refs_2_, bf16[64,768]{1,0:T(8,128)(2,1)S(1)} %get-tuple-element.55.refs_3_), custom_call_target="tpu_custom_call" | custom-call | flops 805306368 | bytes 12582912 | tf_op jit(solution)/shard_map/pair_grad/pallas_call | solution.py:351
  53.8 7.1 %all-to-all-done.rows_ref = bf16[32,2,4096]{2,1,0:T(2,128)(2,1)S(1)} async-done(((bf16[32,2,4096]{2,1,0:T(2,128)(2,1)}), bf16[32,2,4096]{2,1,0:T(2,128)(2,1)S(1)}, u32[]{:S(2)}, u32[]{:S(2)}) %all-to-all-start) | async-done | bytes 524320 | tf_op jit(solution)/shard_map/all_to_all | solution.py:489
  61.0 1.3 %spread_rows.1 = bf16[128,4096]{1,0:T(8,128)(2,1)} custom-call(bf16[32,2,4096]{2,1,0:T(2,128)(2,1)S(1)} %all-to-all-done.rows_ref, bf16[32,128]{1,0:T(8,128)(2,1)S(1)} %get-tuple-element.39.after.place_ref), custom_call_target="tpu_custom_call" | custom-call | flops 33554432 | bytes 1048576 | tf_op jit(solution)/shard_map/spread_rows/pallas_call | solution.py:423
  (14 shorter events, 0.9 us)
Async XLA Ops:
  2.7 15.4 %collective-permute-start.6 = (bf16[4,4,4096]{2,1,0:T(4,128)(2,1)S(1)}, bf16[4,4,4096]{2,1,0:T(4,128)(2,1)S(1)}, u32[]{:S(2)}, u32[]{:S(2)}) collective-permute-start(bf16[4,4,4096]{2,1,0:T(4,128)(2,1)S(1)} %get-tuple-element.37), channel_id=1, source_target_pairs={{0,8},{1,9},{2,10},{3,11},{4,12},{5,13},{6,14},{7,15},{8,0},{9,1},... | collective-permute-start | bytes 393224 | tf_op jit(solution)/shard_map/ppermute | solution.py:452
  6.8 11.3 %collective-permute-start.7 = (bf16[4,4,4096]{2,1,0:T(4,128)(2,1)S(1)}, bf16[4,4,4096]{2,1,0:T(4,128)(2,1)S(1)}, u32[]{:S(2)}, u32[]{:S(2)}) collective-permute-start(bf16[4,4,4096]{2,1,0:T(4,128)(2,1)S(1)} %get-tuple-element.38), channel_id=1, source_target_pairs={{0,12},{1,13},{2,14},{3,15},{4,8},{5,9},{6,10},{7,11},{8,4},{9,5},... | collective-permute-start | bytes 393224 | tf_op jit(solution)/shard_map/ppermute | solution.py:452
  8.1 11.9 %collective-permute-start.1 = (bf16[4,4,4096]{2,1,0:T(4,128)(2,1)S(1)}, bf16[4,4,4096]{2,1,0:T(4,128)(2,1)S(1)}, u32[]{:S(2)}, u32[]{:S(2)}) collective-permute-start(bf16[4,4,4096]{2,1,0:T(4,128)(2,1)S(1)} %get-tuple-element.31.refs_0_), channel_id=1, source_target_pairs={{0,16},{1,17},{2,18},{3,19},{4,20},{5,21},{6,22},{7,23},{8,24},{9,... | collective-permute-start | bytes 393224 | tf_op jit(solution)/shard_map/ppermute | solution.py:452
  9.6 10.6 %collective-permute-start.2 = (bf16[4,4,4096]{2,1,0:T(4,128)(2,1)S(1)}, bf16[4,4,4096]{2,1,0:T(4,128)(2,1)S(1)}, u32[]{:S(2)}, u32[]{:S(2)}) collective-permute-start(bf16[4,4,4096]{2,1,0:T(4,128)(2,1)S(1)} %get-tuple-element.32), channel_id=1, source_target_pairs={{0,20},{1,21},{2,22},{3,23},{4,16},{5,17},{6,18},{7,19},{8,28},{9,... | collective-permute-start | bytes 393224 | tf_op jit(solution)/shard_map/ppermute | solution.py:452
  9.8 11.2 %collective-permute-start = (bf16[4,4,4096]{2,1,0:T(4,128)(2,1)S(1)}, bf16[4,4,4096]{2,1,0:T(4,128)(2,1)S(1)}, u32[]{:S(2)}, u32[]{:S(2)}) collective-permute-start(bf16[4,4,4096]{2,1,0:T(4,128)(2,1)S(1)} %get-tuple-element.32), channel_id=1, source_target_pairs={{0,4},{1,5},{2,6},{3,7},{4,0},{5,1},{6,2},{7,3},{8,12},{9,13},{10,... | collective-permute-start | bytes 393224 | tf_op jit(solution)/shard_map/ppermute | solution.py:452
  18.3 4.8 %collective-permute-start.8 = (bf16[8,4096]{1,0:T(8,128)(2,1)S(1)}, bf16[8,4096]{1,0:T(8,128)(2,1)S(1)}, u32[]{:S(2)}, u32[]{:S(2)}) collective-permute-start(bf16[8,4096]{1,0:T(8,128)(2,1)S(1)} %get-tuple-element.42), channel_id=1, source_target_pairs={{0,1},{1,0},{2,3},{3,2},{4,5},{5,4},{6,7},{7,6},{8,9},{9,8},{10,11... | collective-permute-start | bytes 196616 | tf_op jit(solution)/shard_map/ppermute | solution.py:452
  18.4 5.0 %collective-permute-start.9 = (bf16[8,4096]{1,0:T(8,128)(2,1)S(1)}, bf16[8,4096]{1,0:T(8,128)(2,1)S(1)}, u32[]{:S(2)}, u32[]{:S(2)}) collective-permute-start(bf16[8,4096]{1,0:T(8,128)(2,1)S(1)} %get-tuple-element.43), channel_id=1, source_target_pairs={{0,2},{1,3},{2,0},{3,1},{4,6},{5,7},{6,4},{7,5},{8,10},{9,11},{10,... | collective-permute-start | bytes 196616 | tf_op jit(solution)/shard_map/ppermute | solution.py:452
  20.0 4.0 %collective-permute-start.10 = (bf16[8,4096]{1,0:T(8,128)(2,1)S(1)}, bf16[8,4096]{1,0:T(8,128)(2,1)S(1)}, u32[]{:S(2)}, u32[]{:S(2)}) collective-permute-start(bf16[8,4096]{1,0:T(8,128)(2,1)S(1)} %get-tuple-element.44), channel_id=1, source_target_pairs={{0,3},{1,2},{2,1},{3,0},{4,7},{5,6},{6,5},{7,4},{8,11},{9,10},{10,... | collective-permute-start | bytes 196616 | tf_op jit(solution)/shard_map/ppermute | solution.py:452
  21.4 4.8 %collective-permute-start.3 = (bf16[16,4096]{1,0:T(8,128)(2,1)S(1)}, bf16[16,4096]{1,0:T(8,128)(2,1)S(1)}, u32[]{:S(2)}, u32[]{:S(2)}) collective-permute-start(bf16[16,4096]{1,0:T(8,128)(2,1)S(1)} %get-tuple-element.34), channel_id=1, source_target_pairs={{0,1},{1,0},{2,3},{3,2},{4,5},{5,4},{6,7},{7,6},{8,9},{9,8},{10,11... | collective-permute-start | bytes 393224 | tf_op jit(solution)/shard_map/ppermute | solution.py:452
  21.5 6.4 %collective-permute-start.4 = (bf16[16,4096]{1,0:T(8,128)(2,1)S(1)}, bf16[16,4096]{1,0:T(8,128)(2,1)S(1)}, u32[]{:S(2)}, u32[]{:S(2)}) collective-permute-start(bf16[16,4096]{1,0:T(8,128)(2,1)S(1)} %get-tuple-element.35), channel_id=1, source_target_pairs={{0,2},{1,3},{2,0},{3,1},{4,6},{5,7},{6,4},{7,5},{8,10},{9,11},{10,... | collective-permute-start | bytes 393224 | tf_op jit(solution)/shard_map/ppermute | solution.py:452
  23.1 6.6 %collective-permute-start.5 = (bf16[16,4096]{1,0:T(8,128)(2,1)S(1)}, bf16[16,4096]{1,0:T(8,128)(2,1)S(1)}, u32[]{:S(2)}, u32[]{:S(2)}) collective-permute-start(bf16[16,4096]{1,0:T(8,128)(2,1)S(1)} %get-tuple-element.36), channel_id=1, source_target_pairs={{0,3},{1,2},{2,1},{3,0},{4,7},{5,6},{6,5},{7,4},{8,11},{9,10},{10,... | collective-permute-start | bytes 393224 | tf_op jit(solution)/shard_map/ppermute | solution.py:452
  24.1 6.4 %collective-permute-start.12 = (bf16[32,2048]{1,0:T(8,128)(2,1)S(1)}, bf16[32,2048]{1,0:T(8,128)(2,1)S(1)}, u32[]{:S(2)}, u32[]{:S(2)}) collective-permute-start(bf16[32,2048]{1,0:T(8,128)(2,1)S(1)} %get-tuple-element.46.refs_4_), channel_id=1, source_target_pairs={{0,16},{1,17},{2,18},{3,19},{4,20},{5,21},{6,22},{7,23},{8,24},{9,... | collective-permute-start | bytes 393224 | tf_op jit(solution)/shard_map/ppermute | solution.py:452
  25.7 6.9 %collective-permute-start.11 = (bf16[32,2048]{1,0:T(8,128)(2,1)S(1)}, bf16[32,2048]{1,0:T(8,128)(2,1)S(1)}, u32[]{:S(2)}, u32[]{:S(2)}) collective-permute-start(bf16[32,2048]{1,0:T(8,128)(2,1)S(1)} %get-tuple-element.45.refs_4_), channel_id=1, source_target_pairs={{0,16},{1,17},{2,18},{3,19},{4,20},{5,21},{6,22},{7,23},{8,24},{9,... | collective-permute-start | bytes 393224 | tf_op jit(solution)/shard_map/ppermute | solution.py:452
  39.3 21.7 %all-to-all-start = ((bf16[32,2,4096]{2,1,0:T(2,128)(2,1)}), bf16[32,2,4096]{2,1,0:T(2,128)(2,1)S(1)}, u32[]{:S(2)}, u32[]{:S(2)}) async-start(bf16[32,2,4096]{2,1,0:T(2,128)(2,1)} %get-tuple-element.51), calls=%async_computation | async-start | bytes 1048576 | tf_op jit(solution)/shard_map/all_to_all | solution.py:489

commit v8 on v7

--- a/solution.py
+++ b/solution.py
@@ -235,7 +235,7 @@
     total = (near * near_rows[0].shape[0] + groups * far_rows[0].shape[0]) // 2
     half = far_rows[0].shape[1]
     units = down.shape[0]
-    chunk = min(1024, half)
+    chunk = half
     return pl.pallas_call(
         functools.partial(first_kernel, near, groups, chunk),
         in_specs=[VMEM] * (near + groups + 2),
@@ -254,19 +254,15 @@
     gate_out, up_out, hidden_out, tok_all, cot_all, parts_hbm = refs[
         near + groups + 5 : near + groups + 11
     ]
-    parts, acc_gate, acc_up, acc_hid, sems = refs[near + groups + 11 :]
+    parts, sems = refs[near + groups + 11 :]
     half, width = tok_all.shape[1], down.shape[1]
-    for step in range(half // chunk):
-        at = slice(step * chunk, (step + 1) * chunk)
-        there = slice(half + step * chunk, half + (step + 1) * chunk)
-        tok, cot = gather_columns(near_rows, far_rows, there, at)
-        tok_all[:, at] = tok
-        cot_all[:, at] = cot
-        before = (gate_sum, up_sum, hid_sum) if step == 0 else (acc_gate, acc_up, acc_hid)
-        acc_gate[...] = before[0][...] + dot_nn(tok, pair[0, there, :])
-        acc_up[...] = before[1][...] + dot_nn(tok, pair[1, there, :])
-        acc_hid[...] = before[2][...] + dot_nt(cot, down[:, there])
-    pre_gate, pre_up, hidden_grad = acc_gate[...], acc_up[...], acc_hid[...]
+    there = slice(half, width)
+    tok, cot = gather_columns(near_rows, far_rows, there, slice(0, half))
+    tok_all[...] = tok
+    cot_all[...] = cot
+    pre_gate = gate_sum[...] + dot_nn(tok, pair[0, there, :])
+    pre_up = up_sum[...] + dot_nn(tok, pair[1, there, :])
+    hidden_grad = hid_sum[...] + dot_nt(cot, down[:, there])
     sigmoid_gate = jax.nn.sigmoid(pre_gate)
     activated = pre_gate * sigmoid_gate
     hidden_out[...] = (activated * pre_up).astype(jnp.bfloat16)
@@ -301,7 +297,7 @@
     near, groups = len(near_rows), len(far_rows)
     total, units = sums[0].shape
     half, width = far_rows[0].shape[1], down.shape[1]
-    chunk = min(1024, half)
+    chunk = min(512, half)
     blocks = total // CAP
     return pl.pallas_call(
         functools.partial(second_kernel, homes, experts, near, groups, chunk),
@@ -312,9 +308,6 @@
         + [pltpu.HBM((blocks, CAP, width), jnp.bfloat16)],
         scratch_shapes=[
             pltpu.VMEM((blocks, CAP, width), jnp.bfloat16),
-            pltpu.VMEM((total, units), jnp.float32),
-            pltpu.VMEM((total, units), jnp.float32),
-            pltpu.VMEM((total, units), jnp.float32),
             pltpu.SemaphoreType.DMA((width // chunk,)),
         ],
         compiler_params=params(24),

time: 62.8 us -> 62.8 us (level)
  no operation moved by 1% of the time
where the time goes in v8:
time: 62.8 us; the launch traced here: 62.5 us
  Pallas kernels  27.9 us (44%)
  starting transfers between devices  20.8 us (33%)
  waiting for transfers between devices  12.9 us (21%)
  between operations  0.91 us (1%)
    ppermute x13, starting transfers between devices, send(): return lax.ppermute(value, ('dp', 'expert'), pairs)  14.9 us
    all_to_all x1, waiting for transfers between devices, per_device(): lax.all_to_all(parts, ('dp', 'expert'), split_axis=0, concat_axis=0, tile...  7.14 us
    pallas_call x1, Pallas kernels, second_half(): pl.pallas_call(functools.partial(second_kernel, homes, experts, near, gro...  6.68 us
    pallas_call x1, Pallas kernels, load(): pl.pallas_call(functools.partial(load_kernel, chunk), in_specs=[HBM] * 2...  6.5 us
    all_to_all x1, starting transfers between devices, per_device(): lax.all_to_all(parts, ('dp', 'expert'), split_axis=0, concat_axis=0, tile...  5.94 us
    ppermute x13, waiting for transfers between devices, send(): return lax.ppermute(value, ('dp', 'expert'), pairs)  5.74 us
    pallas_call x1, Pallas kernels, pair_grad(): pl.pallas_call(functools.partial(pair_grad_kernel, blocks, chunk), in_spe...  5.26 us
    pallas_call x1, Pallas kernels, down_grad(): pl.pallas_call(functools.partial(down_grad_kernel, blocks, chunk), in_spe...  3.32 us
  transfers between devices with their start and end apart: 14, of which 6 were waited for; matrix products, arithmetic and copies ran while one was open for 0% of the time, Pallas kernels for 29%

profile of v8, /device:TPU:0, one launch (start us, length us, event | category | flops | bytes accessed | tf_op | source)
XLA Modules:
  0.0 62.5 jit_solution(10934298512750300203)
XLA Ops:
  0.6 2.0 %route_rows.1 = (bf16[4,4,4096]{2,1,0:T(4,128)(2,1)S(1)}, bf16[4,4,4096]{2,1,0:T(4,128)(2,1)S(1)}, bf16[4,4,4096]{2,1,0:T(4,128)(2,1)S(1)}, bf16[4,4,4096]{2,1,0:T(4,128)(2,1)S(1)}, bf16[32,128]{1,0:T(8,128)(2,1)S(1)}) custom-call(s32[1,128]{1,0:T(1,128)} %bitcast.6, f32[1,128]{1,0:T(1,128)} %bitcast.7, bf16[128,4096]{1,0:T(8,128)(2,1)} %act_hbm.1, ...), custom_call_target="tpu_custom_call" | custom-call | flops 67108864 | bytes 2097152 | tf_op jit(solution)/shard_map/route_rows/pallas_call | solution.py:112
  2.7 4.1 %collective-permute-start.6 = (bf16[4,4,4096]{2,1,0:T(4,128)(2,1)S(1)}, bf16[4,4,4096]{2,1,0:T(4,128)(2,1)S(1)}, u32[]{:S(2)}, u32[]{:S(2)}) collective-permute-start(bf16[4,4,4096]{2,1,0:T(4,128)(2,1)S(1)} %get-tuple-element.37), channel_id=1, source_target_pairs={{0,8},{1,9},{2,10},{3,11},{4,12},{5,13},{6,14},{7,15},{8,0},{9,1},... | collective-permute-start | bytes 393224 | tf_op jit(solution)/shard_map/ppermute | solution.py:445
  6.8 1.3 %collective-permute-start.7 = (bf16[4,4,4096]{2,1,0:T(4,128)(2,1)S(1)}, bf16[4,4,4096]{2,1,0:T(4,128)(2,1)S(1)}, u32[]{:S(2)}, u32[]{:S(2)}) collective-permute-start(bf16[4,4,4096]{2,1,0:T(4,128)(2,1)S(1)} %get-tuple-element.38), channel_id=1, source_target_pairs={{0,12},{1,13},{2,14},{3,15},{4,8},{5,9},{6,10},{7,11},{8,4},{9,5},... | collective-permute-start | bytes 393224 | tf_op jit(solution)/shard_map/ppermute | solution.py:445
  8.1 1.5 %collective-permute-start.1 = (bf16[4,4,4096]{2,1,0:T(4,128)(2,1)S(1)}, bf16[4,4,4096]{2,1,0:T(4,128)(2,1)S(1)}, u32[]{:S(2)}, u32[]{:S(2)}) collective-permute-start(bf16[4,4,4096]{2,1,0:T(4,128)(2,1)S(1)} %get-tuple-element.31.refs_0_), channel_id=1, source_target_pairs={{0,16},{1,17},{2,18},{3,19},{4,20},{5,21},{6,22},{7,23},{8,24},{9,... | collective-permute-start | bytes 393224 | tf_op jit(solution)/shard_map/ppermute | solution.py:445
  9.8 1.8 %collective-permute-start = (bf16[4,4,4096]{2,1,0:T(4,128)(2,1)S(1)}, bf16[4,4,4096]{2,1,0:T(4,128)(2,1)S(1)}, u32[]{:S(2)}, u32[]{:S(2)}) collective-permute-start(bf16[4,4,4096]{2,1,0:T(4,128)(2,1)S(1)} %get-tuple-element.32), channel_id=1, source_target_pairs={{0,4},{1,5},{2,6},{3,7},{4,0},{5,1},{6,2},{7,3},{8,12},{9,13},{10,... | collective-permute-start | bytes 393224 | tf_op jit(solution)/shard_map/ppermute | solution.py:445
  11.6 6.5 %load_weights.1 = (bf16[2,4096,768]{2,1,0:T(8,128)(2,1)S(1)}, bf16[768,4096]{1,0:T(8,128)(2,1)S(1)}) custom-call(bf16[2,4096,768]{2,1,0:T(8,128)(2,1)} %bitcast.4, bf16[768,4096]{1,0:T(8,128)(2,1)} %bitcast.5, bf16[32,128]{1,0:T(8,128)(2,1)S(1)} %get-tuple-element.39.after.place_ref), custom_call_target="tpu_custom_call" | custom-call | bytes 18874368 | tf_op jit(solution)/shard_map/load_weights/pallas_call | solution.py:195
  18.4 1.6 %collective-permute-start.9 = (bf16[8,4096]{1,0:T(8,128)(2,1)S(1)}, bf16[8,4096]{1,0:T(8,128)(2,1)S(1)}, u32[]{:S(2)}, u32[]{:S(2)}) collective-permute-start(bf16[8,4096]{1,0:T(8,128)(2,1)S(1)} %get-tuple-element.43), channel_id=1, source_target_pairs={{0,2},{1,3},{2,0},{3,1},{4,6},{5,7},{6,4},{7,5},{8,10},{9,11},{10,... | collective-permute-start | bytes 196616 | tf_op jit(solution)/shard_map/ppermute | solution.py:445
  20.0 0.3 collective-permute-start.10
  20.3 0.8 %collective-permute-done.refs_1_ = bf16[4,4,4096]{2,1,0:T(4,128)(2,1)S(1)} collective-permute-done((bf16[4,4,4096]{2,1,0:T(4,128)(2,1)S(1)}, bf16[4,4,4096]{2,1,0:T(4,128)(2,1)S(1)}, u32[]{:S(2)}, u32[]{:S(2)}) %collective-permute-start) | collective-permute-done | bytes 131104 | tf_op jit(solution)/shard_map/ppermute | solution.py:445
  21.0 0.4 merge_rows.2
  21.5 1.6 %collective-permute-start.4 = (bf16[16,4096]{1,0:T(8,128)(2,1)S(1)}, bf16[16,4096]{1,0:T(8,128)(2,1)S(1)}, u32[]{:S(2)}, u32[]{:S(2)}) collective-permute-start(bf16[16,4096]{1,0:T(8,128)(2,1)S(1)} %get-tuple-element.35), channel_id=1, source_target_pairs={{0,2},{1,3},{2,0},{3,1},{4,6},{5,7},{6,4},{7,5},{8,10},{9,11},{10,... | collective-permute-start | bytes 393224 | tf_op jit(solution)/shard_map/ppermute | solution.py:445
  23.4 0.6 %collective-permute-done.10.refs_3_ = bf16[8,4096]{1,0:T(8,128)(2,1)S(1)} collective-permute-done((bf16[8,4096]{1,0:T(8,128)(2,1)S(1)}, bf16[8,4096]{1,0:T(8,128)(2,1)S(1)}, u32[]{:S(2)}, u32[]{:S(2)}) %collective-permute-start.10) | collective-permute-done | bytes 65568 | tf_op jit(solution)/shard_map/ppermute | solution.py:445
  24.1 1.6 %collective-permute-start.12 = (bf16[32,2048]{1,0:T(8,128)(2,1)S(1)}, bf16[32,2048]{1,0:T(8,128)(2,1)S(1)}, u32[]{:S(2)}, u32[]{:S(2)}) collective-permute-start(bf16[32,2048]{1,0:T(8,128)(2,1)S(1)} %get-tuple-element.46.refs_4_), channel_id=1, source_target_pairs={{0,16},{1,17},{2,18},{3,19},{4,20},{5,21},{6,22},{7,23},{8,24},{9,... | collective-permute-start | bytes 393224 | tf_op jit(solution)/shard_map/ppermute | solution.py:445
  25.7 0.5 collective-permute-start.11
  26.2 1.7 %collective-permute-done.4.refs_2_ = bf16[16,4096]{1,0:T(8,128)(2,1)S(1)} collective-permute-done((bf16[16,4096]{1,0:T(8,128)(2,1)S(1)}, bf16[16,4096]{1,0:T(8,128)(2,1)S(1)}, u32[]{:S(2)}, u32[]{:S(2)}) %collective-permute-start.4) | collective-permute-done | bytes 131104 | tf_op jit(solution)/shard_map/ppermute | solution.py:445
  27.9 1.9 %collective-permute-done.5.refs_3_ = bf16[16,4096]{1,0:T(8,128)(2,1)S(1)} collective-permute-done((bf16[16,4096]{1,0:T(8,128)(2,1)S(1)}, bf16[16,4096]{1,0:T(8,128)(2,1)S(1)}, u32[]{:S(2)}, u32[]{:S(2)}) %collective-permute-start.5) | collective-permute-done | bytes 131104 | tf_op jit(solution)/shard_map/ppermute | solution.py:445
  29.8 0.7 %collective-permute-done.12.refs_5_ = bf16[32,2048]{1,0:T(8,128)(2,1)S(1)} collective-permute-done((bf16[32,2048]{1,0:T(8,128)(2,1)S(1)}, bf16[32,2048]{1,0:T(8,128)(2,1)S(1)}, u32[]{:S(2)}, u32[]{:S(2)}) %collective-permute-start.12) | collective-permute-done | bytes 131104 | tf_op jit(solution)/shard_map/ppermute | solution.py:445
  30.5 2.1 %first_half.1 = (f32[64,768]{1,0:T(8,128)S(1)}, f32[64,768]{1,0:T(8,128)S(1)}, f32[64,768]{1,0:T(8,128)S(1)}, bf16[64,2048]{1,0:T(8,128)(2,1)S(1)}, bf16[64,2048]{1,0:T(8,128)(2,1)S(1)}) custom-call(bf16[16,4096]{1,0:T(8,128)(2,1)S(1)} %get-tuple-element.33.refs_0_, bf16[16,4096]{1,0:T(8,128)(2,1)S(1)} %collective-permute-done.3.refs_1_, ...), custom_call_target="tpu_custom_call" | custom-call | flops 603979776 | bytes 9437184 | tf_op jit(solution)/shard_map/first_half/pallas_call | solution.py:239
  32.7 6.7 %second_half.1 = (bf16[64,768]{1,0:T(8,128)(2,1)S(1)}, bf16[64,768]{1,0:T(8,128)(2,1)S(1)}, bf16[64,768]{1,0:T(8,128)(2,1)S(1)}, bf16[64,2048]{1,0:T(8,128)(2,1)...) custom-call(bf16[16,4096]{1,0:T(8,128)(2,1)S(1)} %get-tuple-element.33.refs_0_, ...), custom_call_target="tpu_custom_call" | custom-call | flops 1409286144 | bytes 18874368 | tf_op jit(solution)/shard_map/second_half/pallas_call | solution.py:302
  39.4 5.9 %all-to-all-start = ((bf16[32,2,4096]{2,1,0:T(2,128)(2,1)}), bf16[32,2,4096]{2,1,0:T(2,128)(2,1)S(1)}, u32[]{:S(2)}, u32[]{:S(2)}) async-start(bf16[32,2,4096]{2,1,0:T(2,128)(2,1)} %get-tuple-element.51), calls=%async_computation | async-start | bytes 1048576 | tf_op jit(solution)/shard_map/all_to_all | solution.py:482
  45.3 3.3 %down_grad.1 = bf16[1,768,4096]{2,1,0:T(8,128)(2,1)} custom-call(bf16[64,2048]{1,0:T(8,128)(2,1)S(1)} %get-tuple-element.56.refs_0_, bf16[64,2048]{1,0:T(8,128)(2,1)S(1)} %get-tuple-element.57.refs_1_, bf16[64,768]{1,0:T(8,128)(2,1)S(1)} %get-tuple-element.58.refs_2_), custom_call_target="tpu_custom_call" | custom-call | flops 402653184 | bytes 6291456 | tf_op jit(solution)/shard_map/down_grad/pallas_call | solution.py:381
  48.6 5.3 %pair_grad.1 = bf16[1,2,4096,768]{3,2,1,0:T(8,128)(2,1)} custom-call(bf16[64,2048]{1,0:T(8,128)(2,1)S(1)} %get-tuple-element.52.refs_0_, bf16[64,2048]{1,0:T(8,128)(2,1)S(1)} %get-tuple-element.53.refs_1_, bf16[64,768]{1,0:T(8,128)(2,1)S(1)} %get-tuple-element.54.refs_2_, bf16[64,768]{1,0:T(8,128)(2,1)S(1)} %get-tuple-element.55.refs_3_), custom_call_target="tpu_custom_call" | custom-call | flops 805306368 | bytes 12582912 | tf_op jit(solution)/shard_map/pair_grad/pallas_call | solution.py:344
  53.9 7.1 %all-to-all-done.rows_ref = bf16[32,2,4096]{2,1,0:T(2,128)(2,1)S(1)} async-done(((bf16[32,2,4096]{2,1,0:T(2,128)(2,1)}), bf16[32,2,4096]{2,1,0:T(2,128)(2,1)S(1)}, u32[]{:S(2)}, u32[]{:S(2)}) %all-to-all-start) | async-done | bytes 524320 | tf_op jit(solution)/shard_map/all_to_all | solution.py:482
  61.0 1.3 %spread_rows.1 = bf16[128,4096]{1,0:T(8,128)(2,1)} custom-call(bf16[32,2,4096]{2,1,0:T(2,128)(2,1)S(1)} %all-to-all-done.rows_ref, bf16[32,128]{1,0:T(8,128)(2,1)S(1)} %get-tuple-element.39.after.place_ref), custom_call_target="tpu_custom_call" | custom-call | flops 33554432 | bytes 1048576 | tf_op jit(solution)/shard_map/spread_rows/pallas_call | solution.py:416
  (14 shorter events, 0.9 us)
Async XLA Ops:
  2.7 15.4 %collective-permute-start.6 = (bf16[4,4,4096]{2,1,0:T(4,128)(2,1)S(1)}, bf16[4,4,4096]{2,1,0:T(4,128)(2,1)S(1)}, u32[]{:S(2)}, u32[]{:S(2)}) collective-permute-start(bf16[4,4,4096]{2,1,0:T(4,128)(2,1)S(1)} %get-tuple-element.37), channel_id=1, source_target_pairs={{0,8},{1,9},{2,10},{3,11},{4,12},{5,13},{6,14},{7,15},{8,0},{9,1},... | collective-permute-start | bytes 393224 | tf_op jit(solution)/shard_map/ppermute | solution.py:445
  6.8 11.3 %collective-permute-start.7 = (bf16[4,4,4096]{2,1,0:T(4,128)(2,1)S(1)}, bf16[4,4,4096]{2,1,0:T(4,128)(2,1)S(1)}, u32[]{:S(2)}, u32[]{:S(2)}) collective-permute-start(bf16[4,4,4096]{2,1,0:T(4,128)(2,1)S(1)} %get-tuple-element.38), channel_id=1, source_target_pairs={{0,12},{1,13},{2,14},{3,15},{4,8},{5,9},{6,10},{7,11},{8,4},{9,5},... | collective-permute-start | bytes 393224 | tf_op jit(solution)/shard_map/ppermute | solution.py:445
  8.1 11.9 %collective-permute-start.1 = (bf16[4,4,4096]{2,1,0:T(4,128)(2,1)S(1)}, bf16[4,4,4096]{2,1,0:T(4,128)(2,1)S(1)}, u32[]{:S(2)}, u32[]{:S(2)}) collective-permute-start(bf16[4,4,4096]{2,1,0:T(4,128)(2,1)S(1)} %get-tuple-element.31.refs_0_), channel_id=1, source_target_pairs={{0,16},{1,17},{2,18},{3,19},{4,20},{5,21},{6,22},{7,23},{8,24},{9,... | collective-permute-start | bytes 393224 | tf_op jit(solution)/shard_map/ppermute | solution.py:445
  9.6 10.6 %collective-permute-start.2 = (bf16[4,4,4096]{2,1,0:T(4,128)(2,1)S(1)}, bf16[4,4,4096]{2,1,0:T(4,128)(2,1)S(1)}, u32[]{:S(2)}, u32[]{:S(2)}) collective-permute-start(bf16[4,4,4096]{2,1,0:T(4,128)(2,1)S(1)} %get-tuple-element.32), channel_id=1, source_target_pairs={{0,20},{1,21},{2,22},{3,23},{4,16},{5,17},{6,18},{7,19},{8,28},{9,... | collective-permute-start | bytes 393224 | tf_op jit(solution)/shard_map/ppermute | solution.py:445
  9.8 11.2 %collective-permute-start = (bf16[4,4,4096]{2,1,0:T(4,128)(2,1)S(1)}, bf16[4,4,4096]{2,1,0:T(4,128)(2,1)S(1)}, u32[]{:S(2)}, u32[]{:S(2)}) collective-permute-start(bf16[4,4,4096]{2,1,0:T(4,128)(2,1)S(1)} %get-tuple-element.32), channel_id=1, source_target_pairs={{0,4},{1,5},{2,6},{3,7},{4,0},{5,1},{6,2},{7,3},{8,12},{9,13},{10,... | collective-permute-start | bytes 393224 | tf_op jit(solution)/shard_map/ppermute | solution.py:445
  18.3 4.8 %collective-permute-start.8 = (bf16[8,4096]{1,0:T(8,128)(2,1)S(1)}, bf16[8,4096]{1,0:T(8,128)(2,1)S(1)}, u32[]{:S(2)}, u32[]{:S(2)}) collective-permute-start(bf16[8,4096]{1,0:T(8,128)(2,1)S(1)} %get-tuple-element.42), channel_id=1, source_target_pairs={{0,1},{1,0},{2,3},{3,2},{4,5},{5,4},{6,7},{7,6},{8,9},{9,8},{10,11... | collective-permute-start | bytes 196616 | tf_op jit(solution)/shard_map/ppermute | solution.py:445
  18.4 5.0 %collective-permute-start.9 = (bf16[8,4096]{1,0:T(8,128)(2,1)S(1)}, bf16[8,4096]{1,0:T(8,128)(2,1)S(1)}, u32[]{:S(2)}, u32[]{:S(2)}) collective-permute-start(bf16[8,4096]{1,0:T(8,128)(2,1)S(1)} %get-tuple-element.43), channel_id=1, source_target_pairs={{0,2},{1,3},{2,0},{3,1},{4,6},{5,7},{6,4},{7,5},{8,10},{9,11},{10,... | collective-permute-start | bytes 196616 | tf_op jit(solution)/shard_map/ppermute | solution.py:445
  20.0 4.0 %collective-permute-start.10 = (bf16[8,4096]{1,0:T(8,128)(2,1)S(1)}, bf16[8,4096]{1,0:T(8,128)(2,1)S(1)}, u32[]{:S(2)}, u32[]{:S(2)}) collective-permute-start(bf16[8,4096]{1,0:T(8,128)(2,1)S(1)} %get-tuple-element.44), channel_id=1, source_target_pairs={{0,3},{1,2},{2,1},{3,0},{4,7},{5,6},{6,5},{7,4},{8,11},{9,10},{10,... | collective-permute-start | bytes 196616 | tf_op jit(solution)/shard_map/ppermute | solution.py:445
  21.4 4.8 %collective-permute-start.3 = (bf16[16,4096]{1,0:T(8,128)(2,1)S(1)}, bf16[16,4096]{1,0:T(8,128)(2,1)S(1)}, u32[]{:S(2)}, u32[]{:S(2)}) collective-permute-start(bf16[16,4096]{1,0:T(8,128)(2,1)S(1)} %get-tuple-element.34), channel_id=1, source_target_pairs={{0,1},{1,0},{2,3},{3,2},{4,5},{5,4},{6,7},{7,6},{8,9},{9,8},{10,11... | collective-permute-start | bytes 393224 | tf_op jit(solution)/shard_map/ppermute | solution.py:445
  21.5 6.4 %collective-permute-start.4 = (bf16[16,4096]{1,0:T(8,128)(2,1)S(1)}, bf16[16,4096]{1,0:T(8,128)(2,1)S(1)}, u32[]{:S(2)}, u32[]{:S(2)}) collective-permute-start(bf16[16,4096]{1,0:T(8,128)(2,1)S(1)} %get-tuple-element.35), channel_id=1, source_target_pairs={{0,2},{1,3},{2,0},{3,1},{4,6},{5,7},{6,4},{7,5},{8,10},{9,11},{10,... | collective-permute-start | bytes 393224 | tf_op jit(solution)/shard_map/ppermute | solution.py:445
  23.1 6.6 %collective-permute-start.5 = (bf16[16,4096]{1,0:T(8,128)(2,1)S(1)}, bf16[16,4096]{1,0:T(8,128)(2,1)S(1)}, u32[]{:S(2)}, u32[]{:S(2)}) collective-permute-start(bf16[16,4096]{1,0:T(8,128)(2,1)S(1)} %get-tuple-element.36), channel_id=1, source_target_pairs={{0,3},{1,2},{2,1},{3,0},{4,7},{5,6},{6,5},{7,4},{8,11},{9,10},{10,... | collective-permute-start | bytes 393224 | tf_op jit(solution)/shard_map/ppermute | solution.py:445
  24.1 6.4 %collective-permute-start.12 = (bf16[32,2048]{1,0:T(8,128)(2,1)S(1)}, bf16[32,2048]{1,0:T(8,128)(2,1)S(1)}, u32[]{:S(2)}, u32[]{:S(2)}) collective-permute-start(bf16[32,2048]{1,0:T(8,128)(2,1)S(1)} %get-tuple-element.46.refs_4_), channel_id=1, source_target_pairs={{0,16},{1,17},{2,18},{3,19},{4,20},{5,21},{6,22},{7,23},{8,24},{9,... | collective-permute-start | bytes 393224 | tf_op jit(solution)/shard_map/ppermute | solution.py:445
  25.7 6.9 %collective-permute-start.11 = (bf16[32,2048]{1,0:T(8,128)(2,1)S(1)}, bf16[32,2048]{1,0:T(8,128)(2,1)S(1)}, u32[]{:S(2)}, u32[]{:S(2)}) collective-permute-start(bf16[32,2048]{1,0:T(8,128)(2,1)S(1)} %get-tuple-element.45.refs_4_), channel_id=1, source_target_pairs={{0,16},{1,17},{2,18},{3,19},{4,20},{5,21},{6,22},{7,23},{8,24},{9,... | collective-permute-start | bytes 393224 | tf_op jit(solution)/shard_map/ppermute | solution.py:445
  39.4 21.7 %all-to-all-start = ((bf16[32,2,4096]{2,1,0:T(2,128)(2,1)}), bf16[32,2,4096]{2,1,0:T(2,128)(2,1)S(1)}, u32[]{:S(2)}, u32[]{:S(2)}) async-start(bf16[32,2,4096]{2,1,0:T(2,128)(2,1)} %get-tuple-element.51), calls=%async_computation | async-start | bytes 1048576 | tf_op jit(solution)/shard_map/all_to_all | solution.py:482

commit v9 on v8

--- a/solution.py
+++ b/solution.py
@@ -458,20 +458,21 @@
     first = merge([arrived[high] for high in early] + first)
     loaded = pltpu.with_memory_space_constraint(down, pltpu.VMEM)
     second = merge([arrived[high] for high in late], (loaded,))
-    mine = [send(second[low], 0, low) for low in range(near)]
+    order = [0] + list(range(near - 1, 0, -1))
+    mine = [send(second[low], 0, low) for low in order]
     halves = stack(mine)
-    near_rows = [send(first[low], 0, low) for low in range(near)]
+    near_rows = [send(first[low], 0, low) for low in order]
     far_rows = [[send(half, group, 0) for group in range(groups)] for half in halves]
     homes = [
         (group, high * near + low)
-        for low in range(near)
+        for low in order
         for group in range(groups)
         for high in early
     ]
     homes += [
         (group, high * near + low)
         for group in range(groups)
-        for low in range(near)
+        for low in order
         for high in late
     ]
     pair = pltpu.with_memory_space_constraint(pair, pltpu.VMEM)

time: 62.8 us -> 63 us (level)
  no operation moved by 1% of the time
where the time goes in v9:
time: 63 us; the launch traced here: 62.7 us
  Pallas kernels  27.9 us (44%)
  starting transfers between devices  20.8 us (33%)
  waiting for transfers between devices  13.1 us (21%)
  between operations  0.9 us (1%)
    ppermute x13, starting transfers between devices, send(): return lax.ppermute(value, ('dp', 'expert'), pairs)  14.9 us
    all_to_all x1, waiting for transfers between devices, per_device(): lax.all_to_all(parts, ('dp', 'expert'), split_axis=0, concat_axis=0, tile...  7.14 us
    pallas_call x1, Pallas kernels, second_half(): pl.pallas_call(functools.partial(second_kernel, homes, experts, near, gro...  6.68 us
    pallas_call x1, Pallas kernels, load(): pl.pallas_call(functools.partial(load_kernel, chunk), in_specs=[HBM] * 2...  6.5 us
    ppermute x13, waiting for transfers between devices, send(): return lax.ppermute(value, ('dp', 'expert'), pairs)  5.96 us
    all_to_all x1, starting transfers between devices, per_device(): lax.all_to_all(parts, ('dp', 'expert'), split_axis=0, concat_axis=0, tile...  5.91 us
    pallas_call x1, Pallas kernels, pair_grad(): pl.pallas_call(functools.partial(pair_grad_kernel, blocks, chunk), in_spe...  5.26 us
    pallas_call x1, Pallas kernels, down_grad(): pl.pallas_call(functools.partial(down_grad_kernel, blocks, chunk), in_spe...  3.32 us
  transfers between devices with their start and end apart: 14, of which 6 were waited for; matrix products, arithmetic and copies ran while one was open for 0% of the time, Pallas kernels for 29%

profile of v9, /device:TPU:0, one launch (start us, length us, event | category | flops | bytes accessed | tf_op | source)
XLA Modules:
  0.0 62.7 jit_solution(10956445749500649839)
XLA Ops:
  0.6 2.0 %route_rows.1 = (bf16[4,4,4096]{2,1,0:T(4,128)(2,1)S(1)}, bf16[4,4,4096]{2,1,0:T(4,128)(2,1)S(1)}, bf16[4,4,4096]{2,1,0:T(4,128)(2,1)S(1)}, bf16[4,4,4096]{2,1,0:T(4,128)(2,1)S(1)}, bf16[32,128]{1,0:T(8,128)(2,1)S(1)}) custom-call(s32[1,128]{1,0:T(1,128)} %bitcast.6, f32[1,128]{1,0:T(1,128)} %bitcast.7, bf16[128,4096]{1,0:T(8,128)(2,1)} %act_hbm.1, ...), custom_call_target="tpu_custom_call" | custom-call | flops 67108864 | bytes 2097152 | tf_op jit(solution)/shard_map/route_rows/pallas_call | solution.py:112
  2.7 4.1 %collective-permute-start.6 = (bf16[4,4,4096]{2,1,0:T(4,128)(2,1)S(1)}, bf16[4,4,4096]{2,1,0:T(4,128)(2,1)S(1)}, u32[]{:S(2)}, u32[]{:S(2)}) collective-permute-start(bf16[4,4,4096]{2,1,0:T(4,128)(2,1)S(1)} %get-tuple-element.37), channel_id=1, source_target_pairs={{0,8},{1,9},{2,10},{3,11},{4,12},{5,13},{6,14},{7,15},{8,0},{9,1},... | collective-permute-start | bytes 393224 | tf_op jit(solution)/shard_map/ppermute | solution.py:445
  6.8 1.3 %collective-permute-start.7 = (bf16[4,4,4096]{2,1,0:T(4,128)(2,1)S(1)}, bf16[4,4,4096]{2,1,0:T(4,128)(2,1)S(1)}, u32[]{:S(2)}, u32[]{:S(2)}) collective-permute-start(bf16[4,4,4096]{2,1,0:T(4,128)(2,1)S(1)} %get-tuple-element.38), channel_id=1, source_target_pairs={{0,12},{1,13},{2,14},{3,15},{4,8},{5,9},{6,10},{7,11},{8,4},{9,5},... | collective-permute-start | bytes 393224 | tf_op jit(solution)/shard_map/ppermute | solution.py:445
  8.1 1.5 %collective-permute-start.1 = (bf16[4,4,4096]{2,1,0:T(4,128)(2,1)S(1)}, bf16[4,4,4096]{2,1,0:T(4,128)(2,1)S(1)}, u32[]{:S(2)}, u32[]{:S(2)}) collective-permute-start(bf16[4,4,4096]{2,1,0:T(4,128)(2,1)S(1)} %get-tuple-element.31.refs_0_), channel_id=1, source_target_pairs={{0,16},{1,17},{2,18},{3,19},{4,20},{5,21},{6,22},{7,23},{8,24},{9,... | collective-permute-start | bytes 393224 | tf_op jit(solution)/shard_map/ppermute | solution.py:445
  9.8 1.8 %collective-permute-start = (bf16[4,4,4096]{2,1,0:T(4,128)(2,1)S(1)}, bf16[4,4,4096]{2,1,0:T(4,128)(2,1)S(1)}, u32[]{:S(2)}, u32[]{:S(2)}) collective-permute-start(bf16[4,4,4096]{2,1,0:T(4,128)(2,1)S(1)} %get-tuple-element.32), channel_id=1, source_target_pairs={{0,4},{1,5},{2,6},{3,7},{4,0},{5,1},{6,2},{7,3},{8,12},{9,13},{10,... | collective-permute-start | bytes 393224 | tf_op jit(solution)/shard_map/ppermute | solution.py:445
  11.6 6.5 %load_weights.1 = (bf16[2,4096,768]{2,1,0:T(8,128)(2,1)S(1)}, bf16[768,4096]{1,0:T(8,128)(2,1)S(1)}) custom-call(bf16[2,4096,768]{2,1,0:T(8,128)(2,1)} %bitcast.4, bf16[768,4096]{1,0:T(8,128)(2,1)} %bitcast.5, bf16[32,128]{1,0:T(8,128)(2,1)S(1)} %get-tuple-element.39.after.place_ref), custom_call_target="tpu_custom_call" | custom-call | bytes 18874368 | tf_op jit(solution)/shard_map/load_weights/pallas_call | solution.py:195
  18.4 1.6 %collective-permute-start.9 = (bf16[8,4096]{1,0:T(8,128)(2,1)S(1)}, bf16[8,4096]{1,0:T(8,128)(2,1)S(1)}, u32[]{:S(2)}, u32[]{:S(2)}) collective-permute-start(bf16[8,4096]{1,0:T(8,128)(2,1)S(1)} %get-tuple-element.43), channel_id=1, source_target_pairs={{0,2},{1,3},{2,0},{3,1},{4,6},{5,7},{6,4},{7,5},{8,10},{9,11},{10,... | collective-permute-start | bytes 196616 | tf_op jit(solution)/shard_map/ppermute | solution.py:445
  20.3 0.8 %collective-permute-done.refs_1_ = bf16[4,4,4096]{2,1,0:T(4,128)(2,1)S(1)} collective-permute-done((bf16[4,4,4096]{2,1,0:T(4,128)(2,1)S(1)}, bf16[4,4,4096]{2,1,0:T(4,128)(2,1)S(1)}, u32[]{:S(2)}, u32[]{:S(2)}) %collective-permute-start) | collective-permute-done | bytes 131104 | tf_op jit(solution)/shard_map/ppermute | solution.py:445
  21.0 0.4 merge_rows.2
  21.4 0.7 %collective-permute-start.3 = (bf16[16,4096]{1,0:T(8,128)(2,1)S(1)}, bf16[16,4096]{1,0:T(8,128)(2,1)S(1)}, u32[]{:S(2)}, u32[]{:S(2)}) collective-permute-start(bf16[16,4096]{1,0:T(8,128)(2,1)S(1)} %get-tuple-element.34), channel_id=1, source_target_pairs={{0,3},{1,2},{2,1},{3,0},{4,7},{5,6},{6,5},{7,4},{8,11},{9,10},{10,... | collective-permute-start | bytes 393224 | tf_op jit(solution)/shard_map/ppermute | solution.py:445
  22.2 1.0 %collective-permute-start.4 = (bf16[16,4096]{1,0:T(8,128)(2,1)S(1)}, bf16[16,4096]{1,0:T(8,128)(2,1)S(1)}, u32[]{:S(2)}, u32[]{:S(2)}) collective-permute-start(bf16[16,4096]{1,0:T(8,128)(2,1)S(1)} %get-tuple-element.35), channel_id=1, source_target_pairs={{0,2},{1,3},{2,0},{3,1},{4,6},{5,7},{6,4},{7,5},{8,10},{9,11},{10,... | collective-permute-start | bytes 393224 | tf_op jit(solution)/shard_map/ppermute | solution.py:445
  23.4 0.8 %collective-permute-done.9.refs_2_ = bf16[8,4096]{1,0:T(8,128)(2,1)S(1)} collective-permute-done((bf16[8,4096]{1,0:T(8,128)(2,1)S(1)}, bf16[8,4096]{1,0:T(8,128)(2,1)S(1)}, u32[]{:S(2)}, u32[]{:S(2)}) %collective-permute-start.9) | collective-permute-done | bytes 65568 | tf_op jit(solution)/shard_map/ppermute | solution.py:445
  24.3 1.6 %collective-permute-start.12 = (bf16[32,2048]{1,0:T(8,128)(2,1)S(1)}, bf16[32,2048]{1,0:T(8,128)(2,1)S(1)}, u32[]{:S(2)}, u32[]{:S(2)}) collective-permute-start(bf16[32,2048]{1,0:T(8,128)(2,1)S(1)} %get-tuple-element.46.refs_4_), channel_id=1, source_target_pairs={{0,16},{1,17},{2,18},{3,19},{4,20},{5,21},{6,22},{7,23},{8,24},{9,... | collective-permute-start | bytes 393224 | tf_op jit(solution)/shard_map/ppermute | solution.py:445
  25.9 0.5 collective-permute-start.11
  26.4 0.8 %collective-permute-done.3.refs_1_ = bf16[16,4096]{1,0:T(8,128)(2,1)S(1)} collective-permute-done((bf16[16,4096]{1,0:T(8,128)(2,1)S(1)}, bf16[16,4096]{1,0:T(8,128)(2,1)S(1)}, u32[]{:S(2)}, u32[]{:S(2)}) %collective-permute-start.3) | collective-permute-done | bytes 131104 | tf_op jit(solution)/shard_map/ppermute | solution.py:445
  27.2 2.9 %collective-permute-done.4.refs_2_ = bf16[16,4096]{1,0:T(8,128)(2,1)S(1)} collective-permute-done((bf16[16,4096]{1,0:T(8,128)(2,1)S(1)}, bf16[16,4096]{1,0:T(8,128)(2,1)S(1)}, u32[]{:S(2)}, u32[]{:S(2)}) %collective-permute-start.4) | collective-permute-done | bytes 131104 | tf_op jit(solution)/shard_map/ppermute | solution.py:445
  30.1 0.6 collective-permute-done.12.refs_5_
  30.7 2.1 %first_half.1 = (f32[64,768]{1,0:T(8,128)S(1)}, f32[64,768]{1,0:T(8,128)S(1)}, f32[64,768]{1,0:T(8,128)S(1)}, bf16[64,2048]{1,0:T(8,128)(2,1)S(1)}, bf16[64,2048]{1,0:T(8,128)(2,1)S(1)}) custom-call(bf16[16,4096]{1,0:T(8,128)(2,1)S(1)} %get-tuple-element.33.refs_0_, bf16[16,4096]{1,0:T(8,128)(2,1)S(1)} %collective-permute-done.3.refs_1_, ...), custom_call_target="tpu_custom_call" | custom-call | flops 603979776 | bytes 9437184 | tf_op jit(solution)/shard_map/first_half/pallas_call | solution.py:239
  32.9 6.7 %second_half.1 = (bf16[64,768]{1,0:T(8,128)(2,1)S(1)}, bf16[64,768]{1,0:T(8,128)(2,1)S(1)}, bf16[64,768]{1,0:T(8,128)(2,1)S(1)}, bf16[64,2048]{1,0:T(8,128)(2,1)...) custom-call(bf16[16,4096]{1,0:T(8,128)(2,1)S(1)} %get-tuple-element.33.refs_0_, ...), custom_call_target="tpu_custom_call" | custom-call | flops 1409286144 | bytes 18874368 | tf_op jit(solution)/shard_map/second_half/pallas_call | solution.py:302
  39.5 5.9 %all-to-all-start = ((bf16[32,2,4096]{2,1,0:T(2,128)(2,1)}), bf16[32,2,4096]{2,1,0:T(2,128)(2,1)S(1)}, u32[]{:S(2)}, u32[]{:S(2)}) async-start(bf16[32,2,4096]{2,1,0:T(2,128)(2,1)} %get-tuple-element.51), calls=%async_computation | async-start | bytes 1048576 | tf_op jit(solution)/shard_map/all_to_all | solution.py:483
  45.5 3.3 %down_grad.1 = bf16[1,768,4096]{2,1,0:T(8,128)(2,1)} custom-call(bf16[64,2048]{1,0:T(8,128)(2,1)S(1)} %get-tuple-element.56.refs_0_, bf16[64,2048]{1,0:T(8,128)(2,1)S(1)} %get-tuple-element.57.refs_1_, bf16[64,768]{1,0:T(8,128)(2,1)S(1)} %get-tuple-element.58.refs_2_), custom_call_target="tpu_custom_call" | custom-call | flops 402653184 | bytes 6291456 | tf_op jit(solution)/shard_map/down_grad/pallas_call | solution.py:381
  48.8 5.3 %pair_grad.1 = bf16[1,2,4096,768]{3,2,1,0:T(8,128)(2,1)} custom-call(bf16[64,2048]{1,0:T(8,128)(2,1)S(1)} %get-tuple-element.52.refs_0_, bf16[64,2048]{1,0:T(8,128)(2,1)S(1)} %get-tuple-element.53.refs_1_, bf16[64,768]{1,0:T(8,128)(2,1)S(1)} %get-tuple-element.54.refs_2_, bf16[64,768]{1,0:T(8,128)(2,1)S(1)} %get-tuple-element.55.refs_3_), custom_call_target="tpu_custom_call" | custom-call | flops 805306368 | bytes 12582912 | tf_op jit(solution)/shard_map/pair_grad/pallas_call | solution.py:344
  54.1 7.1 %all-to-all-done.rows_ref = bf16[32,2,4096]{2,1,0:T(2,128)(2,1)S(1)} async-done(((bf16[32,2,4096]{2,1,0:T(2,128)(2,1)}), bf16[32,2,4096]{2,1,0:T(2,128)(2,1)S(1)}, u32[]{:S(2)}, u32[]{:S(2)}) %all-to-all-start) | async-done | bytes 524320 | tf_op jit(solution)/shard_map/all_to_all | solution.py:483
  61.2 1.3 %spread_rows.1 = bf16[128,4096]{1,0:T(8,128)(2,1)} custom-call(bf16[32,2,4096]{2,1,0:T(2,128)(2,1)S(1)} %all-to-all-done.rows_ref, bf16[32,128]{1,0:T(8,128)(2,1)S(1)} %get-tuple-element.39.after.place_ref), custom_call_target="tpu_custom_call" | custom-call | flops 33554432 | bytes 1048576 | tf_op jit(solution)/shard_map/spread_rows/pallas_call | solution.py:416
  (14 shorter events, 1.1 us)
Async XLA Ops:
  2.7 15.4 %collective-permute-start.6 = (bf16[4,4,4096]{2,1,0:T(4,128)(2,1)S(1)}, bf16[4,4,4096]{2,1,0:T(4,128)(2,1)S(1)}, u32[]{:S(2)}, u32[]{:S(2)}) collective-permute-start(bf16[4,4,4096]{2,1,0:T(4,128)(2,1)S(1)} %get-tuple-element.37), channel_id=1, source_target_pairs={{0,8},{1,9},{2,10},{3,11},{4,12},{5,13},{6,14},{7,15},{8,0},{9,1},... | collective-permute-start | bytes 393224 | tf_op jit(solution)/shard_map/ppermute | solution.py:445
  6.8 11.3 %collective-permute-start.7 = (bf16[4,4,4096]{2,1,0:T(4,128)(2,1)S(1)}, bf16[4,4,4096]{2,1,0:T(4,128)(2,1)S(1)}, u32[]{:S(2)}, u32[]{:S(2)}) collective-permute-start(bf16[4,4,4096]{2,1,0:T(4,128)(2,1)S(1)} %get-tuple-element.38), channel_id=1, source_target_pairs={{0,12},{1,13},{2,14},{3,15},{4,8},{5,9},{6,10},{7,11},{8,4},{9,5},... | collective-permute-start | bytes 393224 | tf_op jit(solution)/shard_map/ppermute | solution.py:445
  8.1 11.9 %collective-permute-start.1 = (bf16[4,4,4096]{2,1,0:T(4,128)(2,1)S(1)}, bf16[4,4,4096]{2,1,0:T(4,128)(2,1)S(1)}, u32[]{:S(2)}, u32[]{:S(2)}) collective-permute-start(bf16[4,4,4096]{2,1,0:T(4,128)(2,1)S(1)} %get-tuple-element.31.refs_0_), channel_id=1, source_target_pairs={{0,16},{1,17},{2,18},{3,19},{4,20},{5,21},{6,22},{7,23},{8,24},{9,... | collective-permute-start | bytes 393224 | tf_op jit(solution)/shard_map/ppermute | solution.py:445
  9.6 10.6 %collective-permute-start.2 = (bf16[4,4,4096]{2,1,0:T(4,128)(2,1)S(1)}, bf16[4,4,4096]{2,1,0:T(4,128)(2,1)S(1)}, u32[]{:S(2)}, u32[]{:S(2)}) collective-permute-start(bf16[4,4,4096]{2,1,0:T(4,128)(2,1)S(1)} %get-tuple-element.32), channel_id=1, source_target_pairs={{0,20},{1,21},{2,22},{3,23},{4,16},{5,17},{6,18},{7,19},{8,28},{9,... | collective-permute-start | bytes 393224 | tf_op jit(solution)/shard_map/ppermute | solution.py:445
  9.8 11.2 %collective-permute-start = (bf16[4,4,4096]{2,1,0:T(4,128)(2,1)S(1)}, bf16[4,4,4096]{2,1,0:T(4,128)(2,1)S(1)}, u32[]{:S(2)}, u32[]{:S(2)}) collective-permute-start(bf16[4,4,4096]{2,1,0:T(4,128)(2,1)S(1)} %get-tuple-element.32), channel_id=1, source_target_pairs={{0,4},{1,5},{2,6},{3,7},{4,0},{5,1},{6,2},{7,3},{8,12},{9,13},{10,... | collective-permute-start | bytes 393224 | tf_op jit(solution)/shard_map/ppermute | solution.py:445
  18.3 4.8 %collective-permute-start.8 = (bf16[8,4096]{1,0:T(8,128)(2,1)S(1)}, bf16[8,4096]{1,0:T(8,128)(2,1)S(1)}, u32[]{:S(2)}, u32[]{:S(2)}) collective-permute-start(bf16[8,4096]{1,0:T(8,128)(2,1)S(1)} %get-tuple-element.42), channel_id=1, source_target_pairs={{0,3},{1,2},{2,1},{3,0},{4,7},{5,6},{6,5},{7,4},{8,11},{9,10},{10,... | collective-permute-start | bytes 196616 | tf_op jit(solution)/shard_map/ppermute | solution.py:445
  18.4 5.8 %collective-permute-start.9 = (bf16[8,4096]{1,0:T(8,128)(2,1)S(1)}, bf16[8,4096]{1,0:T(8,128)(2,1)S(1)}, u32[]{:S(2)}, u32[]{:S(2)}) collective-permute-start(bf16[8,4096]{1,0:T(8,128)(2,1)S(1)} %get-tuple-element.43), channel_id=1, source_target_pairs={{0,2},{1,3},{2,0},{3,1},{4,6},{5,7},{6,4},{7,5},{8,10},{9,11},{10,... | collective-permute-start | bytes 196616 | tf_op jit(solution)/shard_map/ppermute | solution.py:445
  20.0 4.2 %collective-permute-start.10 = (bf16[8,4096]{1,0:T(8,128)(2,1)S(1)}, bf16[8,4096]{1,0:T(8,128)(2,1)S(1)}, u32[]{:S(2)}, u32[]{:S(2)}) collective-permute-start(bf16[8,4096]{1,0:T(8,128)(2,1)S(1)} %get-tuple-element.44), channel_id=1, source_target_pairs={{0,1},{1,0},{2,3},{3,2},{4,5},{5,4},{6,7},{7,6},{8,9},{9,8},{10,11... | collective-permute-start | bytes 196616 | tf_op jit(solution)/shard_map/ppermute | solution.py:445
  21.4 5.8 %collective-permute-start.3 = (bf16[16,4096]{1,0:T(8,128)(2,1)S(1)}, bf16[16,4096]{1,0:T(8,128)(2,1)S(1)}, u32[]{:S(2)}, u32[]{:S(2)}) collective-permute-start(bf16[16,4096]{1,0:T(8,128)(2,1)S(1)} %get-tuple-element.34), channel_id=1, source_target_pairs={{0,3},{1,2},{2,1},{3,0},{4,7},{5,6},{6,5},{7,4},{8,11},{9,10},{10,... | collective-permute-start | bytes 393224 | tf_op jit(solution)/shard_map/ppermute | solution.py:445
  22.2 7.9 %collective-permute-start.4 = (bf16[16,4096]{1,0:T(8,128)(2,1)S(1)}, bf16[16,4096]{1,0:T(8,128)(2,1)S(1)}, u32[]{:S(2)}, u32[]{:S(2)}) collective-permute-start(bf16[16,4096]{1,0:T(8,128)(2,1)S(1)} %get-tuple-element.35), channel_id=1, source_target_pairs={{0,2},{1,3},{2,0},{3,1},{4,6},{5,7},{6,4},{7,5},{8,10},{9,11},{10,... | collective-permute-start | bytes 393224 | tf_op jit(solution)/shard_map/ppermute | solution.py:445
  23.1 7.0 %collective-permute-start.5 = (bf16[16,4096]{1,0:T(8,128)(2,1)S(1)}, bf16[16,4096]{1,0:T(8,128)(2,1)S(1)}, u32[]{:S(2)}, u32[]{:S(2)}) collective-permute-start(bf16[16,4096]{1,0:T(8,128)(2,1)S(1)} %get-tuple-element.36), channel_id=1, source_target_pairs={{0,1},{1,0},{2,3},{3,2},{4,5},{5,4},{6,7},{7,6},{8,9},{9,8},{10,11... | collective-permute-start | bytes 393224 | tf_op jit(solution)/shard_map/ppermute | solution.py:445
  24.3 6.4 %collective-permute-start.12 = (bf16[32,2048]{1,0:T(8,128)(2,1)S(1)}, bf16[32,2048]{1,0:T(8,128)(2,1)S(1)}, u32[]{:S(2)}, u32[]{:S(2)}) collective-permute-start(bf16[32,2048]{1,0:T(8,128)(2,1)S(1)} %get-tuple-element.46.refs_4_), channel_id=1, source_target_pairs={{0,16},{1,17},{2,18},{3,19},{4,20},{5,21},{6,22},{7,23},{8,24},{9,... | collective-permute-start | bytes 393224 | tf_op jit(solution)/shard_map/ppermute | solution.py:445
  25.9 7.0 %collective-permute-start.11 = (bf16[32,2048]{1,0:T(8,128)(2,1)S(1)}, bf16[32,2048]{1,0:T(8,128)(2,1)S(1)}, u32[]{:S(2)}, u32[]{:S(2)}) collective-permute-start(bf16[32,2048]{1,0:T(8,128)(2,1)S(1)} %get-tuple-element.45.refs_4_), channel_id=1, source_target_pairs={{0,16},{1,17},{2,18},{3,19},{4,20},{5,21},{6,22},{7,23},{8,24},{9,... | collective-permute-start | bytes 393224 | tf_op jit(solution)/shard_map/ppermute | solution.py:445
  39.5 21.6 %all-to-all-start = ((bf16[32,2,4096]{2,1,0:T(2,128)(2,1)}), bf16[32,2,4096]{2,1,0:T(2,128)(2,1)S(1)}, u32[]{:S(2)}, u32[]{:S(2)}) async-start(bf16[32,2,4096]{2,1,0:T(2,128)(2,1)} %get-tuple-element.51), calls=%async_computation | async-start | bytes 1048576 | tf_op jit(solution)/shard_map/all_to_all | solution.py:483

commit v10 on v8

--- a/solution.py
+++ b/solution.py
@@ -260,18 +260,21 @@
     tok, cot = gather_columns(near_rows, far_rows, there, slice(0, half))
     tok_all[...] = tok
     cot_all[...] = cot
-    pre_gate = gate_sum[...] + dot_nn(tok, pair[0, there, :])
-    pre_up = up_sum[...] + dot_nn(tok, pair[1, there, :])
-    hidden_grad = hid_sum[...] + dot_nt(cot, down[:, there])
-    sigmoid_gate = jax.nn.sigmoid(pre_gate)
-    activated = pre_gate * sigmoid_gate
-    hidden_out[...] = (activated * pre_up).astype(jnp.bfloat16)
-    gate_grad = (
-        hidden_grad * pre_up * sigmoid_gate * (1.0 + pre_gate * (1.0 - sigmoid_gate))
-    ).astype(jnp.bfloat16)
-    up_grad = (hidden_grad * activated).astype(jnp.bfloat16)
-    gate_out[...] = gate_grad
-    up_out[...] = up_grad
+    units = down.shape[0]
+    tile = 256 if units % 256 == 0 else units
+    for start in range(0, units, tile):
+        unit = slice(start, start + tile)
+        pre_gate = gate_sum[:, unit] + dot_nn(tok, pair[0, there, unit])
+        pre_up = up_sum[:, unit] + dot_nn(tok, pair[1, there, unit])
+        hidden_grad = hid_sum[:, unit] + dot_nt(cot, down[unit, there])
+        sigmoid_gate = jax.nn.sigmoid(pre_gate)
+        activated = pre_gate * sigmoid_gate
+        hidden_out[:, unit] = (activated * pre_up).astype(jnp.bfloat16)
+        gate_out[:, unit] = (
+            hidden_grad * pre_up * sigmoid_gate * (1.0 + pre_gate * (1.0 - sigmoid_gate))
+        ).astype(jnp.bfloat16)
+        up_out[:, unit] = (hidden_grad * activated).astype(jnp.bfloat16)
+    gate_grad, up_grad = gate_out[...], up_out[...]
     me, group = lax.axis_index("expert"), lax.axis_index("dp")
     rows = [
         lax.rem(group - back + groups, groups) * experts + (me ^ turn) for back, turn in homes

time: 62.8 us -> 62.8 us (level)
  no operation moved by 1% of the time
where the time goes in v10:
time: 62.8 us; the launch traced here: 62.5 us
  Pallas kernels  27.9 us (44%)
  starting transfers between devices  20.8 us (33%)
  waiting for transfers between devices  12.9 us (21%)
  between operations  0.91 us (1%)
    ppermute x13, starting transfers between devices, send(): return lax.ppermute(value, ('dp', 'expert'), pairs)  14.9 us
    all_to_all x1, waiting for transfers between devices, per_device(): lax.all_to_all(parts, ('dp', 'expert'), split_axis=0, concat_axis=0, tile...  7.14 us
    pallas_call x1, Pallas kernels, second_half(): pl.pallas_call(functools.partial(second_kernel, homes, experts, near, gro...  6.65 us
    pallas_call x1, Pallas kernels, load(): pl.pallas_call(functools.partial(load_kernel, chunk), in_specs=[HBM] * 2...  6.5 us
    all_to_all x1, starting transfers between devices, per_device(): lax.all_to_all(parts, ('dp', 'expert'), split_axis=0, concat_axis=0, tile...  5.94 us
    ppermute x13, waiting for transfers between devices, send(): return lax.ppermute(value, ('dp', 'expert'), pairs)  5.74 us
    pallas_call x1, Pallas kernels, pair_grad(): pl.pallas_call(functools.partial(pair_grad_kernel, blocks, chunk), in_spe...  5.26 us
    pallas_call x1, Pallas kernels, down_grad(): pl.pallas_call(functools.partial(down_grad_kernel, blocks, chunk), in_spe...  3.32 us
  transfers between devices with their start and end apart: 14, of which 6 were waited for; matrix products, arithmetic and copies ran while one was open for 0% of the time, Pallas kernels for 29%

profile of v10, /device:TPU:0, one launch (start us, length us, event | category | flops | bytes accessed | tf_op | source)
XLA Modules:
  0.0 62.5 jit_solution(10090418621740598266)
XLA Ops:
  0.6 2.0 %route_rows.1 = (bf16[4,4,4096]{2,1,0:T(4,128)(2,1)S(1)}, bf16[4,4,4096]{2,1,0:T(4,128)(2,1)S(1)}, bf16[4,4,4096]{2,1,0:T(4,128)(2,1)S(1)}, bf16[4,4,4096]{2,1,0:T(4,128)(2,1)S(1)}, bf16[32,128]{1,0:T(8,128)(2,1)S(1)}) custom-call(s32[1,128]{1,0:T(1,128)} %bitcast.6, f32[1,128]{1,0:T(1,128)} %bitcast.7, bf16[128,4096]{1,0:T(8,128)(2,1)} %act_hbm.1, ...), custom_call_target="tpu_custom_call" | custom-call | flops 67108864 | bytes 2097152 | tf_op jit(solution)/shard_map/route_rows/pallas_call | solution.py:112
  2.7 4.1 %collective-permute-start.6 = (bf16[4,4,4096]{2,1,0:T(4,128)(2,1)S(1)}, bf16[4,4,4096]{2,1,0:T(4,128)(2,1)S(1)}, u32[]{:S(2)}, u32[]{:S(2)}) collective-permute-start(bf16[4,4,4096]{2,1,0:T(4,128)(2,1)S(1)} %get-tuple-element.37), channel_id=1, source_target_pairs={{0,8},{1,9},{2,10},{3,11},{4,12},{5,13},{6,14},{7,15},{8,0},{9,1},... | collective-permute-start | bytes 393224 | tf_op jit(solution)/shard_map/ppermute | solution.py:448
  6.8 1.3 %collective-permute-start.7 = (bf16[4,4,4096]{2,1,0:T(4,128)(2,1)S(1)}, bf16[4,4,4096]{2,1,0:T(4,128)(2,1)S(1)}, u32[]{:S(2)}, u32[]{:S(2)}) collective-permute-start(bf16[4,4,4096]{2,1,0:T(4,128)(2,1)S(1)} %get-tuple-element.38), channel_id=1, source_target_pairs={{0,12},{1,13},{2,14},{3,15},{4,8},{5,9},{6,10},{7,11},{8,4},{9,5},... | collective-permute-start | bytes 393224 | tf_op jit(solution)/shard_map/ppermute | solution.py:448
  8.1 1.5 %collective-permute-start.1 = (bf16[4,4,4096]{2,1,0:T(4,128)(2,1)S(1)}, bf16[4,4,4096]{2,1,0:T(4,128)(2,1)S(1)}, u32[]{:S(2)}, u32[]{:S(2)}) collective-permute-start(bf16[4,4,4096]{2,1,0:T(4,128)(2,1)S(1)} %get-tuple-element.31.refs_0_), channel_id=1, source_target_pairs={{0,16},{1,17},{2,18},{3,19},{4,20},{5,21},{6,22},{7,23},{8,24},{9,... | collective-permute-start | bytes 393224 | tf_op jit(solution)/shard_map/ppermute | solution.py:448
  9.8 1.8 %collective-permute-start = (bf16[4,4,4096]{2,1,0:T(4,128)(2,1)S(1)}, bf16[4,4,4096]{2,1,0:T(4,128)(2,1)S(1)}, u32[]{:S(2)}, u32[]{:S(2)}) collective-permute-start(bf16[4,4,4096]{2,1,0:T(4,128)(2,1)S(1)} %get-tuple-element.32), channel_id=1, source_target_pairs={{0,4},{1,5},{2,6},{3,7},{4,0},{5,1},{6,2},{7,3},{8,12},{9,13},{10,... | collective-permute-start | bytes 393224 | tf_op jit(solution)/shard_map/ppermute | solution.py:448
  11.6 6.5 %load_weights.1 = (bf16[2,4096,768]{2,1,0:T(8,128)(2,1)S(1)}, bf16[768,4096]{1,0:T(8,128)(2,1)S(1)}) custom-call(bf16[2,4096,768]{2,1,0:T(8,128)(2,1)} %bitcast.4, bf16[768,4096]{1,0:T(8,128)(2,1)} %bitcast.5, bf16[32,128]{1,0:T(8,128)(2,1)S(1)} %get-tuple-element.39.after.place_ref), custom_call_target="tpu_custom_call" | custom-call | bytes 18874368 | tf_op jit(solution)/shard_map/load_weights/pallas_call | solution.py:195
  18.4 1.6 %collective-permute-start.9 = (bf16[8,4096]{1,0:T(8,128)(2,1)S(1)}, bf16[8,4096]{1,0:T(8,128)(2,1)S(1)}, u32[]{:S(2)}, u32[]{:S(2)}) collective-permute-start(bf16[8,4096]{1,0:T(8,128)(2,1)S(1)} %get-tuple-element.43), channel_id=1, source_target_pairs={{0,2},{1,3},{2,0},{3,1},{4,6},{5,7},{6,4},{7,5},{8,10},{9,11},{10,... | collective-permute-start | bytes 196616 | tf_op jit(solution)/shard_map/ppermute | solution.py:448
  20.0 0.3 collective-permute-start.10
  20.3 0.8 %collective-permute-done.refs_1_ = bf16[4,4,4096]{2,1,0:T(4,128)(2,1)S(1)} collective-permute-done((bf16[4,4,4096]{2,1,0:T(4,128)(2,1)S(1)}, bf16[4,4,4096]{2,1,0:T(4,128)(2,1)S(1)}, u32[]{:S(2)}, u32[]{:S(2)}) %collective-permute-start) | collective-permute-done | bytes 131104 | tf_op jit(solution)/shard_map/ppermute | solution.py:448
  21.0 0.4 merge_rows.2
  21.5 1.6 %collective-permute-start.4 = (bf16[16,4096]{1,0:T(8,128)(2,1)S(1)}, bf16[16,4096]{1,0:T(8,128)(2,1)S(1)}, u32[]{:S(2)}, u32[]{:S(2)}) collective-permute-start(bf16[16,4096]{1,0:T(8,128)(2,1)S(1)} %get-tuple-element.35), channel_id=1, source_target_pairs={{0,2},{1,3},{2,0},{3,1},{4,6},{5,7},{6,4},{7,5},{8,10},{9,11},{10,... | collective-permute-start | bytes 393224 | tf_op jit(solution)/shard_map/ppermute | solution.py:448
  23.4 0.6 %collective-permute-done.10.refs_3_ = bf16[8,4096]{1,0:T(8,128)(2,1)S(1)} collective-permute-done((bf16[8,4096]{1,0:T(8,128)(2,1)S(1)}, bf16[8,4096]{1,0:T(8,128)(2,1)S(1)}, u32[]{:S(2)}, u32[]{:S(2)}) %collective-permute-start.10) | collective-permute-done | bytes 65568 | tf_op jit(solution)/shard_map/ppermute | solution.py:448
  24.1 1.6 %collective-permute-start.12 = (bf16[32,2048]{1,0:T(8,128)(2,1)S(1)}, bf16[32,2048]{1,0:T(8,128)(2,1)S(1)}, u32[]{:S(2)}, u32[]{:S(2)}) collective-permute-start(bf16[32,2048]{1,0:T(8,128)(2,1)S(1)} %get-tuple-element.46.refs_4_), channel_id=1, source_target_pairs={{0,16},{1,17},{2,18},{3,19},{4,20},{5,21},{6,22},{7,23},{8,24},{9,... | collective-permute-start | bytes 393224 | tf_op jit(solution)/shard_map/ppermute | solution.py:448
  25.7 0.5 collective-permute-start.11
  26.2 1.7 %collective-permute-done.4.refs_2_ = bf16[16,4096]{1,0:T(8,128)(2,1)S(1)} collective-permute-done((bf16[16,4096]{1,0:T(8,128)(2,1)S(1)}, bf16[16,4096]{1,0:T(8,128)(2,1)S(1)}, u32[]{:S(2)}, u32[]{:S(2)}) %collective-permute-start.4) | collective-permute-done | bytes 131104 | tf_op jit(solution)/shard_map/ppermute | solution.py:448
  27.9 1.9 %collective-permute-done.5.refs_3_ = bf16[16,4096]{1,0:T(8,128)(2,1)S(1)} collective-permute-done((bf16[16,4096]{1,0:T(8,128)(2,1)S(1)}, bf16[16,4096]{1,0:T(8,128)(2,1)S(1)}, u32[]{:S(2)}, u32[]{:S(2)}) %collective-permute-start.5) | collective-permute-done | bytes 131104 | tf_op jit(solution)/shard_map/ppermute | solution.py:448
  29.8 0.7 %collective-permute-done.12.refs_5_ = bf16[32,2048]{1,0:T(8,128)(2,1)S(1)} collective-permute-done((bf16[32,2048]{1,0:T(8,128)(2,1)S(1)}, bf16[32,2048]{1,0:T(8,128)(2,1)S(1)}, u32[]{:S(2)}, u32[]{:S(2)}) %collective-permute-start.12) | collective-permute-done | bytes 131104 | tf_op jit(solution)/shard_map/ppermute | solution.py:448
  30.5 2.1 %first_half.1 = (f32[64,768]{1,0:T(8,128)S(1)}, f32[64,768]{1,0:T(8,128)S(1)}, f32[64,768]{1,0:T(8,128)S(1)}, bf16[64,2048]{1,0:T(8,128)(2,1)S(1)}, bf16[64,2048]{1,0:T(8,128)(2,1)S(1)}) custom-call(bf16[16,4096]{1,0:T(8,128)(2,1)S(1)} %get-tuple-element.33.refs_0_, bf16[16,4096]{1,0:T(8,128)(2,1)S(1)} %collective-permute-done.3.refs_1_, ...), custom_call_target="tpu_custom_call" | custom-call | flops 603979776 | bytes 9437184 | tf_op jit(solution)/shard_map/first_half/pallas_call | solution.py:239
  32.7 6.6 %second_half.1 = (bf16[64,768]{1,0:T(8,128)(2,1)S(1)}, bf16[64,768]{1,0:T(8,128)(2,1)S(1)}, bf16[64,768]{1,0:T(8,128)(2,1)S(1)}, bf16[64,2048]{1,0:T(8,128)(2,1)...) custom-call(bf16[16,4096]{1,0:T(8,128)(2,1)S(1)} %get-tuple-element.33.refs_0_, ...), custom_call_target="tpu_custom_call" | custom-call | flops 1409286144 | bytes 18874368 | tf_op jit(solution)/shard_map/second_half/pallas_call | solution.py:305
  39.3 5.9 %all-to-all-start = ((bf16[32,2,4096]{2,1,0:T(2,128)(2,1)}), bf16[32,2,4096]{2,1,0:T(2,128)(2,1)S(1)}, u32[]{:S(2)}, u32[]{:S(2)}) async-start(bf16[32,2,4096]{2,1,0:T(2,128)(2,1)} %get-tuple-element.51), calls=%async_computation | async-start | bytes 1048576 | tf_op jit(solution)/shard_map/all_to_all | solution.py:485
  45.3 3.3 %down_grad.1 = bf16[1,768,4096]{2,1,0:T(8,128)(2,1)} custom-call(bf16[64,2048]{1,0:T(8,128)(2,1)S(1)} %get-tuple-element.56.refs_0_, bf16[64,2048]{1,0:T(8,128)(2,1)S(1)} %get-tuple-element.57.refs_1_, bf16[64,768]{1,0:T(8,128)(2,1)S(1)} %get-tuple-element.58.refs_2_), custom_call_target="tpu_custom_call" | custom-call | flops 402653184 | bytes 6291456 | tf_op jit(solution)/shard_map/down_grad/pallas_call | solution.py:384
  48.6 5.3 %pair_grad.1 = bf16[1,2,4096,768]{3,2,1,0:T(8,128)(2,1)} custom-call(bf16[64,2048]{1,0:T(8,128)(2,1)S(1)} %get-tuple-element.52.refs_0_, bf16[64,2048]{1,0:T(8,128)(2,1)S(1)} %get-tuple-element.53.refs_1_, bf16[64,768]{1,0:T(8,128)(2,1)S(1)} %get-tuple-element.54.refs_2_, bf16[64,768]{1,0:T(8,128)(2,1)S(1)} %get-tuple-element.55.refs_3_), custom_call_target="tpu_custom_call" | custom-call | flops 805306368 | bytes 12582912 | tf_op jit(solution)/shard_map/pair_grad/pallas_call | solution.py:347
  53.9 7.1 %all-to-all-done.rows_ref = bf16[32,2,4096]{2,1,0:T(2,128)(2,1)S(1)} async-done(((bf16[32,2,4096]{2,1,0:T(2,128)(2,1)}), bf16[32,2,4096]{2,1,0:T(2,128)(2,1)S(1)}, u32[]{:S(2)}, u32[]{:S(2)}) %all-to-all-start) | async-done | bytes 524320 | tf_op jit(solution)/shard_map/all_to_all | solution.py:485
  61.0 1.3 %spread_rows.1 = bf16[128,4096]{1,0:T(8,128)(2,1)} custom-call(bf16[32,2,4096]{2,1,0:T(2,128)(2,1)S(1)} %all-to-all-done.rows_ref, bf16[32,128]{1,0:T(8,128)(2,1)S(1)} %get-tuple-element.39.after.place_ref), custom_call_target="tpu_custom_call" | custom-call | flops 33554432 | bytes 1048576 | tf_op jit(solution)/shard_map/spread_rows/pallas_call | solution.py:419
  (14 shorter events, 0.9 us)
Async XLA Ops:
  2.7 15.4 %collective-permute-start.6 = (bf16[4,4,4096]{2,1,0:T(4,128)(2,1)S(1)}, bf16[4,4,4096]{2,1,0:T(4,128)(2,1)S(1)}, u32[]{:S(2)}, u32[]{:S(2)}) collective-permute-start(bf16[4,4,4096]{2,1,0:T(4,128)(2,1)S(1)} %get-tuple-element.37), channel_id=1, source_target_pairs={{0,8},{1,9},{2,10},{3,11},{4,12},{5,13},{6,14},{7,15},{8,0},{9,1},... | collective-permute-start | bytes 393224 | tf_op jit(solution)/shard_map/ppermute | solution.py:448
  6.8 11.3 %collective-permute-start.7 = (bf16[4,4,4096]{2,1,0:T(4,128)(2,1)S(1)}, bf16[4,4,4096]{2,1,0:T(4,128)(2,1)S(1)}, u32[]{:S(2)}, u32[]{:S(2)}) collective-permute-start(bf16[4,4,4096]{2,1,0:T(4,128)(2,1)S(1)} %get-tuple-element.38), channel_id=1, source_target_pairs={{0,12},{1,13},{2,14},{3,15},{4,8},{5,9},{6,10},{7,11},{8,4},{9,5},... | collective-permute-start | bytes 393224 | tf_op jit(solution)/shard_map/ppermute | solution.py:448
  8.1 11.9 %collective-permute-start.1 = (bf16[4,4,4096]{2,1,0:T(4,128)(2,1)S(1)}, bf16[4,4,4096]{2,1,0:T(4,128)(2,1)S(1)}, u32[]{:S(2)}, u32[]{:S(2)}) collective-permute-start(bf16[4,4,4096]{2,1,0:T(4,128)(2,1)S(1)} %get-tuple-element.31.refs_0_), channel_id=1, source_target_pairs={{0,16},{1,17},{2,18},{3,19},{4,20},{5,21},{6,22},{7,23},{8,24},{9,... | collective-permute-start | bytes 393224 | tf_op jit(solution)/shard_map/ppermute | solution.py:448
  9.6 10.6 %collective-permute-start.2 = (bf16[4,4,4096]{2,1,0:T(4,128)(2,1)S(1)}, bf16[4,4,4096]{2,1,0:T(4,128)(2,1)S(1)}, u32[]{:S(2)}, u32[]{:S(2)}) collective-permute-start(bf16[4,4,4096]{2,1,0:T(4,128)(2,1)S(1)} %get-tuple-element.32), channel_id=1, source_target_pairs={{0,20},{1,21},{2,22},{3,23},{4,16},{5,17},{6,18},{7,19},{8,28},{9,... | collective-permute-start | bytes 393224 | tf_op jit(solution)/shard_map/ppermute | solution.py:448
  9.8 11.2 %collective-permute-start = (bf16[4,4,4096]{2,1,0:T(4,128)(2,1)S(1)}, bf16[4,4,4096]{2,1,0:T(4,128)(2,1)S(1)}, u32[]{:S(2)}, u32[]{:S(2)}) collective-permute-start(bf16[4,4,4096]{2,1,0:T(4,128)(2,1)S(1)} %get-tuple-element.32), channel_id=1, source_target_pairs={{0,4},{1,5},{2,6},{3,7},{4,0},{5,1},{6,2},{7,3},{8,12},{9,13},{10,... | collective-permute-start | bytes 393224 | tf_op jit(solution)/shard_map/ppermute | solution.py:448
  18.3 4.8 %collective-permute-start.8 = (bf16[8,4096]{1,0:T(8,128)(2,1)S(1)}, bf16[8,4096]{1,0:T(8,128)(2,1)S(1)}, u32[]{:S(2)}, u32[]{:S(2)}) collective-permute-start(bf16[8,4096]{1,0:T(8,128)(2,1)S(1)} %get-tuple-element.42), channel_id=1, source_target_pairs={{0,1},{1,0},{2,3},{3,2},{4,5},{5,4},{6,7},{7,6},{8,9},{9,8},{10,11... | collective-permute-start | bytes 196616 | tf_op jit(solution)/shard_map/ppermute | solution.py:448
  18.4 5.0 %collective-permute-start.9 = (bf16[8,4096]{1,0:T(8,128)(2,1)S(1)}, bf16[8,4096]{1,0:T(8,128)(2,1)S(1)}, u32[]{:S(2)}, u32[]{:S(2)}) collective-permute-start(bf16[8,4096]{1,0:T(8,128)(2,1)S(1)} %get-tuple-element.43), channel_id=1, source_target_pairs={{0,2},{1,3},{2,0},{3,1},{4,6},{5,7},{6,4},{7,5},{8,10},{9,11},{10,... | collective-permute-start | bytes 196616 | tf_op jit(solution)/shard_map/ppermute | solution.py:448
  20.0 4.0 %collective-permute-start.10 = (bf16[8,4096]{1,0:T(8,128)(2,1)S(1)}, bf16[8,4096]{1,0:T(8,128)(2,1)S(1)}, u32[]{:S(2)}, u32[]{:S(2)}) collective-permute-start(bf16[8,4096]{1,0:T(8,128)(2,1)S(1)} %get-tuple-element.44), channel_id=1, source_target_pairs={{0,3},{1,2},{2,1},{3,0},{4,7},{5,6},{6,5},{7,4},{8,11},{9,10},{10,... | collective-permute-start | bytes 196616 | tf_op jit(solution)/shard_map/ppermute | solution.py:448
  21.4 4.8 %collective-permute-start.3 = (bf16[16,4096]{1,0:T(8,128)(2,1)S(1)}, bf16[16,4096]{1,0:T(8,128)(2,1)S(1)}, u32[]{:S(2)}, u32[]{:S(2)}) collective-permute-start(bf16[16,4096]{1,0:T(8,128)(2,1)S(1)} %get-tuple-element.34), channel_id=1, source_target_pairs={{0,1},{1,0},{2,3},{3,2},{4,5},{5,4},{6,7},{7,6},{8,9},{9,8},{10,11... | collective-permute-start | bytes 393224 | tf_op jit(solution)/shard_map/ppermute | solution.py:448
  21.5 6.4 %collective-permute-start.4 = (bf16[16,4096]{1,0:T(8,128)(2,1)S(1)}, bf16[16,4096]{1,0:T(8,128)(2,1)S(1)}, u32[]{:S(2)}, u32[]{:S(2)}) collective-permute-start(bf16[16,4096]{1,0:T(8,128)(2,1)S(1)} %get-tuple-element.35), channel_id=1, source_target_pairs={{0,2},{1,3},{2,0},{3,1},{4,6},{5,7},{6,4},{7,5},{8,10},{9,11},{10,... | collective-permute-start | bytes 393224 | tf_op jit(solution)/shard_map/ppermute | solution.py:448
  23.1 6.6 %collective-permute-start.5 = (bf16[16,4096]{1,0:T(8,128)(2,1)S(1)}, bf16[16,4096]{1,0:T(8,128)(2,1)S(1)}, u32[]{:S(2)}, u32[]{:S(2)}) collective-permute-start(bf16[16,4096]{1,0:T(8,128)(2,1)S(1)} %get-tuple-element.36), channel_id=1, source_target_pairs={{0,3},{1,2},{2,1},{3,0},{4,7},{5,6},{6,5},{7,4},{8,11},{9,10},{10,... | collective-permute-start | bytes 393224 | tf_op jit(solution)/shard_map/ppermute | solution.py:448
  24.1 6.4 %collective-permute-start.12 = (bf16[32,2048]{1,0:T(8,128)(2,1)S(1)}, bf16[32,2048]{1,0:T(8,128)(2,1)S(1)}, u32[]{:S(2)}, u32[]{:S(2)}) collective-permute-start(bf16[32,2048]{1,0:T(8,128)(2,1)S(1)} %get-tuple-element.46.refs_4_), channel_id=1, source_target_pairs={{0,16},{1,17},{2,18},{3,19},{4,20},{5,21},{6,22},{7,23},{8,24},{9,... | collective-permute-start | bytes 393224 | tf_op jit(solution)/shard_map/ppermute | solution.py:448
  25.7 6.9 %collective-permute-start.11 = (bf16[32,2048]{1,0:T(8,128)(2,1)S(1)}, bf16[32,2048]{1,0:T(8,128)(2,1)S(1)}, u32[]{:S(2)}, u32[]{:S(2)}) collective-permute-start(bf16[32,2048]{1,0:T(8,128)(2,1)S(1)} %get-tuple-element.45.refs_4_), channel_id=1, source_target_pairs={{0,16},{1,17},{2,18},{3,19},{4,20},{5,21},{6,22},{7,23},{8,24},{9,... | collective-permute-start | bytes 393224 | tf_op jit(solution)/shard_map/ppermute | solution.py:448
  39.3 21.7 %all-to-all-start = ((bf16[32,2,4096]{2,1,0:T(2,128)(2,1)}), bf16[32,2,4096]{2,1,0:T(2,128)(2,1)S(1)}, u32[]{:S(2)}, u32[]{:S(2)}) async-start(bf16[32,2,4096]{2,1,0:T(2,128)(2,1)} %get-tuple-element.51), calls=%async_computation | async-start | bytes 1048576 | tf_op jit(solution)/shard_map/all_to_all | solution.py:485

commit v11 on v8

--- a/solution.py
+++ b/solution.py
@@ -277,15 +277,16 @@
         lax.rem(group - back + groups, groups) * experts + (me ^ turn) for back, turn in homes
     ]
     copies = []
-    for step in range(width // chunk):
-        at = slice(step * chunk, (step + 1) * chunk)
-        value = dot_nt(gate_grad, pair[0, at, :]) + dot_nt(up_grad, pair[1, at, :])
-        value = value.astype(jnp.bfloat16)
-        for block, row in enumerate(rows):
-            parts[row, :, at] = value[block * CAP : (block + 1) * CAP]
-        where = pl.ds(step * chunk, chunk)
+    for side in range(HALVES):
+        for step in range(side * half // chunk, (side + 1) * half // chunk):
+            at = slice(step * chunk, (step + 1) * chunk)
+            value = dot_nt(gate_grad, pair[0, at, :]) + dot_nt(up_grad, pair[1, at, :])
+            value = value.astype(jnp.bfloat16)
+            for block, row in enumerate(rows):
+                parts[row, :, at] = value[block * CAP : (block + 1) * CAP]
+        where = pl.ds(side * half, half)
         one = pltpu.make_async_copy(
-            parts.at[:, :, where], parts_hbm.at[:, :, where], sems.at[step]
+            parts.at[:, :, where], parts_hbm.at[:, :, where], sems.at[side]
         )
         one.start()
         copies.append(one)
@@ -308,7 +309,7 @@
         + [pltpu.HBM((blocks, CAP, width), jnp.bfloat16)],
         scratch_shapes=[
             pltpu.VMEM((blocks, CAP, width), jnp.bfloat16),
-            pltpu.SemaphoreType.DMA((width // chunk,)),
+            pltpu.SemaphoreType.DMA((HALVES,)),
         ],
         compiler_params=params(24),
         cost_estimate=cost(7 * total * width * units, 6 * width * units),
@@ -412,7 +413,7 @@
 def spread(rows, place):
     width = rows.shape[2]
     slots, tokens = place.shape
-    chunk = min(1024, width)
+    chunk = width // HALVES
     return pl.pallas_call(
         functools.partial(spread_kernel, chunk),
         in_specs=[VMEM] * 2,

time: 62.8 us -> 62.9 us (level)
  no operation moved by 1% of the time
where the time goes in v11:
time: 62.9 us; the launch traced here: 62.6 us
  Pallas kernels  28 us (45%)
  starting transfers between devices  20.8 us (33%)
  waiting for transfers between devices  12.9 us (21%)
  between operations  0.91 us (1%)
    ppermute x13, starting transfers between devices, send(): return lax.ppermute(value, ('dp', 'expert'), pairs)  14.9 us
    all_to_all x1, waiting for transfers between devices, per_device(): lax.all_to_all(parts, ('dp', 'expert'), split_axis=0, concat_axis=0, tile...  7.14 us
    pallas_call x1, Pallas kernels, second_half(): pl.pallas_call(functools.partial(second_kernel, homes, experts, near, gro...  6.7 us
    pallas_call x1, Pallas kernels, load(): pl.pallas_call(functools.partial(load_kernel, chunk), in_specs=[HBM] * 2...  6.5 us
    all_to_all x1, starting transfers between devices, per_device(): lax.all_to_all(parts, ('dp', 'expert'), split_axis=0, concat_axis=0, tile...  5.94 us
    ppermute x13, waiting for transfers between devices, send(): return lax.ppermute(value, ('dp', 'expert'), pairs)  5.74 us
    pallas_call x1, Pallas kernels, pair_grad(): pl.pallas_call(functools.partial(pair_grad_kernel, blocks, chunk), in_spe...  5.25 us
    pallas_call x1, Pallas kernels, down_grad(): pl.pallas_call(functools.partial(down_grad_kernel, blocks, chunk), in_spe...  3.33 us
  transfers between devices with their start and end apart: 14, of which 6 were waited for; matrix products, arithmetic and copies ran while one was open for 0% of the time, Pallas kernels for 29%

profile of v11, /device:TPU:0, one launch (start us, length us, event | category | flops | bytes accessed | tf_op | source)
XLA Modules:
  0.0 62.6 jit_solution(3653879911883229726)
XLA Ops:
  0.6 2.0 %route_rows.1 = (bf16[4,4,4096]{2,1,0:T(4,128)(2,1)S(1)}, bf16[4,4,4096]{2,1,0:T(4,128)(2,1)S(1)}, bf16[4,4,4096]{2,1,0:T(4,128)(2,1)S(1)}, bf16[4,4,4096]{2,1,0:T(4,128)(2,1)S(1)}, bf16[32,128]{1,0:T(8,128)(2,1)S(1)}) custom-call(s32[1,128]{1,0:T(1,128)} %bitcast.6, f32[1,128]{1,0:T(1,128)} %bitcast.7, bf16[128,4096]{1,0:T(8,128)(2,1)} %act_hbm.1, ...), custom_call_target="tpu_custom_call" | custom-call | flops 67108864 | bytes 2097152 | tf_op jit(solution)/shard_map/route_rows/pallas_call | solution.py:112
  2.7 4.1 %collective-permute-start.6 = (bf16[4,4,4096]{2,1,0:T(4,128)(2,1)S(1)}, bf16[4,4,4096]{2,1,0:T(4,128)(2,1)S(1)}, u32[]{:S(2)}, u32[]{:S(2)}) collective-permute-start(bf16[4,4,4096]{2,1,0:T(4,128)(2,1)S(1)} %get-tuple-element.37), channel_id=1, source_target_pairs={{0,8},{1,9},{2,10},{3,11},{4,12},{5,13},{6,14},{7,15},{8,0},{9,1},... | collective-permute-start | bytes 393224 | tf_op jit(solution)/shard_map/ppermute | solution.py:446
  6.8 1.3 %collective-permute-start.7 = (bf16[4,4,4096]{2,1,0:T(4,128)(2,1)S(1)}, bf16[4,4,4096]{2,1,0:T(4,128)(2,1)S(1)}, u32[]{:S(2)}, u32[]{:S(2)}) collective-permute-start(bf16[4,4,4096]{2,1,0:T(4,128)(2,1)S(1)} %get-tuple-element.38), channel_id=1, source_target_pairs={{0,12},{1,13},{2,14},{3,15},{4,8},{5,9},{6,10},{7,11},{8,4},{9,5},... | collective-permute-start | bytes 393224 | tf_op jit(solution)/shard_map/ppermute | solution.py:446
  8.1 1.5 %collective-permute-start.1 = (bf16[4,4,4096]{2,1,0:T(4,128)(2,1)S(1)}, bf16[4,4,4096]{2,1,0:T(4,128)(2,1)S(1)}, u32[]{:S(2)}, u32[]{:S(2)}) collective-permute-start(bf16[4,4,4096]{2,1,0:T(4,128)(2,1)S(1)} %get-tuple-element.31.refs_0_), channel_id=1, source_target_pairs={{0,16},{1,17},{2,18},{3,19},{4,20},{5,21},{6,22},{7,23},{8,24},{9,... | collective-permute-start | bytes 393224 | tf_op jit(solution)/shard_map/ppermute | solution.py:446
  9.8 1.8 %collective-permute-start = (bf16[4,4,4096]{2,1,0:T(4,128)(2,1)S(1)}, bf16[4,4,4096]{2,1,0:T(4,128)(2,1)S(1)}, u32[]{:S(2)}, u32[]{:S(2)}) collective-permute-start(bf16[4,4,4096]{2,1,0:T(4,128)(2,1)S(1)} %get-tuple-element.32), channel_id=1, source_target_pairs={{0,4},{1,5},{2,6},{3,7},{4,0},{5,1},{6,2},{7,3},{8,12},{9,13},{10,... | collective-permute-start | bytes 393224 | tf_op jit(solution)/shard_map/ppermute | solution.py:446
  11.6 6.5 %load_weights.1 = (bf16[2,4096,768]{2,1,0:T(8,128)(2,1)S(1)}, bf16[768,4096]{1,0:T(8,128)(2,1)S(1)}) custom-call(bf16[2,4096,768]{2,1,0:T(8,128)(2,1)} %bitcast.4, bf16[768,4096]{1,0:T(8,128)(2,1)} %bitcast.5, bf16[32,128]{1,0:T(8,128)(2,1)S(1)} %get-tuple-element.39.after.place_ref), custom_call_target="tpu_custom_call" | custom-call | bytes 18874368 | tf_op jit(solution)/shard_map/load_weights/pallas_call | solution.py:195
  18.4 1.6 %collective-permute-start.9 = (bf16[8,4096]{1,0:T(8,128)(2,1)S(1)}, bf16[8,4096]{1,0:T(8,128)(2,1)S(1)}, u32[]{:S(2)}, u32[]{:S(2)}) collective-permute-start(bf16[8,4096]{1,0:T(8,128)(2,1)S(1)} %get-tuple-element.43), channel_id=1, source_target_pairs={{0,2},{1,3},{2,0},{3,1},{4,6},{5,7},{6,4},{7,5},{8,10},{9,11},{10,... | collective-permute-start | bytes 196616 | tf_op jit(solution)/shard_map/ppermute | solution.py:446
  20.0 0.3 collective-permute-start.10
  20.3 0.8 %collective-permute-done.refs_1_ = bf16[4,4,4096]{2,1,0:T(4,128)(2,1)S(1)} collective-permute-done((bf16[4,4,4096]{2,1,0:T(4,128)(2,1)S(1)}, bf16[4,4,4096]{2,1,0:T(4,128)(2,1)S(1)}, u32[]{:S(2)}, u32[]{:S(2)}) %collective-permute-start) | collective-permute-done | bytes 131104 | tf_op jit(solution)/shard_map/ppermute | solution.py:446
  21.0 0.4 merge_rows.2
  21.5 1.6 %collective-permute-start.4 = (bf16[16,4096]{1,0:T(8,128)(2,1)S(1)}, bf16[16,4096]{1,0:T(8,128)(2,1)S(1)}, u32[]{:S(2)}, u32[]{:S(2)}) collective-permute-start(bf16[16,4096]{1,0:T(8,128)(2,1)S(1)} %get-tuple-element.35), channel_id=1, source_target_pairs={{0,2},{1,3},{2,0},{3,1},{4,6},{5,7},{6,4},{7,5},{8,10},{9,11},{10,... | collective-permute-start | bytes 393224 | tf_op jit(solution)/shard_map/ppermute | solution.py:446
  23.4 0.6 %collective-permute-done.10.refs_3_ = bf16[8,4096]{1,0:T(8,128)(2,1)S(1)} collective-permute-done((bf16[8,4096]{1,0:T(8,128)(2,1)S(1)}, bf16[8,4096]{1,0:T(8,128)(2,1)S(1)}, u32[]{:S(2)}, u32[]{:S(2)}) %collective-permute-start.10) | collective-permute-done | bytes 65568 | tf_op jit(solution)/shard_map/ppermute | solution.py:446
  24.1 1.6 %collective-permute-start.12 = (bf16[32,2048]{1,0:T(8,128)(2,1)S(1)}, bf16[32,2048]{1,0:T(8,128)(2,1)S(1)}, u32[]{:S(2)}, u32[]{:S(2)}) collective-permute-start(bf16[32,2048]{1,0:T(8,128)(2,1)S(1)} %get-tuple-element.46.refs_4_), channel_id=1, source_target_pairs={{0,16},{1,17},{2,18},{3,19},{4,20},{5,21},{6,22},{7,23},{8,24},{9,... | collective-permute-start | bytes 393224 | tf_op jit(solution)/shard_map/ppermute | solution.py:446
  25.7 0.5 collective-permute-start.11
  26.2 1.7 %collective-permute-done.4.refs_2_ = bf16[16,4096]{1,0:T(8,128)(2,1)S(1)} collective-permute-done((bf16[16,4096]{1,0:T(8,128)(2,1)S(1)}, bf16[16,4096]{1,0:T(8,128)(2,1)S(1)}, u32[]{:S(2)}, u32[]{:S(2)}) %collective-permute-start.4) | collective-permute-done | bytes 131104 | tf_op jit(solution)/shard_map/ppermute | solution.py:446
  27.9 1.9 %collective-permute-done.5.refs_3_ = bf16[16,4096]{1,0:T(8,128)(2,1)S(1)} collective-permute-done((bf16[16,4096]{1,0:T(8,128)(2,1)S(1)}, bf16[16,4096]{1,0:T(8,128)(2,1)S(1)}, u32[]{:S(2)}, u32[]{:S(2)}) %collective-permute-start.5) | collective-permute-done | bytes 131104 | tf_op jit(solution)/shard_map/ppermute | solution.py:446
  29.8 0.7 %collective-permute-done.12.refs_5_ = bf16[32,2048]{1,0:T(8,128)(2,1)S(1)} collective-permute-done((bf16[32,2048]{1,0:T(8,128)(2,1)S(1)}, bf16[32,2048]{1,0:T(8,128)(2,1)S(1)}, u32[]{:S(2)}, u32[]{:S(2)}) %collective-permute-start.12) | collective-permute-done | bytes 131104 | tf_op jit(solution)/shard_map/ppermute | solution.py:446
  30.5 2.1 %first_half.1 = (f32[64,768]{1,0:T(8,128)S(1)}, f32[64,768]{1,0:T(8,128)S(1)}, f32[64,768]{1,0:T(8,128)S(1)}, bf16[64,2048]{1,0:T(8,128)(2,1)S(1)}, bf16[64,2048]{1,0:T(8,128)(2,1)S(1)}) custom-call(bf16[16,4096]{1,0:T(8,128)(2,1)S(1)} %get-tuple-element.33.refs_0_, bf16[16,4096]{1,0:T(8,128)(2,1)S(1)} %collective-permute-done.3.refs_1_, ...), custom_call_target="tpu_custom_call" | custom-call | flops 603979776 | bytes 9437184 | tf_op jit(solution)/shard_map/first_half/pallas_call | solution.py:239
  32.7 6.7 %second_half.1 = (bf16[64,768]{1,0:T(8,128)(2,1)S(1)}, bf16[64,768]{1,0:T(8,128)(2,1)S(1)}, bf16[64,768]{1,0:T(8,128)(2,1)S(1)}, bf16[64,2048]{1,0:T(8,128)(2,1)...) custom-call(bf16[16,4096]{1,0:T(8,128)(2,1)S(1)} %get-tuple-element.33.refs_0_, ...), custom_call_target="tpu_custom_call" | custom-call | flops 1409286144 | bytes 18874368 | tf_op jit(solution)/shard_map/second_half/pallas_call | solution.py:303
  39.4 5.9 %all-to-all-start = ((bf16[32,2,4096]{2,1,0:T(2,128)(2,1)}), bf16[32,2,4096]{2,1,0:T(2,128)(2,1)S(1)}, u32[]{:S(2)}, u32[]{:S(2)}) async-start(bf16[32,2,4096]{2,1,0:T(2,128)(2,1)} %get-tuple-element.51), calls=%async_computation | async-start | bytes 1048576 | tf_op jit(solution)/shard_map/all_to_all | solution.py:483
  45.3 3.3 %down_grad.1 = bf16[1,768,4096]{2,1,0:T(8,128)(2,1)} custom-call(bf16[64,2048]{1,0:T(8,128)(2,1)S(1)} %get-tuple-element.56.refs_0_, bf16[64,2048]{1,0:T(8,128)(2,1)S(1)} %get-tuple-element.57.refs_1_, bf16[64,768]{1,0:T(8,128)(2,1)S(1)} %get-tuple-element.58.refs_2_), custom_call_target="tpu_custom_call" | custom-call | flops 402653184 | bytes 6291456 | tf_op jit(solution)/shard_map/down_grad/pallas_call | solution.py:382
  48.7 5.3 %pair_grad.1 = bf16[1,2,4096,768]{3,2,1,0:T(8,128)(2,1)} custom-call(bf16[64,2048]{1,0:T(8,128)(2,1)S(1)} %get-tuple-element.52.refs_0_, bf16[64,2048]{1,0:T(8,128)(2,1)S(1)} %get-tuple-element.53.refs_1_, bf16[64,768]{1,0:T(8,128)(2,1)S(1)} %get-tuple-element.54.refs_2_, bf16[64,768]{1,0:T(8,128)(2,1)S(1)} %get-tuple-element.55.refs_3_), custom_call_target="tpu_custom_call" | custom-call | flops 805306368 | bytes 12582912 | tf_op jit(solution)/shard_map/pair_grad/pallas_call | solution.py:345
  53.9 7.1 %all-to-all-done.rows_ref = bf16[32,2,4096]{2,1,0:T(2,128)(2,1)S(1)} async-done(((bf16[32,2,4096]{2,1,0:T(2,128)(2,1)}), bf16[32,2,4096]{2,1,0:T(2,128)(2,1)S(1)}, u32[]{:S(2)}, u32[]{:S(2)}) %all-to-all-start) | async-done | bytes 524320 | tf_op jit(solution)/shard_map/all_to_all | solution.py:483
  61.1 1.4 %spread_rows.1 = bf16[128,4096]{1,0:T(8,128)(2,1)} custom-call(bf16[32,2,4096]{2,1,0:T(2,128)(2,1)S(1)} %all-to-all-done.rows_ref, bf16[32,128]{1,0:T(8,128)(2,1)S(1)} %get-tuple-element.39.after.place_ref), custom_call_target="tpu_custom_call" | custom-call | flops 33554432 | bytes 1048576 | tf_op jit(solution)/shard_map/spread_rows/pallas_call | solution.py:417
  (14 shorter events, 0.9 us)
Async XLA Ops:
  2.7 15.4 %collective-permute-start.6 = (bf16[4,4,4096]{2,1,0:T(4,128)(2,1)S(1)}, bf16[4,4,4096]{2,1,0:T(4,128)(2,1)S(1)}, u32[]{:S(2)}, u32[]{:S(2)}) collective-permute-start(bf16[4,4,4096]{2,1,0:T(4,128)(2,1)S(1)} %get-tuple-element.37), channel_id=1, source_target_pairs={{0,8},{1,9},{2,10},{3,11},{4,12},{5,13},{6,14},{7,15},{8,0},{9,1},... | collective-permute-start | bytes 393224 | tf_op jit(solution)/shard_map/ppermute | solution.py:446
  6.8 11.3 %collective-permute-start.7 = (bf16[4,4,4096]{2,1,0:T(4,128)(2,1)S(1)}, bf16[4,4,4096]{2,1,0:T(4,128)(2,1)S(1)}, u32[]{:S(2)}, u32[]{:S(2)}) collective-permute-start(bf16[4,4,4096]{2,1,0:T(4,128)(2,1)S(1)} %get-tuple-element.38), channel_id=1, source_target_pairs={{0,12},{1,13},{2,14},{3,15},{4,8},{5,9},{6,10},{7,11},{8,4},{9,5},... | collective-permute-start | bytes 393224 | tf_op jit(solution)/shard_map/ppermute | solution.py:446
  8.1 11.9 %collective-permute-start.1 = (bf16[4,4,4096]{2,1,0:T(4,128)(2,1)S(1)}, bf16[4,4,4096]{2,1,0:T(4,128)(2,1)S(1)}, u32[]{:S(2)}, u32[]{:S(2)}) collective-permute-start(bf16[4,4,4096]{2,1,0:T(4,128)(2,1)S(1)} %get-tuple-element.31.refs_0_), channel_id=1, source_target_pairs={{0,16},{1,17},{2,18},{3,19},{4,20},{5,21},{6,22},{7,23},{8,24},{9,... | collective-permute-start | bytes 393224 | tf_op jit(solution)/shard_map/ppermute | solution.py:446
  9.6 10.6 %collective-permute-start.2 = (bf16[4,4,4096]{2,1,0:T(4,128)(2,1)S(1)}, bf16[4,4,4096]{2,1,0:T(4,128)(2,1)S(1)}, u32[]{:S(2)}, u32[]{:S(2)}) collective-permute-start(bf16[4,4,4096]{2,1,0:T(4,128)(2,1)S(1)} %get-tuple-element.32), channel_id=1, source_target_pairs={{0,20},{1,21},{2,22},{3,23},{4,16},{5,17},{6,18},{7,19},{8,28},{9,... | collective-permute-start | bytes 393224 | tf_op jit(solution)/shard_map/ppermute | solution.py:446
  9.8 11.2 %collective-permute-start = (bf16[4,4,4096]{2,1,0:T(4,128)(2,1)S(1)}, bf16[4,4,4096]{2,1,0:T(4,128)(2,1)S(1)}, u32[]{:S(2)}, u32[]{:S(2)}) collective-permute-start(bf16[4,4,4096]{2,1,0:T(4,128)(2,1)S(1)} %get-tuple-element.32), channel_id=1, source_target_pairs={{0,4},{1,5},{2,6},{3,7},{4,0},{5,1},{6,2},{7,3},{8,12},{9,13},{10,... | collective-permute-start | bytes 393224 | tf_op jit(solution)/shard_map/ppermute | solution.py:446
  18.3 4.8 %collective-permute-start.8 = (bf16[8,4096]{1,0:T(8,128)(2,1)S(1)}, bf16[8,4096]{1,0:T(8,128)(2,1)S(1)}, u32[]{:S(2)}, u32[]{:S(2)}) collective-permute-start(bf16[8,4096]{1,0:T(8,128)(2,1)S(1)} %get-tuple-element.42), channel_id=1, source_target_pairs={{0,1},{1,0},{2,3},{3,2},{4,5},{5,4},{6,7},{7,6},{8,9},{9,8},{10,11... | collective-permute-start | bytes 196616 | tf_op jit(solution)/shard_map/ppermute | solution.py:446
  18.4 5.0 %collective-permute-start.9 = (bf16[8,4096]{1,0:T(8,128)(2,1)S(1)}, bf16[8,4096]{1,0:T(8,128)(2,1)S(1)}, u32[]{:S(2)}, u32[]{:S(2)}) collective-permute-start(bf16[8,4096]{1,0:T(8,128)(2,1)S(1)} %get-tuple-element.43), channel_id=1, source_target_pairs={{0,2},{1,3},{2,0},{3,1},{4,6},{5,7},{6,4},{7,5},{8,10},{9,11},{10,... | collective-permute-start | bytes 196616 | tf_op jit(solution)/shard_map/ppermute | solution.py:446
  20.0 4.0 %collective-permute-start.10 = (bf16[8,4096]{1,0:T(8,128)(2,1)S(1)}, bf16[8,4096]{1,0:T(8,128)(2,1)S(1)}, u32[]{:S(2)}, u32[]{:S(2)}) collective-permute-start(bf16[8,4096]{1,0:T(8,128)(2,1)S(1)} %get-tuple-element.44), channel_id=1, source_target_pairs={{0,3},{1,2},{2,1},{3,0},{4,7},{5,6},{6,5},{7,4},{8,11},{9,10},{10,... | collective-permute-start | bytes 196616 | tf_op jit(solution)/shard_map/ppermute | solution.py:446
  21.4 4.8 %collective-permute-start.3 = (bf16[16,4096]{1,0:T(8,128)(2,1)S(1)}, bf16[16,4096]{1,0:T(8,128)(2,1)S(1)}, u32[]{:S(2)}, u32[]{:S(2)}) collective-permute-start(bf16[16,4096]{1,0:T(8,128)(2,1)S(1)} %get-tuple-element.34), channel_id=1, source_target_pairs={{0,1},{1,0},{2,3},{3,2},{4,5},{5,4},{6,7},{7,6},{8,9},{9,8},{10,11... | collective-permute-start | bytes 393224 | tf_op jit(solution)/shard_map/ppermute | solution.py:446
  21.5 6.4 %collective-permute-start.4 = (bf16[16,4096]{1,0:T(8,128)(2,1)S(1)}, bf16[16,4096]{1,0:T(8,128)(2,1)S(1)}, u32[]{:S(2)}, u32[]{:S(2)}) collective-permute-start(bf16[16,4096]{1,0:T(8,128)(2,1)S(1)} %get-tuple-element.35), channel_id=1, source_target_pairs={{0,2},{1,3},{2,0},{3,1},{4,6},{5,7},{6,4},{7,5},{8,10},{9,11},{10,... | collective-permute-start | bytes 393224 | tf_op jit(solution)/shard_map/ppermute | solution.py:446
  23.1 6.6 %collective-permute-start.5 = (bf16[16,4096]{1,0:T(8,128)(2,1)S(1)}, bf16[16,4096]{1,0:T(8,128)(2,1)S(1)}, u32[]{:S(2)}, u32[]{:S(2)}) collective-permute-start(bf16[16,4096]{1,0:T(8,128)(2,1)S(1)} %get-tuple-element.36), channel_id=1, source_target_pairs={{0,3},{1,2},{2,1},{3,0},{4,7},{5,6},{6,5},{7,4},{8,11},{9,10},{10,... | collective-permute-start | bytes 393224 | tf_op jit(solution)/shard_map/ppermute | solution.py:446
  24.1 6.4 %collective-permute-start.12 = (bf16[32,2048]{1,0:T(8,128)(2,1)S(1)}, bf16[32,2048]{1,0:T(8,128)(2,1)S(1)}, u32[]{:S(2)}, u32[]{:S(2)}) collective-permute-start(bf16[32,2048]{1,0:T(8,128)(2,1)S(1)} %get-tuple-element.46.refs_4_), channel_id=1, source_target_pairs={{0,16},{1,17},{2,18},{3,19},{4,20},{5,21},{6,22},{7,23},{8,24},{9,... | collective-permute-start | bytes 393224 | tf_op jit(solution)/shard_map/ppermute | solution.py:446
  25.7 6.9 %collective-permute-start.11 = (bf16[32,2048]{1,0:T(8,128)(2,1)S(1)}, bf16[32,2048]{1,0:T(8,128)(2,1)S(1)}, u32[]{:S(2)}, u32[]{:S(2)}) collective-permute-start(bf16[32,2048]{1,0:T(8,128)(2,1)S(1)} %get-tuple-element.45.refs_4_), channel_id=1, source_target_pairs={{0,16},{1,17},{2,18},{3,19},{4,20},{5,21},{6,22},{7,23},{8,24},{9,... | collective-permute-start | bytes 393224 | tf_op jit(solution)/shard_map/ppermute | solution.py:446
  39.4 21.7 %all-to-all-start = ((bf16[32,2,4096]{2,1,0:T(2,128)(2,1)}), bf16[32,2,4096]{2,1,0:T(2,128)(2,1)S(1)}, u32[]{:S(2)}, u32[]{:S(2)}) async-start(bf16[32,2,4096]{2,1,0:T(2,128)(2,1)} %get-tuple-element.51), calls=%async_computation | async-start | bytes 1048576 | tf_op jit(solution)/shard_map/all_to_all | solution.py:483
